TPU v7x, 512 devices: a whole 4x4x16 slice. The times are simulated.
512 devices in a mesh: seq: 32 (over y, z_hi, core), clip: 16 (over z_lo, x).
Axes of the slice: x: 4, y: 4, z: 16 (z_hi: 4, z_lo: 4; z = z_hi * 4 + z_lo), core: 2. Of those that a mesh axis runs over, the one named last changes fastest.
Arguments:
- hidden: bfloat16 [16, 32, 128, 1152], P('clip', 'seq'), may hold values from -56 to 56
- exponent: int32 [16, 32], P('clip', 'seq'), may hold values from 2 to 7
- modulation: float32 [16, 2, 3, 1152], P('clip'), may hold values from -3 to 3
- out_grad: bfloat16 [16, 32, 128, 1152], P('clip', 'seq'), may hold values from -6 to 6
- w_qkv: bfloat16 [1152, 3456], P('clip'), may hold values from -0.1875 to 0.1875
- w_out: bfloat16 [1152, 1152], P('clip'), may hold values from -0.1875 to 0.1875
- qk_gain: float32 [2, 72], replicated, may hold values from 0.25 to 1.75
Outputs:
- d_hidden: bfloat16 [16, 32, 128, 1152], P('clip', 'seq')
- grad_out_proj: float32 [1152, 1152], P('seq')
All inputs are finite; a program needn't handle non-finite values.
Results may differ from a plain program's by a relative error of at most 0.03.
Values may be sent and summed in bfloat16 or wider, within the bound.
No kernel may reach another device: no remote copies, remote signals or barrier semaphores. Data moves between devices by JAX's collectives and lax.ppermute only.
A program may use at most 128 MiB of HBM per device.

v0:
```python
import jax
import jax.numpy as jnp
from jax import lax
from jax.sharding import PartitionSpec as P


def rotary_tables(frame_count, head_dim, head_count):
    position = lax.broadcasted_iota(jnp.int32, (frame_count, head_dim), 0).astype(jnp.float32)
    column = lax.broadcasted_iota(jnp.int32, (frame_count, head_dim), 1)
    exponent_part = (2 * (column // 2)).astype(jnp.float32) / head_dim
    frequency = jnp.power(10000.0, -exponent_part)
    angles = position * frequency
    return (jnp.tile(jnp.cos(angles), (1, head_count)), jnp.tile(jnp.sin(angles), (1, head_count)))


def rotate(values):
    shifted_up = jnp.roll(values, -1, axis=-1)
    shifted_down = jnp.roll(values, 1, axis=-1)
    parity = lax.broadcasted_iota(jnp.int32, values.shape, values.ndim - 1) % 2
    return jnp.where(parity == 0, -shifted_up, shifted_down)


def product(form, left, right):
    return jnp.einsum(form, left, right, preferred_element_type=jnp.float32)


def contract_last(left, right):
    return lax.dot_general(
        left, right, (((1,), (1,)), ((), ())), preferred_element_type=jnp.float32
    )


def exact_dot(left, right):
    return jnp.dot(left, right, precision=lax.Precision.HIGHEST, preferred_element_type=jnp.float32)


def branch_pass(row_grid, cotangent, clip_mod, w_qkv, w_out, qk_gain):
    clip_count, frame_count, item_count, model_dim = row_grid.shape
    inner_dim = w_out.shape[0]
    head_dim = qk_gain.shape[1]
    head_count = inner_dim // head_dim
    head_shape = (clip_count, frame_count, item_count, head_count, head_dim)
    shift_row = clip_mod[:, 0][:, None, None, :]
    scale_row = clip_mod[:, 1][:, None, None, :]
    gate_row = clip_mod[:, 2][:, None, None, :]
    row_mean = jnp.mean(row_grid, axis=-1, keepdims=True)
    centred = row_grid - row_mean
    norm_factor = lax.rsqrt(jnp.mean(centred * centred, axis=-1, keepdims=True) + 1e-06)
    normed = centred * norm_factor
    modded = (normed * (1.0 + scale_row) + shift_row).astype(jnp.bfloat16)
    packed = jnp.dot(
        modded.reshape(-1, model_dim), w_qkv, preferred_element_type=jnp.float32
    ).astype(jnp.bfloat16)
    query_raw = packed[:, :inner_dim].astype(jnp.float32)
    key_raw = packed[:, inner_dim : 2 * inner_dim].astype(jnp.float32)
    value_rows = packed[:, 2 * inner_dim :]
    cosine_table, sine_table = rotary_tables(frame_count, head_dim, head_count)
    cosine_table = cosine_table[None, :, None, :]
    sine_table = sine_table[None, :, None, :]
    head_column = lax.broadcasted_iota(jnp.int32, (inner_dim, head_count), 0) // head_dim
    head_number = lax.broadcasted_iota(jnp.int32, (inner_dim, head_count), 1)
    head_member = (head_column == head_number).astype(jnp.float32)
    head_spread = head_member.T

    def head_mean(values):
        return exact_dot(values, head_member) / head_dim

    def prepare(raw_rows, gain_values):
        root_factor = lax.rsqrt(head_mean(raw_rows * raw_rows) + 1e-06)
        root_wide = exact_dot(root_factor, head_spread)
        gain_wide = jnp.tile(gain_values, head_count)
        normal_rows = (raw_rows * root_wide * gain_wide).reshape(
            clip_count, frame_count, item_count, inner_dim
        )
        turned = normal_rows * cosine_table + rotate(normal_rows) * sine_table
        return (turned.astype(jnp.bfloat16), root_wide)

    query_hat, query_factor = prepare(query_raw, qk_gain[0])
    key_hat, key_factor = prepare(key_raw, qk_gain[1])
    query_grid = query_hat.reshape(head_shape)
    key_grid = key_hat.reshape(head_shape)
    value_grid = value_rows.reshape(head_shape)
    temper = head_dim ** (-0.5)
    scores = product("cfnhd,cgnhd->cnhfg", query_grid, key_grid) * temper
    exp_scores = jnp.exp(scores)
    prob_full = exp_scores / jnp.sum(exp_scores, axis=-1, keepdims=True)
    prob_half = prob_full.astype(jnp.bfloat16)
    attended = product("cnhfg,cgnhd->cfnhd", prob_half, value_grid).astype(jnp.bfloat16)
    attended = attended.reshape(clip_count, frame_count, item_count, inner_dim)
    branch_grad = (gate_row * cotangent.astype(jnp.float32)).astype(jnp.bfloat16)
    grad_attended = contract_last(branch_grad.reshape(-1, model_dim), w_out).astype(jnp.bfloat16)
    grad_grid = grad_attended.reshape(head_shape)
    grad_prob = product("cfnhd,cgnhd->cnhfg", grad_grid, value_grid)
    grad_value = product("cnhfg,cfnhd->cgnhd", prob_half, grad_grid).astype(jnp.bfloat16)
    grad_score = (
        prob_full * (grad_prob - jnp.sum(prob_full * grad_prob, axis=-1, keepdims=True)) * temper
    ).astype(jnp.bfloat16)
    grad_qhat = product("cnhfg,cgnhd->cfnhd", grad_score, key_grid)
    grad_khat = product("cnhfg,cfnhd->cgnhd", grad_score, query_grid)

    def restore(grad_turned, raw_rows, root_wide, gain_values):
        grad_turned = grad_turned.reshape(clip_count, frame_count, item_count, inner_dim)
        grad_normal = grad_turned * cosine_table - rotate(grad_turned) * sine_table
        scaled_grad = grad_normal.reshape(-1, inner_dim) * jnp.tile(gain_values, head_count)
        inner_mean = exact_dot(head_mean(raw_rows * scaled_grad), head_spread)
        grad_raw = root_wide * scaled_grad - raw_rows * root_wide**3 * inner_mean
        return grad_raw.astype(jnp.bfloat16)

    grad_packed = jnp.concatenate(
        [
            restore(grad_qhat, query_raw, query_factor, qk_gain[0]),
            restore(grad_khat, key_raw, key_factor, qk_gain[1]),
            grad_value.reshape(-1, inner_dim),
        ],
        axis=1,
    )
    grad_modded = contract_last(grad_packed, w_qkv)
    grad_normed = grad_modded.reshape(clip_count, frame_count, item_count, model_dim) * (
        1.0 + scale_row
    )
    grad_rows = norm_factor * (
        grad_normed
        - jnp.mean(grad_normed, axis=-1, keepdims=True)
        - normed * jnp.mean(grad_normed * normed, axis=-1, keepdims=True)
    )
    return (grad_rows.astype(jnp.bfloat16), attended, branch_grad)


def on_device(hidden, exponent, modulation, out_grad, w_qkv, w_out, qk_gain):
    seq_count = lax.axis_size("seq")
    frames_dev = hidden.shape[1]
    spatial = hidden.shape[2]
    model_dim = hidden.shape[3]
    per_device = spatial // seq_count
    power_scale = jnp.exp2(exponent[0].astype(jnp.float32))
    lifted = hidden[0].astype(jnp.float32) * power_scale[:, None, None]
    scaled = (
        jnp.clip(lifted, -448.0, 448.0)
        .astype(jnp.bfloat16)
        .reshape(frames_dev, seq_count, per_device, model_dim)
    )
    descale = jnp.broadcast_to(
        (1.0 / power_scale)[:, None, None], (frames_dev, seq_count, per_device)
    ).astype(jnp.bfloat16)
    cotangent = out_grad[0].reshape(frames_dev, seq_count, per_device, model_dim)
    full_qkv, full_out = (
        lax.all_gather(w_qkv, "clip", axis=0, tiled=True),
        lax.all_gather(w_out, "clip", axis=0, tiled=True),
    )
    clip_mod = modulation[0]
    clip_count = clip_mod.shape[0]
    rows_in = lax.all_to_all(scaled, "seq", split_axis=1, concat_axis=0, tiled=True)
    scale_in = lax.all_to_all(descale, "seq", split_axis=1, concat_axis=0, tiled=True)
    cot_in = lax.all_to_all(cotangent, "seq", split_axis=1, concat_axis=0, tiled=True)
    frames_all = rows_in.shape[0]
    item_count = rows_in.shape[2]
    frame_count = frames_all // clip_count
    restored = rows_in[:, 0].astype(jnp.float32) * scale_in[:, 0][:, :, None].astype(jnp.float32)
    row_grid = restored.reshape(clip_count, frame_count, item_count, model_dim)
    cot_grid = cot_in[:, 0].reshape(clip_count, frame_count, item_count, model_dim)
    grad_rows, attended, branch_grad = branch_pass(
        row_grid, cot_grid, clip_mod, full_qkv, full_out, qk_gain
    )
    grad_local, attended, branch_grad = (
        grad_rows.reshape(frames_all, item_count, model_dim),
        attended.reshape(frames_all, item_count, -1),
        branch_grad.reshape(frames_all, item_count, model_dim),
    )
    grad_back = lax.all_to_all(grad_local, "seq", split_axis=0, concat_axis=1, tiled=True)
    d_hidden = (out_grad[0].astype(jnp.float32) + grad_back.astype(jnp.float32)).astype(
        jnp.bfloat16
    )[None]
    inner_dim = attended.shape[2]
    attended_flat = attended.reshape(-1, inner_dim)
    grad_flat = branch_grad.reshape(-1, model_dim)
    grad_share = lax.psum_scatter(
        lax.dot_general(
            attended_flat, grad_flat, (((0,), (0,)), ((), ())), preferred_element_type=jnp.float32
        ).astype(jnp.bfloat16),
        "seq",
        scatter_dimension=0,
        tiled=True,
    ).astype(jnp.float32)
    grad_share = lax.psum(grad_share.astype(jnp.bfloat16), "clip").astype(jnp.float32)
    grad_out_proj = grad_share / (clip_count * lax.axis_size("clip"))
    return (d_hidden, grad_out_proj)


def solution(mesh):
    placed = (
        P("clip", "seq", None, None),
        P("clip", "seq"),
        P("clip", None, None, None),
        P("clip", "seq", None, None),
        P("clip", None),
        P("clip", None),
        P(),
    )
    return jax.shard_map(
        on_device,
        mesh=mesh,
        in_specs=placed,
        out_specs=(P("clip", "seq", None, None), P("seq", None)),
        check_vma=False,
    )
```

profile of v0, /device:TPU:24, one launch (start us, length us, event | category | flops | bytes accessed | tf_op | source)
XLA Modules:
  0.0 686.2 jit_solution(2201314992103018802)
XLA Ops:
  10.0 18.1 %all-to-all-start.1 = ((bf16[1,32,4]{2,0,1:T(2,128)(2,1)}), bf16[1,32,4]{2,0,1:T(2,128)(2,1)S(1)}, u32[]{:S(2)}, u32[]{:S(2)}) async-start(bf16[1,32,4]{2,0,1:T(2,128)(2,1)} %broadcast_in_dim.2), calls=%async_computation.1 | async-start | bytes 32768 | tf_op jit(solution)/shard_map/all_to_all | solution.py:153
  30.6 10.2 %all-to-all-done.1 = bf16[1,32,4]{2,0,1:T(2,128)(2,1)S(1)} async-done(((bf16[1,32,4]{2,0,1:T(2,128)(2,1)}), bf16[1,32,4]{2,0,1:T(2,128)(2,1)S(1)}, u32[]{:S(2)}, u32[]{:S(2)}) %all-to-all-start.1) | async-done | bytes 288 | tf_op jit(solution)/shard_map/all_to_all | solution.py:153
  40.8 5.8 all-to-all-start
  48.8 19.6 %all-to-all-done = bf16[1,32,4,1152]{3,2,0,1:T(4,128)(2,1)S(1)} async-done(((bf16[1,32,4,1152]{3,2,0,1:T(4,128)(2,1)}), bf16[1,32,4,1152]{3,2,0,1:T(4,128)(2,1)S(1)}, u32[]{:S(2)}, u32[]{:S(2)}) %all-to-all-start) | async-done | bytes 294944 | tf_op jit(solution)/shard_map/all_to_all | solution.py:152
  68.4 6.1 all-to-all-start.2
  83.9 12.2 %all-to-all-done.2 = bf16[1,32,4,1152]{3,2,0,1:T(4,128)(2,1)S(1)} async-done(((bf16[1,32,4,1152]{3,2,0,1:T(4,128)(2,1)}), bf16[1,32,4,1152]{3,2,0,1:T(4,128)(2,1)S(1)}, u32[]{:S(2)}, u32[]{:S(2)}) %all-to-all-start.2) | async-done | bytes 294944 | tf_op jit(solution)/shard_map/all_to_all | solution.py:154
  97.1 16.8 %all-gather.5.cloned.1.call-done = bf16[1152,1152]{1,0:T(8,128)(2,1)} async-done(((bf16[72,1152]{1,0:T(8,128)(2,1)}), bf16[1152,1152]{1,0:T(8,128)(2,1)}) %all-gather.5.cloned.1.call-update) | async-done | bytes 2654224 | tf_op jit(solution)/shard_map/all_gather | solution.py:148
  113.9 2.7 convolution_convert_fusion.2
  118.4 104.1 %all-gather.3.cloned.1.call-done = bf16[1152,3456]{1,0:T(8,128)(2,1)} async-done(((bf16[72,3456]{1,0:T(8,128)(2,1)}), bf16[1152,3456]{1,0:T(8,128)(2,1)}) %all-gather.3.cloned.1.call-update) | async-done | bytes 7962640 | tf_op jit(solution)/shard_map/all_gather | solution.py:147
  222.4 4.7 convolution_convert_fusion.1
  230.5 2.7 fusion.32
  252.5 3.0 fusion.18
  258.0 3.0 fusion.12
  262.8 2.8 convolution_bitcast_fusion
  271.7 2.8 convolution_bitcast_fusion.1
  279.7 2.9 fusion.11
  284.3 2.2 copy.101
  288.6 2.1 copy.105
  301.8 2.8 fusion.37
  307.5 2.5 fusion.4
  311.4 3.0 fusion.5
  314.5 6.1 multiply_reduce_fusion.4
  322.3 12.6 %all-to-all-start.3 = ((bf16[32,4,1152]{2,1,0:T(4,128)(2,1)}), bf16[32,4,1152]{2,1,0:T(4,128)(2,1)S(1)}, u32[]{:S(2)}, u32[]{:S(2)}) async-start(bf16[32,4,1152]{2,1,0:T(4,128)(2,1)} %fusion.47), calls=%async_computation.3 | async-start | bytes 589824 | tf_op jit(solution)/shard_map/all_to_all | solution.py:169
  335.9 117.7 %fusion = bf16[48,1152]{1,0:T(8,128)(2,1)S(1)} fusion(bf16[1152,1152]{1,0:T(8,128)(2,1)S(1)} %convolution_convert_fusion), kind=kCustom, calls=%all-reduce-scatter | all-reduce-scatter fusion | flops 1769473 | bytes 2766848
  455.5 7.0 %collective-permute-start.1 = (bf16[48,1152]{1,0:T(8,128)(2,1)S(1)}, bf16[48,1152]{1,0:T(8,128)(2,1)S(1)}, u32[]{:S(2)}, u32[]{:S(2)}) collective-permute-start(bf16[48,1152]{1,0:T(8,128)(2,1)S(1)} %fusion), channel_id=1, source_target_pairs={{0,32},{16,48},{32,64},{48,80},{64,96},{80,112},{96,128},{112,144}... | collective-permute-start | bytes 331784
  463.8 6.3 collective-permute-start.2
  472.1 3.9 collective-permute-start.4
  481.8 11.3 %collective-permute-done.2 = bf16[48,1152]{1,0:T(8,128)(2,1)S(1)} collective-permute-done((bf16[48,1152]{1,0:T(8,128)(2,1)S(1)}, bf16[48,1152]{1,0:T(8,128)(2,1)S(1)}, u32[]{:S(2)}, u32[]{:S(2)}) %collective-permute-start.2) | collective-permute-done | bytes 110624
  493.1 5.7 collective-permute-done.3
  498.9 10.9 %collective-permute-done.4 = bf16[48,1152]{1,0:T(8,128)(2,1)S(1)} collective-permute-done((bf16[48,1152]{1,0:T(8,128)(2,1)S(1)}, bf16[48,1152]{1,0:T(8,128)(2,1)S(1)}, u32[]{:S(2)}, u32[]{:S(2)}) %collective-permute-start.4) | collective-permute-done | bytes 110624
  510.0 2.2 concatenate.76
  512.9 164.0 %all-reduce.4.cloned.1.call-done = bf16[36,1152]{1,0:T(8,128)(2,1)} async-done(((bf16[36,1152]{1,0:T(8,128)(2,1)}), bf16[36,1152]{1,0:T(8,128)(2,1)}) %all-reduce.4.cloned.1.call-update) | async-done | bytes 82960 | tf_op jit(solution)/shard_map/psum | solution.py:184
  (270 shorter events, 91.7 us)
Async XLA Ops:
  7.2 39.4 %copy-start.19 = (bf16[1,1,128,1152]{3,2,1,0:T(8,128)(2,1)S(1)}, bf16[1,1,128,1152]{3,2,1,0:T(8,128)(2,1)}, u32[]{:S(2)}) copy-start(bf16[1,1,128,1152]{3,2,1,0:T(8,128)(2,1)} %param.10) | copy-start | bytes 884740
  7.2 41.4 %copy-start.61 = (f32[2,72]{1,0:T(2,128)S(1)}, f32[2,72]{1,0:T(2,128)}, u32[]{:S(2)}) copy-start(f32[2,72]{1,0:T(2,128)} %param.13) | copy-start | bytes 1732
  7.2 41.5 %copy-start.55 = (f32[1,2,3,1152]{3,1,2,0:T(2,128)S(1)}, f32[1,2,3,1152]{3,1,2,0:T(2,128)}, u32[]{:S(2)}) copy-start(f32[1,2,3,1152]{3,1,2,0:T(2,128)} %param.9) | copy-start | bytes 82948
  7.2 106.7 %all-gather.5.cloned.1.call-start = ((), (), s32[]{:S(2)}) async-start(), calls=%async_computation.5 | async-start | bytes 2820096 | tf_op jit(solution)/shard_map/all_gather | solution.py:148
  7.9 214.5 %all-gather.3.cloned.1.call-start = ((), (), s32[]{:S(2)}) async-start(), calls=%async_computation.4 | async-start | bytes 8460288 | tf_op jit(solution)/shard_map/all_gather | solution.py:147
  10.0 30.8 %all-to-all-start.1 = ((bf16[1,32,4]{2,0,1:T(2,128)(2,1)}), bf16[1,32,4]{2,0,1:T(2,128)(2,1)S(1)}, u32[]{:S(2)}, u32[]{:S(2)}) async-start(bf16[1,32,4]{2,0,1:T(2,128)(2,1)} %broadcast_in_dim.2), calls=%async_computation.1 | async-start | bytes 32768 | tf_op jit(solution)/shard_map/all_to_all | solution.py:153
  40.8 27.6 %all-to-all-start = ((bf16[1,32,4,1152]{3,2,0,1:T(4,128)(2,1)}), bf16[1,32,4,1152]{3,2,0,1:T(4,128)(2,1)S(1)}, u32[]{:S(2)}, u32[]{:S(2)}) async-start(bf16[1,32,4,1152]{3,2,0,1:T(4,128)(2,1)} %convert_element_type.245), calls=%async_computation | async-start | bytes 589824 | tf_op jit(solution)/shard_map/all_to_all | solution.py:152
  48.7 28.6 %copy-start.45 = (f32[16,72]{1,0:T(8,128)}, f32[16,72]{1,0:T(8,128)S(1)}, u32[]{:S(2)}) copy-start(f32[16,72]{1,0:T(8,128)S(1)} %get-tuple-element.29) | copy-start | bytes 13828
  48.7 29.9 %copy-start.47 = (f32[16,72]{1,0:T(8,128)}, f32[16,72]{1,0:T(8,128)S(1)}, u32[]{:S(2)}) copy-start(f32[16,72]{1,0:T(8,128)S(1)} %get-tuple-element.30) | copy-start | bytes 13828
  48.7 26.3 %copy-start.39 = (f32[2,1152]{1,0:T(2,128)}, f32[2,1152]{1,0:T(2,128)S(1)}, u32[]{:S(2)}) copy-start(f32[2,1152]{1,0:T(2,128)S(1)} %get-tuple-element.26) | copy-start | bytes 27652
  68.4 27.7 %all-to-all-start.2 = ((bf16[1,32,4,1152]{3,2,0,1:T(4,128)(2,1)}), bf16[1,32,4,1152]{3,2,0,1:T(4,128)(2,1)S(1)}, u32[]{:S(2)}, u32[]{:S(2)}) async-start(bf16[1,32,4,1152]{3,2,0,1:T(4,128)(2,1)} %reshape_squeeze.4), calls=%async_computation.2 | async-start | bytes 589824 | tf_op jit(solution)/shard_map/all_to_all | solution.py:154
  75.3 147.1 %copy-start.2 = (f32[128,1152]{1,0:T(8,128)}, f32[128,1152]{1,0:T(8,128)S(1)}, u32[]{:S(2)}) copy-start(f32[128,1152]{1,0:T(8,128)S(1)} %mul.360) | copy-start | bytes 1769476
  97.1 125.4 %copy-start.4 = (f32[128,1152]{1,0:T(8,128)}, f32[128,1152]{1,0:T(8,128)S(1)}, u32[]{:S(2)}) copy-start(f32[128,1152]{1,0:T(8,128)S(1)} %reshape.452) | copy-start | bytes 1769476
  118.3 108.8 %copy-start.33 = (s32[1152]{0:T(1024)S(1)}, s32[1152]{0:T(1024)}, u32[]{:S(2)}) copy-start(s32[1152]{0:T(1024)} %get-tuple-element.35) | copy-start | bytes 13828
  118.3 108.8 %copy-start.35 = (s32[1152]{0:T(1024)S(1)}, s32[1152]{0:T(1024)}, u32[]{:S(2)}) copy-start(s32[1152]{0:T(1024)} %get-tuple-element.36) | copy-start | bytes 13828
  118.3 108.8 %copy-start.49 = (pred[1152]{0:T(1024)(128)(4,1)S(1)}, pred[1152]{0:T(1024)(128)(4,1)}, u32[]{:S(2)}) copy-start(pred[1152]{0:T(1024)(128)(4,1)} %fusion.105) | copy-start | bytes 3460
  118.3 112.1 %copy-start.41 = (f32[1152]{0:T(1024)S(1)}, f32[1152]{0:T(1024)}, u32[]{:S(2)}) copy-start(f32[1152]{0:T(1024)} %mul.365) | copy-start | bytes 13828
  118.3 112.1 %copy-start.43 = (f32[1152]{0:T(1024)S(1)}, f32[1152]{0:T(1024)}, u32[]{:S(2)}) copy-start(f32[1152]{0:T(1024)} %mul.375) | copy-start | bytes 13828
  227.1 14.3 %copy-start = (bf16[128,3456]{1,0:T(8,128)(2,1)}, bf16[128,3456]{1,0:T(8,128)(2,1)S(1)}, u32[]{:S(2)}) copy-start(bf16[128,3456]{1,0:T(8,128)(2,1)S(1)} %convolution_convert_fusion.1) | copy-start | bytes 2654212
  320.6 14.4 %copy-start.17 = (bf16[128,1152]{1,0:T(8,128)(2,1)S(1)}, bf16[128,1152]{1,0:T(8,128)(2,1)}, u32[]{:S(2)}) copy-start(bf16[128,1152]{1,0:T(8,128)(2,1)} %reshape_reshape_reshape.3) | copy-start | bytes 884740
  320.6 14.4 %copy-start.18 = (bf16[128,1152]{1,0:T(8,128)(2,1)S(1)}, bf16[128,1152]{1,0:T(8,128)(2,1)}, u32[]{:S(2)}) copy-start(bf16[128,1152]{1,0:T(8,128)(2,1)} %convert_element_type.283) | copy-start | bytes 884740
  322.3 356.3 %all-to-all-start.3 = ((bf16[32,4,1152]{2,1,0:T(4,128)(2,1)}), bf16[32,4,1152]{2,1,0:T(4,128)(2,1)S(1)}, u32[]{:S(2)}, u32[]{:S(2)}) async-start(bf16[32,4,1152]{2,1,0:T(4,128)(2,1)} %fusion.47), calls=%async_computation.3 | async-start | bytes 589824 | tf_op jit(solution)/shard_map/all_to_all | solution.py:169
  334.9 342.0 %all-reduce.4.cloned.1.call-start = ((), (), s32[]{:S(2)}) async-start(), calls=%async_computation.6 | async-start | bytes 184320 | tf_op jit(solution)/shard_map/psum | solution.py:184
  335.9 342.7 %copy-start.20 = (bf16[1,1,128,1152]{3,2,1,0:T(8,128)(2,1)S(1)}, bf16[1,1,128,1152]{3,2,1,0:T(8,128)(2,1)}, u32[]{:S(2)}) copy-start(bf16[1,1,128,1152]{3,2,1,0:T(8,128)(2,1)} %param.10) | copy-start | bytes 884740
  453.6 22.4 %collective-permute-start = (bf16[48,1152]{1,0:T(8,128)(2,1)S(1)}, bf16[48,1152]{1,0:T(8,128)(2,1)S(1)}, u32[]{:S(2)}, u32[]{:S(2)}) collective-permute-start(bf16[48,1152]{1,0:T(8,128)(2,1)S(1)} %fusion), channel_id=1, source_target_pairs={{0,16},{16,32},{32,48},{48,64},{64,80},{80,96},{96,112},{112,128},... | collective-permute-start | bytes 331784
  455.5 22.5 %collective-permute-start.1 = (bf16[48,1152]{1,0:T(8,128)(2,1)S(1)}, bf16[48,1152]{1,0:T(8,128)(2,1)S(1)}, u32[]{:S(2)}, u32[]{:S(2)}) collective-permute-start(bf16[48,1152]{1,0:T(8,128)(2,1)S(1)} %fusion), channel_id=1, source_target_pairs={{0,32},{16,48},{32,64},{48,80},{64,96},{80,112},{96,128},{112,144}... | collective-permute-start | bytes 331784
  462.5 9.6 %collective-permute-start.7 = (bf16[36,1152]{1,0:T(8,128)(2,1)S(1)}, bf16[36,1152]{1,0:T(8,128)(2,1)S(1)}, u32[]{:S(2)}, u32[]{:S(2)}) collective-permute-start(bf16[36,1152]{1,0:T(8,128)(2,1)S(1)} %slice.124), channel_id=1, source_target_pairs={{0,128},{16,144},{32,160},{48,176},{64,192},{80,208},{96,224},{112... | collective-permute-start | bytes 248840
  463.8 29.3 %collective-permute-start.2 = (bf16[48,1152]{1,0:T(8,128)(2,1)S(1)}, bf16[48,1152]{1,0:T(8,128)(2,1)S(1)}, u32[]{:S(2)}, u32[]{:S(2)}) collective-permute-start(bf16[48,1152]{1,0:T(8,128)(2,1)S(1)} %fusion), channel_id=1, source_target_pairs={{0,48},{16,64},{32,80},{48,96},{64,112},{80,128},{96,144},{112,160... | collective-permute-start | bytes 331784
  470.2 28.7 %collective-permute-start.3 = (bf16[48,1152]{1,0:T(8,128)(2,1)S(1)}, bf16[48,1152]{1,0:T(8,128)(2,1)S(1)}, u32[]{:S(2)}, u32[]{:S(2)}) collective-permute-start(bf16[48,1152]{1,0:T(8,128)(2,1)S(1)} %fusion), channel_id=1, source_target_pairs={{0,64},{16,80},{32,96},{48,112},{64,128},{80,144},{96,160},{112,17... | collective-permute-start | bytes 331784
  472.1 37.7 %collective-permute-start.4 = (bf16[48,1152]{1,0:T(8,128)(2,1)S(1)}, bf16[48,1152]{1,0:T(8,128)(2,1)S(1)}, u32[]{:S(2)}, u32[]{:S(2)}) collective-permute-start(bf16[48,1152]{1,0:T(8,128)(2,1)S(1)} %fusion), channel_id=1, source_target_pairs={{0,80},{16,96},{32,112},{48,128},{64,144},{80,160},{96,176},{112,1... | collective-permute-start | bytes 331784
  476.0 33.9 %collective-permute-start.5 = (bf16[48,1152]{1,0:T(8,128)(2,1)S(1)}, bf16[48,1152]{1,0:T(8,128)(2,1)S(1)}, u32[]{:S(2)}, u32[]{:S(2)}) collective-permute-start(bf16[48,1152]{1,0:T(8,128)(2,1)S(1)} %fusion), channel_id=1, source_target_pairs={{0,96},{16,112},{32,128},{48,144},{64,160},{80,176},{96,192},{112,... | collective-permute-start | bytes 331784
  478.0 32.0 %collective-permute-start.6 = (bf16[48,1152]{1,0:T(8,128)(2,1)S(1)}, bf16[48,1152]{1,0:T(8,128)(2,1)S(1)}, u32[]{:S(2)}, u32[]{:S(2)}) collective-permute-start(bf16[48,1152]{1,0:T(8,128)(2,1)S(1)} %fusion), channel_id=1, source_target_pairs={{0,112},{16,128},{32,144},{48,160},{64,176},{80,192},{96,208},{112... | collective-permute-start | bytes 331784
  (46 other events, 201.7 us)
Sparse Core Ops, SparseCore 0:
  10.1 103.7 all-gather.4
  116.0 106.3 all-gather.2
  513.0 163.8 all-reduce.3
where the time goes:
time: 695 us; the launch traced here: 686 us
  waiting for transfers between devices  356 us (51%)
  blocking collectives  118 us (17%)
  starting transfers between devices  68.9 us (10%)
  local copies, waits for them, and re-layouts  67.4 us (10%)
  matrix products  42.4 us (6%)
  other arithmetic  16.7 us (2%)
  between operations  16.6 us (2%)
    psum x1, waiting for transfers between devices, on_device(): lax.psum(grad_share.astype(jnp.bfloat16), 'clip').astype(jnp.float32)  164 us
    unnamed x1, blocking collectives  118 us
    all_gather x1, waiting for transfers between devices, on_device(): lax.all_gather(w_qkv, 'clip', axis=0, tiled=True)  104 us
    unnamed x11, waiting for transfers between devices  29.6 us
    unnamed x8, starting transfers between devices  26.2 us
    all_to_all x1, waiting for transfers between devices, on_device(): lax.all_to_all(scaled, 'seq', split_axis=1, concat_axis=0, tiled=True)  19.6 us
    all_to_all x1, starting transfers between devices, on_device(): lax.all_to_all(descale, 'seq', split_axis=1, concat_axis=0, tiled=True)  18.1 us
    all_gather x1, waiting for transfers between devices, on_device(): lax.all_gather(w_out, 'clip', axis=0, tiled=True)  16.8 us
  transfers between devices with their start and end apart: 15, of which 10 were waited for; matrix products, arithmetic and copies ran while one was open for 21% of the time, Pallas kernels for 0%

commit v1 on v0

v1 whole, which is shorter than its diff:
```python
import jax
import jax.numpy as jnp
from jax import lax
from jax.experimental import pallas as pl
from jax.experimental.pallas import tpu as pltpu
from jax.sharding import Mesh
from jax.sharding import PartitionSpec as P

FINE = (("yh", 2), ("yl", 2), ("zh", 4), ("c", 2), ("zl", 4), ("x", 4))
SEQ = ("yh", "yl", "zh", "c")
CLIP = ("zl", "x")
D = 1152
HD = 72
HALF = 576
WIDE = 640
PEERS = 8
TOK = 16
ROWS = PEERS * TOK
ALL = 2 * ROWS
F32 = jnp.float32
BF16 = jnp.bfloat16
EPS = 1e-06
TEMPER = HD ** (-0.5)
PARAMS = pltpu.CompilerParams(vmem_limit_bytes=56 * 1024 * 1024)


def cost(flops, nbytes):
    return pl.CostEstimate(flops=flops, bytes_accessed=nbytes, transcendentals=0)


def normalise(hidden, power, inverse):
    scaled = jnp.clip(hidden.astype(F32) * power, -448.0, 448.0)
    rows = scaled * inverse
    centred = rows - jnp.mean(rows, axis=-1, keepdims=True)
    factor = lax.rsqrt(jnp.mean(centred * centred, axis=-1, keepdims=True) + EPS)
    return centred * factor, factor


def home_forward(power_ref, hidden_ref, grad_ref, mod_ref, out_ref):
    normed, _ = normalise(hidden_ref[...], power_ref[0], power_ref[1])
    modded = (normed * (1.0 + mod_ref[1:2, :]) + mod_ref[0:1, :]).astype(BF16)
    branch = (mod_ref[2:3, :] * grad_ref[...].astype(F32)).astype(BF16)
    out_ref[:, 0:TOK, :] = modded.reshape(PEERS, TOK, D)
    out_ref[:, TOK : 2 * TOK, :] = branch.reshape(PEERS, TOK, D)


def home_backward(power_ref, hidden_ref, grad_ref, mod_ref, back_ref, out_ref):
    normed, factor = normalise(hidden_ref[...], power_ref[0], power_ref[1])
    d_normed = back_ref[...].astype(F32) * (1.0 + mod_ref[1:2, :])
    d_rows = factor * (
        d_normed
        - jnp.mean(d_normed, axis=-1, keepdims=True)
        - normed * jnp.mean(d_normed * normed, axis=-1, keepdims=True)
    )
    out_ref[...] = (grad_ref[...].astype(F32) + d_rows.astype(BF16).astype(F32)).astype(BF16)


def nt(left, right):
    return lax.dot_general(left, right, (((1,), (1,)), ((), ())), preferred_element_type=F32)


def nn(left, right):
    return lax.dot_general(left, right, (((1,), (0,)), ((), ())), preferred_element_type=F32)


def tn(left, right):
    return lax.dot_general(left, right, (((0,), (0,)), ((), ())), preferred_element_type=F32)


def swap_pairs(values):
    parity = lax.broadcasted_iota(jnp.int32, (values.shape[0], 128), 1) % 2
    tiles = []
    for start in range(0, values.shape[1], 128):
        tile = values[:, start : start + 128]
        tiles.append(jnp.where(parity == 0, pltpu.roll(tile, 127, 1), pltpu.roll(tile, 1, 1)))
    return jnp.concatenate(tiles, axis=1)


def head_members():
    entry = lax.broadcasted_iota(jnp.int32, (WIDE, 128), 0)
    first = lax.broadcasted_iota(jnp.int32, (WIDE, 128), 1) * HD
    return ((entry >= first) & (entry < first + HD) & (entry < HALF)).astype(F32).astype(BF16)


def split_dot(dot, values, members):
    high = values.astype(BF16)
    low = (values - high.astype(F32)).astype(BF16)
    return dot(high, members) + dot(low, members)


def window(head):
    start = head * HD // 128 * 128
    end = -(-(head + 1) * HD // 128) * 128
    column = lax.broadcasted_iota(jnp.int32, (ALL, end - start), 1) + start
    return start, end, (column >= head * HD) & (column < (head + 1) * HD)


def keep(values, mask):
    return jnp.where(mask, values, jnp.zeros_like(values))


def same_token():
    row = lax.broadcasted_iota(jnp.int32, (ALL, ALL), 0) % TOK
    column = lax.broadcasted_iota(jnp.int32, (ALL, ALL), 1) % TOK
    return row == column


def probabilities(q_hat_ref, k_hat_ref, head, same):
    start, end, mask = window(head)
    scores = nt(keep(q_hat_ref[:, start:end], mask), k_hat_ref[:, start:end]) * TEMPER
    exps = jnp.where(same, jnp.exp(scores), 0.0)
    return exps / jnp.sum(exps, axis=-1, keepdims=True)


def gather_rows(own_ref, other_ref, first):
    return jnp.concatenate(
        [ref[:, first : first + TOK, :].reshape(ROWS, D) for ref in (own_ref, other_ref)], axis=0
    )


def widen(values):
    return jnp.concatenate([values, jnp.zeros((ALL, WIDE - HALF), values.dtype)], axis=1)


def chip_forward(
    own_ref, other_ref, w_ref, tab_ref, part_ref, q_ref, k_ref, v_ref, qh_ref, kh_ref, qf_ref, kf_ref, att_ref
):
    modded = gather_rows(own_ref, other_ref, 0)
    members = head_members()
    for place, (raw_ref, hat_ref, factor_ref) in enumerate(((q_ref, qh_ref, qf_ref), (k_ref, kh_ref, kf_ref))):
        raw = widen(nn(modded, w_ref[place]).astype(BF16))
        raw_ref[...] = raw
        raw = raw.astype(F32)
        factor = lax.rsqrt(split_dot(nn, raw * raw, members) / HD + EPS)
        factor_ref[...] = factor
        turned = raw * tab_ref[2 * place] + swap_pairs(raw) * tab_ref[2 * place + 1]
        hat_ref[...] = (split_dot(nt, factor, members) * turned).astype(BF16)
    v_ref[...] = widen(nn(modded, w_ref[2]).astype(BF16))
    same = same_token()
    att_ref[...] = jnp.zeros_like(att_ref)
    for head in range(8):
        start, end, mask = window(head)
        probs = probabilities(qh_ref, kh_ref, head, same).astype(BF16)
        found = nn(probs, v_ref[:, start:end]).astype(BF16)
        att_ref[:, start:end] = jnp.where(mask, found, att_ref[:, start:end])
    branch = gather_rows(own_ref, other_ref, TOK)
    part_ref[...] = tn(att_ref[...], branch)[:HALF].astype(BF16)


def chip_backward(
    own_ref, other_ref, w_ref, wo_ref, tab_ref, q_ref, k_ref, v_ref, qh_ref, kh_ref, qf_ref, kf_ref,
    mine_ref, theirs_ref, do_ref, dv_ref, dqh_ref, dkh_ref,
):
    branch = gather_rows(own_ref, other_ref, TOK)
    do_ref[...] = widen(nt(branch, wo_ref[...]).astype(BF16))
    same = same_token()
    members = head_members()
    for ref in (dv_ref, dqh_ref, dkh_ref):
        ref[...] = jnp.zeros_like(ref)
    for head in range(8):
        start, end, mask = window(head)
        probs = probabilities(qh_ref, kh_ref, head, same)
        d_out = do_ref[:, start:end]
        d_probs = nt(keep(d_out, mask), v_ref[:, start:end])
        d_value = tn(probs.astype(BF16), d_out)
        spread = probs * d_probs
        d_scores = ((spread - probs * jnp.sum(spread, axis=-1, keepdims=True)) * TEMPER).astype(BF16)
        d_q = nn(d_scores, kh_ref[:, start:end])
        d_k = tn(d_scores, qh_ref[:, start:end])
        dv_ref[:, start:end] = jnp.where(mask, d_value.astype(BF16), dv_ref[:, start:end])
        dqh_ref[:, start:end] = jnp.where(mask, d_q, dqh_ref[:, start:end])
        dkh_ref[:, start:end] = jnp.where(mask, d_k, dkh_ref[:, start:end])
    total = nt(dv_ref[:, :HALF], w_ref[2])
    for place, (raw_ref, factor_ref, turned_ref) in enumerate(
        ((q_ref, qf_ref, dqh_ref), (k_ref, kf_ref, dkh_ref))
    ):
        raw = raw_ref[...].astype(F32)
        factor = factor_ref[...]
        turned = turned_ref[...]
        scaled = turned * tab_ref[2 * place] + swap_pairs(turned) * tab_ref[2 * place + 1]
        inner = split_dot(nn, raw * scaled, members) / HD
        wide = split_dot(nt, factor, members)
        pulled = split_dot(nt, factor * factor * factor * inner, members)
        d_raw = (wide * scaled - raw * pulled).astype(BF16)
        total = total + nt(d_raw[:, :HALF], w_ref[place])
    mine_ref[...] = total[:ROWS].reshape(PEERS, TOK, D)
    theirs_ref[...] = total[ROWS:].reshape(PEERS, TOK, D).astype(BF16)


def turn_tables(qk_gain, core):
    frame = 2 * jnp.arange(PEERS, dtype=jnp.int32)
    position = jnp.concatenate([frame + core, frame + 1 - core]).astype(F32)
    column = jnp.arange(HD, dtype=jnp.int32)
    frequency = jnp.power(10000.0, -((2 * (column // 2)).astype(F32) / HD))
    angles = position[:, None] * frequency[None, :]
    cosine, sine = jnp.cos(angles), jnp.sin(angles)
    even = column % 2 == 0
    swapped = qk_gain.reshape(2, HD // 2, 2)[:, :, ::-1].reshape(2, HD)

    def spread(table):
        table = jnp.pad(jnp.tile(table, (1, 1, HALF // HD)), ((0, 0), (0, 0), (0, WIDE - HALF)))
        return jnp.broadcast_to(table[:, :, None, :], (4, 2 * PEERS, TOK, WIDE)).reshape(4, ALL, WIDE)

    straight = [qk_gain[i] * cosine for i in range(2)]
    ahead = [jnp.where(even, -sine, sine) * swapped[i] for i in range(2)]
    back = [jnp.where(even, sine, -sine) * qk_gain[i] for i in range(2)]
    return (
        spread(jnp.stack([straight[0], ahead[0], straight[1], ahead[1]])),
        spread(jnp.stack([straight[0], back[0], straight[1], back[1]])),
    )


def on_device(hidden, exponent, modulation, out_grad, w_qkv, w_out, qk_gain):
    core = lax.axis_index("c")
    zh = lax.axis_index("zh")
    rows, cotangent = hidden[0, 0], out_grad[0, 0]
    shift_by = exponent[0, 0]
    power = jnp.stack(
        [
            lax.shift_left(jnp.int32(1), shift_by).astype(F32),
            lax.shift_left(jnp.int32(1), 24 - shift_by).astype(F32) * 2.0**-24,
        ]
    )
    mod = lax.dynamic_index_in_dim(modulation[0], lax.axis_index("yh"), 0, keepdims=False)

    qkv_heads = w_qkv.reshape(HD, 3, 4, 2, 2 * HD)
    qkv_mine = lax.dynamic_index_in_dim(qkv_heads, core, 3, keepdims=False).reshape(HD, 3 * HALF)
    qkv_full = lax.all_gather(qkv_mine, CLIP, axis=0, tiled=True)
    out_full = lax.all_gather(w_out, CLIP, axis=0, tiled=True)
    w_in = jnp.stack([qkv_full[:, i * HALF : (i + 1) * HALF] for i in range(3)])
    w_back = lax.dynamic_index_in_dim(out_full.reshape(4, 2, 2 * HD, D), core, 1, keepdims=False).reshape(HALF, D)

    smem = pl.BlockSpec(memory_space=pltpu.SMEM)
    vmem = pl.BlockSpec(memory_space=pltpu.VMEM)
    sent = pl.pallas_call(
        home_forward,
        out_shape=jax.ShapeDtypeStruct((PEERS, 2 * TOK, D), BF16),
        in_specs=[smem, vmem, vmem, vmem],
        out_specs=vmem,
        compiler_params=PARAMS,
        cost_estimate=cost(20 * ROWS * D, 8 * ROWS * D),
    )(power, rows, cotangent, mod)
    own = lax.all_to_all(sent, ("yl", "zh"), 0, 0, tiled=True)
    other = lax.ppermute(own, "c", [(0, 1), (1, 0)])

    tables, tables_back = turn_tables(qk_gain, core)
    wide = jax.ShapeDtypeStruct((ALL, WIDE), BF16)
    factors = jax.ShapeDtypeStruct((ALL, 128), F32)
    part, *kept = pl.pallas_call(
        chip_forward,
        out_shape=[jax.ShapeDtypeStruct((HALF, D), BF16)] + [wide] * 5 + [factors] * 2,
        in_specs=[vmem] * 4,
        out_specs=[vmem] * 8,
        scratch_shapes=[pltpu.VMEM((ALL, WIDE), BF16)],
        compiler_params=PARAMS,
        cost_estimate=cost(2 * ALL * D * 4 * HALF, 12 * 10**6),
    )(own, other, w_in, tables)

    pieces = part.reshape(4, 4, 36, D).reshape(16, 36, D)
    plane = lax.all_to_all(pieces, ("yh", "yl", "x"), 0, 0, tiled=True)
    plane = jnp.sum(plane.astype(F32), axis=0).astype(BF16)
    plane = jnp.pad(plane, ((0, 12), (0, 0))).reshape(16, 3, D)

    mine, theirs = pl.pallas_call(
        chip_backward,
        out_shape=[jax.ShapeDtypeStruct((PEERS, TOK, D), F32), jax.ShapeDtypeStruct((PEERS, TOK, D), BF16)],
        in_specs=[vmem] * 12,
        out_specs=[vmem] * 2,
        scratch_shapes=[
            pltpu.VMEM((ALL, WIDE), BF16),
            pltpu.VMEM((ALL, WIDE), BF16),
            pltpu.VMEM((ALL, WIDE), F32),
            pltpu.VMEM((ALL, WIDE), F32),
        ],
        compiler_params=PARAMS,
        cost_estimate=cost(2 * ALL * D * 4 * HALF, 14 * 10**6),
    )(own, other, w_in, w_back, tables_back, *kept)
    arrived = lax.ppermute(theirs, "c", [(0, 1), (1, 0)])
    summed = (mine + arrived.astype(F32)).astype(BF16)
    back = lax.all_to_all(summed, ("yl", "zh"), 0, 0, tiled=True).reshape(ROWS, D)
    d_hidden = pl.pallas_call(
        home_backward,
        out_shape=jax.ShapeDtypeStruct((ROWS, D), BF16),
        in_specs=[smem, vmem, vmem, vmem, vmem],
        out_specs=vmem,
        compiler_params=PARAMS,
        cost_estimate=cost(30 * ROWS * D, 8 * ROWS * D),
    )(power, rows, cotangent, mod, back)

    levels = lax.all_to_all(plane, ("zh", "zl"), 0, 0, tiled=True)
    level = jnp.sum(levels.astype(F32), axis=0).astype(BF16)
    spread = lax.all_to_all(jnp.broadcast_to(level[None], (8, 3, D)), ("c", "x"), 0, 0, tiled=True)
    wanted = lax.dynamic_index_in_dim(spread.reshape(4, 2, 3, D), core, 1, keepdims=False)
    wanted = jnp.broadcast_to(wanted[:, None], (4, 4, 3, D)).reshape(16, 3, D)
    final = lax.all_to_all(wanted, ("zh", "zl"), 0, 0, tiled=True).reshape(48, D)[:36]
    return d_hidden[None, None], final.astype(F32) / 32.0


def solution(mesh):
    fine = Mesh(mesh.devices.reshape([size for _, size in FINE]), [name for name, _ in FINE])
    placed = (
        P(CLIP, SEQ, None, None),
        P(CLIP, SEQ),
        P(CLIP, None, None, None),
        P(CLIP, SEQ, None, None),
        P(CLIP, None),
        P(CLIP, None),
        P(),
    )
    return jax.shard_map(
        on_device,
        mesh=fine,
        in_specs=placed,
        out_specs=(P(CLIP, SEQ, None, None), P(SEQ, None)),
        check_vma=False,
    )
```

time: 695 us -> 325 us (0.47)
  waiting for transfers between devices: 356 us -> 192 us
  blocking collectives: 118 us -> 0 us
  local copies, waits for them, and re-layouts: 67.4 us -> 24.9 us
  matrix products: 42.4 us -> 0 us
  Pallas kernels: 0 us -> 25.6 us
  other arithmetic: 16.7 us -> 5.56 us
  starting transfers between devices: 68.9 us -> 60 us
    psum x1 -> x0, waiting for transfers between devices: 164 us -> none  [on_device(): lax.psum(grad_share.astype(jnp.bfloat16), 'clip').astype(jnp.float32)]
    unnamed x1 -> x0, blocking collectives: 118 us -> none
    dot_general x18 -> x0, matrix products: 42.4 us -> none  [the longest x8 14.4 us: exact_dot(): jnp.dot(left, right, precision=lax.Precision.HIGHEST, preferred_element_t...]
    unnamed x11 -> x2, waiting for transfers between devices: 29.6 us -> 0.71 us
    unnamed x8 -> x0, starting transfers between devices: 26.2 us -> none
    pallas_call x0 -> x4, Pallas kernels: none -> 25.6 us  [the longest x1 12.1 us: on_device(): pl.pallas_call(chip_backward, out_shape=[jax.ShapeDtypeStruct((PEERS, TOK...]
    all_to_all x4 -> x6, waiting for transfers between devices: 42 us -> 61.2 us  [the longest x1 27.5 us: on_device(): own = lax.all_to_all(sent, ('yl', 'zh'), 0, 0, tiled=True)]
    slice x18 -> x5, local copies, waits for them, and re-layouts: 16.1 us -> 0.37 us  [the longest x4 0.35 us: turn_tables(): ahead = [jnp.where(even, -sine, sine) * swapped[i] for i in range(2)]]
  transfers between devices with their start and end apart: 15 -> 10, of which waited for: 10 -> 6; matrix products, arithmetic and copies ran while one was open for 21% -> 6% of each run, Pallas kernels for 0% -> 8%
where the time goes in v1:
time: 325 us; the launch traced here: 323 us
  waiting for transfers between devices  192 us (59%)
  starting transfers between devices  60 us (18%)
  Pallas kernels  25.6 us (8%)
  local copies, waits for them, and re-layouts  24.9 us (8%)
  between operations  14.9 us (5%)
  other arithmetic  5.56 us (2%)
    all_gather x1, waiting for transfers between devices, on_device(): out_full = lax.all_gather(w_out, CLIP, axis=0, tiled=True)  65.9 us
    all_gather x1, waiting for transfers between devices, on_device(): qkv_full = lax.all_gather(qkv_mine, CLIP, axis=0, tiled=True)  64.3 us
    all_to_all x1, waiting for transfers between devices, on_device(): own = lax.all_to_all(sent, ('yl', 'zh'), 0, 0, tiled=True)  27.5 us
    all_to_all x1, waiting for transfers between devices, on_device(): lax.all_to_all(summed, ('yl', 'zh'), 0, 0, tiled=True).reshape(ROWS, D)  17.3 us
    all_to_all x1, starting transfers between devices, on_device(): own = lax.all_to_all(sent, ('yl', 'zh'), 0, 0, tiled=True)  16.5 us
    all_to_all x1, starting transfers between devices, on_device(): lax.all_to_all(summed, ('yl', 'zh'), 0, 0, tiled=True).reshape(ROWS, D)  13.4 us
    all_to_all x1, waiting for transfers between devices, on_device(): lax.all_to_all(wanted, ('zh', 'zl'), 0, 0, tiled=True).reshape(48, D)[:36]  12.9 us
    pallas_call x1, Pallas kernels, on_device(): pl.pallas_call(chip_backward, out_shape=[jax.ShapeDtypeStruct((PEERS, TOK...  12.1 us
  transfers between devices with their start and end apart: 10, of which 6 were waited for; matrix products, arithmetic and copies ran while one was open for 6% of the time, Pallas kernels for 8%

profile of v1, /device:TPU:24, one launch (start us, length us, event | category | flops | bytes accessed | tf_op | source)
XLA Modules:
  0.0 323.1 jit_solution(14014105079252426471)
XLA Ops:
  7.2 4.0 %reshape.605 = bf16[72,3,4,2,144]{4,3,2,1,0:T(2,128)(2,1)S(1)} reshape(bf16[72,3456]{1,0:T(8,128)(2,1)} %param.11) | data formatting | bytes 995328 | tf_op jit(solution)/shard_map/reshape | solution.py:226
  11.2 3.0 dynamic-slice_reduce_fusion
  14.2 1.0 reshape.606
  15.3 0.7 all-gather.5.cloned.1.call-update
  18.0 2.2 shard_map.86
  20.2 16.5 %all-to-all-start = ((bf16[8,32,1152]{2,1,0:T(8,128)(2,1)}), bf16[8,32,1152]{2,1,0:T(8,128)(2,1)S(1)}, u32[]{:S(2)}, u32[]{:S(2)}) async-start(bf16[8,32,1152]{2,1,0:T(8,128)(2,1)} %shard_map.86), calls=%async_computation | async-start | bytes 1179648 | tf_op jit(solution)/shard_map/all_to_all | solution.py:243
  37.8 27.5 %all-to-all-done.own_ref = bf16[8,32,1152]{2,1,0:T(8,128)(2,1)S(1)} async-done(((bf16[8,32,1152]{2,1,0:T(8,128)(2,1)}), bf16[8,32,1152]{2,1,0:T(8,128)(2,1)S(1)}, u32[]{:S(2)}, u32[]{:S(2)}) %all-to-all-start) | async-done | bytes 589856 | tf_op jit(solution)/shard_map/all_to_all | solution.py:243
  65.3 2.1 collective-permute-start
  67.4 64.3 %all-gather.3.cloned.1.call-done = bf16[1152,1728]{1,0:T(8,128)(2,1)} async-done(((bf16[72,1728]{1,0:T(8,128)(2,1)}), bf16[1152,1728]{1,0:T(8,128)(2,1)}) %all-gather.3.cloned.1.call-update) | async-done | bytes 3981328 | tf_op jit(solution)/shard_map/all_gather | solution.py:228
  131.7 3.3 %slice_bitcast_fusion.2 = (bf16[1,1152,576]{2,1,0:T(8,128)(2,1)S(1)}, bf16[1,1152,576]{2,1,0:T(8,128)(2,1)S(1)}, bf16[1,1152,576]{2,1,0:T(8,128)(2,1)S(1)}) fusion(bf16[1152,1728]{1,0:T(8,128)(2,1)} %all-gather.3.cloned.1.call-done), kind=kLoop, calls=%fused_computation.3 | loop fusion | bytes 7962624 | tf_op jit(solution)/shard_map/stack | solution.py:230
  135.0 2.4 pad_maximum_fusion.w_ref
  137.5 1.7 broadcast_in_dim.42
  139.2 8.9 %shard_map.87 = (bf16[576,1152]{1,0:T(8,128)(2,1)}, bf16[256,640]{1,0:T(8,128)(2,1)}, bf16[256,640]{1,0:T(8,128)(2,1)}, bf16[256,640]{1,0:T(8,128)(2,1)}, bf16[2...) custom-call(bf16[8,32,1152]{2,1,0:T(8,128)(2,1)} %copy-done.1, ...), custom_call_target="tpu_custom_call" | custom-call | flops 1358954496 | bytes 12000000 | tf_op jit(solution)/shard_map/pallas_call | solution.py:249
  148.1 3.2 reshape_reshape.3
  151.3 5.2 %all-to-all-start.2 = ((bf16[16,36,1152]{2,1,0:T(8,128)(2,1)}), bf16[16,36,1152]{2,1,0:T(8,128)(2,1)S(1)}, u32[]{:S(2)}, u32[]{:S(2)}) async-start(bf16[16,36,1152]{2,1,0:T(8,128)(2,1)} %reshape_reshape.3), calls=%async_computation.2 | async-start | bytes 2949120 | tf_op jit(solution)/shard_map/all_to_all | solution.py:260
  156.7 65.9 %all-gather.5.cloned.1.call-done = bf16[1152,1152]{1,0:T(8,128)(2,1)} async-done(((bf16[72,1152]{1,0:T(8,128)(2,1)}), bf16[1152,1152]{1,0:T(8,128)(2,1)}) %all-gather.5.cloned.1.call-update) | async-done | bytes 2654224 | tf_op jit(solution)/shard_map/all_gather | solution.py:229
  222.6 2.5 constant_dynamic-slice_fusion
  225.4 0.7 reshape.612
  226.2 8.7 %all-to-all-start.3 = ((bf16[16,3,1152]{2,1,0:T(4,128)(2,1)}), bf16[16,3,1152]{2,1,0:T(4,128)(2,1)S(1)}, u32[]{:S(2)}, u32[]{:S(2)}) async-start(bf16[16,3,1152]{2,1,0:T(4,128)(2,1)} %reshape.612), calls=%async_computation.3 | async-start | bytes 294912 | tf_op jit(solution)/shard_map/all_to_all | solution.py:290
  234.9 1.7 broadcast_in_dim.41
  236.6 12.1 %shard_map.88 = (f32[8,16,1152]{2,1,0:T(8,128)}, bf16[8,16,1152]{2,1,0:T(8,128)(2,1)}) custom-call(bf16[8,32,1152]{2,1,0:T(8,128)(2,1)} %copy-done.1, bf16[8,32,1152]{2,1,0:T(8,128)(2,1)} %copy-done.2, bf16[3,1152,576]{2,1,0:T(8,128)(2,1)} %pad_maximum_fusion.w_ref, bf16[576,1152]{1,0:T(8,128)(2,1)} %bitcast.37, f32[4,256,640]{2,1,0:T(8,128)} %bitcast.36, ...), custom_call_target="tpu_custom_call" | custom-call | flops 1358954496 | bytes 14000000 | tf_op jit(solution)/shard_map/pallas_call | solution.py:264
  248.7 1.9 collective-permute-start.1
  251.3 3.9 %all-to-all-start.4 = ((bf16[8,3,1152]{2,1,0:T(4,128)(2,1)}), bf16[8,3,1152]{2,1,0:T(4,128)(2,1)S(1)}, u32[]{:S(2)}, u32[]{:S(2)}) async-start(bf16[8,3,1152]{2,1,0:T(4,128)(2,1)} %broadcast_in_dim.44), calls=%async_computation.4 | async-start | bytes 147456 | tf_op jit(solution)/shard_map/all_to_all | solution.py:292
  255.3 1.8 add_convert_fusion
  257.1 3.5 %all-to-all-done.4 = bf16[8,3,1152]{2,1,0:T(4,128)(2,1)S(1)} async-done(((bf16[8,3,1152]{2,1,0:T(4,128)(2,1)}), bf16[8,3,1152]{2,1,0:T(4,128)(2,1)S(1)}, u32[]{:S(2)}, u32[]{:S(2)}) %all-to-all-start.4) | async-done | bytes 55328 | tf_op jit(solution)/shard_map/all_to_all | solution.py:292
  260.6 13.4 %all-to-all-start.1 = ((bf16[8,16,1152]{2,1,0:T(8,128)(2,1)}), bf16[8,16,1152]{2,1,0:T(8,128)(2,1)S(1)}, u32[]{:S(2)}, u32[]{:S(2)}) async-start(bf16[8,16,1152]{2,1,0:T(8,128)(2,1)} %add_convert_fusion), calls=%async_computation.1 | async-start | bytes 589824 | tf_op jit(solution)/shard_map/all_to_all | solution.py:280
  274.0 17.3 %all-to-all-done.1 = bf16[8,16,1152]{2,1,0:T(8,128)(2,1)S(1)} async-done(((bf16[8,16,1152]{2,1,0:T(8,128)(2,1)}), bf16[8,16,1152]{2,1,0:T(8,128)(2,1)S(1)}, u32[]{:S(2)}, u32[]{:S(2)}) %all-to-all-start.1) | async-done | bytes 294944 | tf_op jit(solution)/shard_map/all_to_all | solution.py:280
  291.3 0.8 broadcast_in_dim.46
  292.0 8.1 %all-to-all-start.5 = ((bf16[16,3,1152]{2,1,0:T(4,128)(2,1)}), bf16[16,3,1152]{2,1,0:T(4,128)(2,1)S(1)}, u32[]{:S(2)}, u32[]{:S(2)}) async-start(bf16[16,3,1152]{2,1,0:T(4,128)(2,1)} %bitcast.17), calls=%async_computation.5 | async-start | bytes 294912 | tf_op jit(solution)/shard_map/all_to_all | solution.py:295
  300.2 2.4 shard_map.89
  302.5 12.9 %all-to-all-done.5 = bf16[16,3,1152]{2,1,0:T(4,128)(2,1)S(1)} async-done(((bf16[16,3,1152]{2,1,0:T(4,128)(2,1)}), bf16[16,3,1152]{2,1,0:T(4,128)(2,1)S(1)}, u32[]{:S(2)}, u32[]{:S(2)}) %all-to-all-start.5) | async-done | bytes 110624 | tf_op jit(solution)/shard_map/all_to_all | solution.py:295
  315.5 0.8 div.25
  (45 shorter events, 3.6 us)
Async XLA Ops:
  7.2 9.5 %copy-start = (f32[1,2,3,1152]{3,1,2,0:T(2,128)S(1)}, f32[1,2,3,1152]{3,1,2,0:T(2,128)}, u32[]{:S(2)}) copy-start(f32[1,2,3,1152]{3,1,2,0:T(2,128)} %param.9) | copy-start | bytes 82948
  7.2 124.5 %all-gather.3.cloned.1.call-start = ((), (), s32[]{:S(2)}) async-start(), calls=%async_computation.6 | async-start | bytes 4386816 | tf_op jit(solution)/shard_map/all_gather | solution.py:228
  15.2 21.5 %copy-start.4 = (f32[2,72]{1,0:T(2,128)S(1)}, f32[2,72]{1,0:T(2,128)}, u32[]{:S(2)}) copy-start(f32[2,72]{1,0:T(2,128)} %param.13) | copy-start | bytes 1732
  15.2 207.4 %all-gather.5.cloned.1.call-start = ((), (), s32[]{:S(2)}) async-start(), calls=%async_computation.7 | async-start | bytes 2820096 | tf_op jit(solution)/shard_map/all_gather | solution.py:229
  20.2 45.1 %all-to-all-start = ((bf16[8,32,1152]{2,1,0:T(8,128)(2,1)}), bf16[8,32,1152]{2,1,0:T(8,128)(2,1)S(1)}, u32[]{:S(2)}, u32[]{:S(2)}) async-start(bf16[8,32,1152]{2,1,0:T(8,128)(2,1)} %shard_map.86), calls=%async_computation | async-start | bytes 1179648 | tf_op jit(solution)/shard_map/all_to_all | solution.py:243
  65.3 69.7 %copy-start.1 = (bf16[8,32,1152]{2,1,0:T(8,128)(2,1)}, bf16[8,32,1152]{2,1,0:T(8,128)(2,1)S(1)}, u32[]{:S(2)}) copy-start(bf16[8,32,1152]{2,1,0:T(8,128)(2,1)S(1)} %all-to-all-done.own_ref) | copy-start | bytes 1769476
  65.3 72.2 %collective-permute-start = (bf16[8,32,1152]{2,1,0:T(8,128)(2,1)S(1)}, bf16[8,32,1152]{2,1,0:T(8,128)(2,1)S(1)}, u32[]{:S(2)}, u32[]{:S(2)}) collective-permute-start(bf16[8,32,1152]{2,1,0:T(8,128)(2,1)S(1)} %all-to-all-done.own_ref), channel_id=1, source_target_pairs={{0,16},{16,0},{1,17},{17,1},{2,18},{18,2},{3,19},{19,3},{4,20},{20... | collective-permute-start | bytes 1769480 | tf_op jit(solution)/shard_map/ppermute | solution.py:244
  137.5 1.7 copy-start.2
  151.3 73.8 %all-to-all-start.2 = ((bf16[16,36,1152]{2,1,0:T(8,128)(2,1)}), bf16[16,36,1152]{2,1,0:T(8,128)(2,1)S(1)}, u32[]{:S(2)}, u32[]{:S(2)}) async-start(bf16[16,36,1152]{2,1,0:T(8,128)(2,1)} %reshape_reshape.3), calls=%async_computation.2 | async-start | bytes 2949120 | tf_op jit(solution)/shard_map/all_to_all | solution.py:260
  226.2 24.4 %all-to-all-start.3 = ((bf16[16,3,1152]{2,1,0:T(4,128)(2,1)}), bf16[16,3,1152]{2,1,0:T(4,128)(2,1)S(1)}, u32[]{:S(2)}, u32[]{:S(2)}) async-start(bf16[16,3,1152]{2,1,0:T(4,128)(2,1)} %reshape.612), calls=%async_computation.3 | async-start | bytes 294912 | tf_op jit(solution)/shard_map/all_to_all | solution.py:290
  248.7 6.6 %collective-permute-start.1 = (bf16[8,16,1152]{2,1,0:T(8,128)(2,1)}, bf16[8,16,1152]{2,1,0:T(8,128)(2,1)S(1)}, u32[]{:S(2)}, u32[]{:S(2)}) collective-permute-start(bf16[8,16,1152]{2,1,0:T(8,128)(2,1)} %get-tuple-element.20), channel_id=1, source_target_pairs={{0,16},{16,0},{1,17},{17,1},{2,18},{18,2},{3,19},{19,3},{4,20},{20... | collective-permute-start | bytes 884744 | tf_op jit(solution)/shard_map/ppermute | solution.py:278
  251.3 9.3 %all-to-all-start.4 = ((bf16[8,3,1152]{2,1,0:T(4,128)(2,1)}), bf16[8,3,1152]{2,1,0:T(4,128)(2,1)S(1)}, u32[]{:S(2)}, u32[]{:S(2)}) async-start(bf16[8,3,1152]{2,1,0:T(4,128)(2,1)} %broadcast_in_dim.44), calls=%async_computation.4 | async-start | bytes 147456 | tf_op jit(solution)/shard_map/all_to_all | solution.py:292
  260.6 30.6 %all-to-all-start.1 = ((bf16[8,16,1152]{2,1,0:T(8,128)(2,1)}), bf16[8,16,1152]{2,1,0:T(8,128)(2,1)S(1)}, u32[]{:S(2)}, u32[]{:S(2)}) async-start(bf16[8,16,1152]{2,1,0:T(8,128)(2,1)} %add_convert_fusion), calls=%async_computation.1 | async-start | bytes 589824 | tf_op jit(solution)/shard_map/all_to_all | solution.py:280
  291.3 8.9 %copy-start.3 = (bf16[8,16,1152]{2,1,0:T(8,128)(2,1)}, bf16[8,16,1152]{2,1,0:T(8,128)(2,1)S(1)}, u32[]{:S(2)}) copy-start(bf16[8,16,1152]{2,1,0:T(8,128)(2,1)S(1)} %all-to-all-done.1) | copy-start | bytes 884740
  292.0 23.4 %all-to-all-start.5 = ((bf16[16,3,1152]{2,1,0:T(4,128)(2,1)}), bf16[16,3,1152]{2,1,0:T(4,128)(2,1)S(1)}, u32[]{:S(2)}, u32[]{:S(2)}) async-start(bf16[16,3,1152]{2,1,0:T(4,128)(2,1)} %bitcast.17), calls=%async_computation.5 | async-start | bytes 294912 | tf_op jit(solution)/shard_map/all_to_all | solution.py:295
Sparse Core Ops, SparseCore 0:
  15.4 116.3 all-gather.2
  133.8 88.7 all-gather.4

commit v2 on v1

v2 whole, which is shorter than its diff:
```python
import jax
import jax.numpy as jnp
from jax import lax
from jax.experimental import pallas as pl
from jax.experimental.pallas import tpu as pltpu
from jax.sharding import Mesh
from jax.sharding import PartitionSpec as P

FINE = (("yh", 2), ("yl", 2), ("zh", 4), ("c", 2), ("zl", 4), ("x", 4))
SEQ = ("yh", "yl", "zh", "c")
CLIP = ("zl", "x")
D = 1152
HD = 72
PART = 288
WIDE = 384
HEADS = 4
ZS = 4
TOK = 32
ROWS = ZS * TOK
ALL = 4 * ROWS
BLOCK = 256
F32 = jnp.float32
BF16 = jnp.bfloat16
EPS = 1e-06
TEMPER = HD ** (-0.5)
PARAMS = pltpu.CompilerParams(vmem_limit_bytes=56 * 1024 * 1024)


def cost(flops, nbytes):
    return pl.CostEstimate(flops=flops, bytes_accessed=nbytes, transcendentals=0)


def normalise(hidden, power, inverse):
    scaled = jnp.clip(hidden.astype(F32) * power, -448.0, 448.0)
    rows = scaled * inverse
    centred = rows - jnp.mean(rows, axis=-1, keepdims=True)
    factor = lax.rsqrt(jnp.mean(centred * centred, axis=-1, keepdims=True) + EPS)
    return centred * factor, factor


def home_forward(power_ref, x_ref, hidden_ref, grad_ref, mod_ref, out_ref, branch_ref, turned_ref):
    normed, _ = normalise(hidden_ref[...], power_ref[0], power_ref[1])
    modded = normed * (1.0 + mod_ref[1:2, :]) + mod_ref[0:1, :]
    for x in range(4):

        @pl.when(x_ref[0] == x)
        def _(x=x):
            for place, block in enumerate(block_order(x)):
                turned_ref[:, place * HD : (place + 1) * HD] = modded[:, block * HD : (block + 1) * HD]

    out_ref[...] = turned_ref[...].astype(BF16).reshape(ZS, TOK, D)
    branch_ref[...] = (mod_ref[2:3, :] * grad_ref[...].astype(F32)).astype(BF16).reshape(ZS, TOK, D)


def home_backward(power_ref, x_ref, hidden_ref, grad_ref, mod_ref, back_ref, out_ref, turned_ref):
    normed, factor = normalise(hidden_ref[...], power_ref[0], power_ref[1])
    back = back_ref[...].astype(F32)
    for x in range(4):

        @pl.when(x_ref[0] == x)
        def _(x=x):
            for place, block in enumerate(block_order(x)):
                turned_ref[:, block * HD : (block + 1) * HD] = back[:, place * HD : (place + 1) * HD]

    d_normed = turned_ref[...] * (1.0 + mod_ref[1:2, :])
    d_rows = factor * (
        d_normed
        - jnp.mean(d_normed, axis=-1, keepdims=True)
        - normed * jnp.mean(d_normed * normed, axis=-1, keepdims=True)
    )
    out_ref[...] = (grad_ref[...].astype(F32) + d_rows.astype(BF16).astype(F32)).astype(BF16)


def block_order(x):
    return [4 * zl + (x + step) % 4 for step in range(4) for zl in range(4)]


def pick_weights(place_ref, w_qkv_ref, w_out_ref, out_ref, unit_ref):
    qkv = w_qkv_ref[...].astype(F32)
    out = w_out_ref[...].astype(F32)
    for place in range(4):

        @pl.when(place_ref[0] == place)
        def _(place=place):
            yl, core = place // 2, place % 2
            for part in range(3):
                for high in range(2):
                    first = part * D + HD * (4 * (2 * high + yl) + 2 * core)
                    to = part * PART + high * 2 * HD
                    unit_ref[:, to : to + 2 * HD] = qkv[:, first : first + 2 * HD]
            unit_ref[:, 3 * PART :] = out[:, place * PART : (place + 1) * PART]

    unit = unit_ref[...].astype(BF16)
    for copy in range(4):
        out_ref[copy] = unit


def out_rows(x_ref, *refs):
    *block_refs, send_ref, rows_ref, sem = refs
    copies = [
        pltpu.make_async_copy(ref.at[:, pl.ds(768, 384)], rows_ref.at[step], sem.at[step])
        for step, ref in enumerate(block_refs)
    ]
    for copy in copies:
        copy.start()
    for copy in copies:
        copy.wait()
    blocks = [rows_ref[step].astype(F32)[:, 96:384] for step in range(4)]
    for x in range(4):

        @pl.when(x_ref[0] == x)
        def _(x=x):
            for place in range(4):
                yl, core = place // 2, place % 2
                pieces = []
                for high in range(2):
                    for low in range(2):
                        first = (2 * high + yl) * HD
                        pieces.append(blocks[(2 * core + low - x) % 4][first : first + HD])
                send_ref[place] = jnp.concatenate(pieces, axis=0).astype(BF16)


def nt(left, right):
    return lax.dot_general(left, right, (((1,), (1,)), ((), ())), preferred_element_type=F32)


def nn(left, right):
    return lax.dot_general(left, right, (((1,), (0,)), ((), ())), preferred_element_type=F32)


def tn(left, right):
    return lax.dot_general(left, right, (((0,), (0,)), ((), ())), preferred_element_type=F32)


def swap_pairs(values):
    parity = lax.broadcasted_iota(jnp.int32, (values.shape[0], 128), 1) % 2
    tiles = []
    for start in range(0, values.shape[1], 128):
        tile = values[:, start : start + 128]
        tiles.append(jnp.where(parity == 0, pltpu.roll(tile, 127, 1), pltpu.roll(tile, 1, 1)))
    return jnp.concatenate(tiles, axis=1)


def head_members():
    entry = lax.broadcasted_iota(jnp.int32, (WIDE, 128), 0)
    first = lax.broadcasted_iota(jnp.int32, (WIDE, 128), 1) * HD
    return ((entry >= first) & (entry < first + HD) & (entry < PART)).astype(F32).astype(BF16)


def split_dot(dot, values, members):
    high = values.astype(BF16)
    low = (values - high.astype(F32)).astype(BF16)
    return dot(high, members) + dot(low, members)


def window(head):
    start = head * HD // 128 * 128
    end = -(-(head + 1) * HD // 128) * 128
    column = lax.broadcasted_iota(jnp.int32, (BLOCK, end - start), 1) + start
    return start, end, (column >= head * HD) & (column < (head + 1) * HD)


def keep(values, mask):
    return jnp.where(mask, values, jnp.zeros_like(values))


def same_token():
    row = lax.broadcasted_iota(jnp.int32, (BLOCK, BLOCK), 0) % 16
    column = lax.broadcasted_iota(jnp.int32, (BLOCK, BLOCK), 1) % 16
    return row == column


def probabilities(q_hat, k_hat, same):
    scores = nt(q_hat, k_hat) * TEMPER
    exps = jnp.where(same, jnp.exp(scores), 0.0)
    return exps / jnp.sum(exps, axis=-1, keepdims=True)


def gather_rows(refs):
    return jnp.concatenate(
        [ref[:, first : first + 16, :].reshape(ZS * 16, D) for first in (0, 16) for ref in refs], axis=0
    )


def fetch_weights(block_refs, w_ref, sem):
    copies = [
        pltpu.make_async_copy(ref, w_ref.at[pl.ds(PART * step, PART), :], sem.at[step])
        for step, ref in enumerate(block_refs)
    ]
    for copy in copies:
        copy.start()
    return copies


def widen(values):
    return jnp.concatenate([values, jnp.zeros((values.shape[0], WIDE - PART), values.dtype)], axis=1)


def chip_forward(*refs):
    row_refs, block_refs, (tab_ref, q_ref, k_ref, v_ref, qh_ref, kh_ref, qf_ref, kf_ref, att_ref, w_ref, sem) = (
        refs[:4], refs[4:8], refs[8:]
    )
    copies = fetch_weights(block_refs, w_ref, sem)
    modded = gather_rows(row_refs)
    members = head_members()
    for copy in copies:
        copy.wait()
    packed = nn(modded, w_ref[:, : 7 * 128])
    for place, (raw_ref, hat_ref, factor_ref) in enumerate(((q_ref, qh_ref, qf_ref), (k_ref, kh_ref, kf_ref))):
        raw = widen(packed[:, place * PART : (place + 1) * PART])
        raw_ref[...] = raw.astype(BF16)
        raw = raw_ref[...].astype(F32)
        factor = lax.rsqrt(split_dot(nn, raw * raw, members) / HD + EPS)
        factor_ref[...] = factor
        wide = split_dot(nt, factor, members)
        swapped = swap_pairs(raw)
        for half in range(2):
            rows = slice(half * BLOCK, (half + 1) * BLOCK)
            turned = raw[rows] * tab_ref[2 * place] + swapped[rows] * tab_ref[2 * place + 1]
            hat_ref[rows, :] = (wide[rows] * turned).astype(BF16)
    v_ref[...] = widen(packed[:, 2 * PART : 3 * PART]).astype(BF16)
    same = same_token()
    att_ref[...] = jnp.zeros_like(att_ref)
    for head in range(HEADS):
        start, end, mask = window(head)
        for half in range(2):
            rows = slice(half * BLOCK, (half + 1) * BLOCK)
            probs = probabilities(keep(qh_ref[rows, start:end], mask), kh_ref[rows, start:end], same).astype(BF16)
            found = nn(probs, v_ref[rows, start:end]).astype(BF16)
            att_ref[rows, start:end] = jnp.where(mask, found, att_ref[rows, start:end])


def chip_term(*refs):
    row_refs, (att_ref, part_ref) = refs[:4], refs[4:]
    part_ref[...] = tn(att_ref[...], gather_rows(row_refs))[:PART].astype(BF16)


def chip_backward(*refs):
    row_refs, block_refs = refs[:4], refs[4:8]
    (
        wo_ref, tab_ref, q_ref, k_ref, v_ref, qh_ref, kh_ref, qf_ref, kf_ref,
        mine_ref, theirs_ref, do_ref, dv_ref, dqh_ref, dkh_ref, dqkv_ref, wide_ref, w_ref, sem,
    ) = refs[8:]
    copies = fetch_weights(block_refs, w_ref, sem)
    for place in range(4):
        wide_ref[:, place * PART : (place + 1) * PART] = wo_ref[place].astype(F32)
    do_ref[...] = widen(nt(gather_rows(row_refs), wide_ref[...].astype(BF16))).astype(BF16)
    same = same_token()
    members = head_members()
    for ref in (dv_ref, dqh_ref, dkh_ref):
        ref[...] = jnp.zeros_like(ref)
    for head in range(HEADS):
        start, end, mask = window(head)
        for half in range(2):
            rows = slice(half * BLOCK, (half + 1) * BLOCK)
            q_hat, k_hat = qh_ref[rows, start:end], kh_ref[rows, start:end]
            probs = probabilities(keep(q_hat, mask), k_hat, same)
            d_out = do_ref[rows, start:end]
            d_probs = nt(keep(d_out, mask), v_ref[rows, start:end])
            d_value = tn(probs.astype(BF16), d_out)
            spread = probs * d_probs
            d_scores = ((spread - probs * jnp.sum(spread, axis=-1, keepdims=True)) * TEMPER).astype(BF16)
            d_q = nn(d_scores, k_hat)
            d_k = tn(d_scores, q_hat)
            dv_ref[rows, start:end] = jnp.where(mask, d_value, dv_ref[rows, start:end])
            dqh_ref[rows, start:end] = jnp.where(mask, d_q, dqh_ref[rows, start:end])
            dkh_ref[rows, start:end] = jnp.where(mask, d_k, dkh_ref[rows, start:end])
    dqkv_ref[:, 3 * PART :] = jnp.zeros((ALL, 7 * 128 - 3 * PART), F32)
    dqkv_ref[:, 2 * PART : 3 * PART] = dv_ref[:, :PART]
    for place, (raw_ref, factor_ref, turned_ref) in enumerate(
        ((q_ref, qf_ref, dqh_ref), (k_ref, kf_ref, dkh_ref))
    ):
        raw = raw_ref[...].astype(F32)
        factor = factor_ref[...]
        turned = turned_ref[...]
        swapped = swap_pairs(turned)
        scaled = jnp.concatenate(
            [
                turned[first : first + BLOCK] * tab_ref[2 * place]
                + swapped[first : first + BLOCK] * tab_ref[2 * place + 1]
                for first in (0, BLOCK)
            ],
            axis=0,
        )
        inner = split_dot(nn, raw * scaled, members) / HD
        wide = split_dot(nt, factor, members)
        pulled = split_dot(nt, factor * factor * factor * inner, members)
        dqkv_ref[:, place * PART : (place + 1) * PART] = (wide * scaled - raw * pulled)[:, :PART]
    for copy in copies:
        copy.wait()
    total = nt(dqkv_ref[...].astype(BF16), w_ref[:, : 7 * 128])
    for half in range(2):
        for device in range(4):
            first = half * BLOCK + device * ZS * 16
            rows = total[first : first + ZS * 16].reshape(ZS, 16, D)
            out_ref = theirs_ref if device % 2 else mine_ref
            out_ref[device // 2, :, half * 16 : half * 16 + 16, :] = rows.astype(out_ref.dtype)


def turn_tables(qk_gain, yl, core):
    level = 2 * jnp.arange(ZS, dtype=jnp.int32)
    position = jnp.concatenate(
        [8 * y + level + c for y in (yl, 1 - yl) for c in (core, 1 - core)]
    ).astype(F32)
    column = jnp.arange(HD, dtype=jnp.int32)
    frequency = jnp.power(10000.0, -((2 * (column // 2)).astype(F32) / HD))
    angles = position[:, None] * frequency[None, :]
    cosine, sine = jnp.cos(angles), jnp.sin(angles)
    even = column % 2 == 0
    swapped = qk_gain.reshape(2, HD // 2, 2)[:, :, ::-1].reshape(2, HD)

    def spread(table):
        table = jnp.pad(jnp.tile(table, (1, 1, HEADS)), ((0, 0), (0, 0), (0, WIDE - PART)))
        return jnp.broadcast_to(table[:, :, None, :], (4, 16, 16, WIDE)).reshape(4, BLOCK, WIDE)

    straight = [qk_gain[i] * cosine for i in range(2)]
    ahead = [jnp.where(even, -sine, sine) * swapped[i] for i in range(2)]
    back = [jnp.where(even, sine, -sine) * qk_gain[i] for i in range(2)]
    return (
        spread(jnp.stack([straight[0], ahead[0], straight[1], ahead[1]])),
        spread(jnp.stack([straight[0], back[0], straight[1], back[1]])),
    )


def on_device(hidden, exponent, modulation, out_grad, w_qkv, w_out, qk_gain):
    core, yl, x = lax.axis_index("c"), lax.axis_index("yl"), lax.axis_index("x")
    rows, cotangent = hidden[0, 0], out_grad[0, 0]
    shift_by = exponent[0, 0]
    power = jnp.stack(
        [
            lax.shift_left(jnp.int32(1), shift_by).astype(F32),
            lax.shift_left(jnp.int32(1), 24 - shift_by).astype(F32) * 2.0**-24,
        ]
    )
    mod = lax.dynamic_index_in_dim(modulation[0], lax.axis_index("yh"), 0, keepdims=False)
    x_place = x[None]
    smem = pl.BlockSpec(memory_space=pltpu.SMEM)
    vmem = pl.BlockSpec(memory_space=pltpu.VMEM)
    hbm = pl.BlockSpec(memory_space=pl.ANY)
    four = pltpu.SemaphoreType.DMA((4,))

    unit = pl.pallas_call(
        pick_weights,
        out_shape=jax.ShapeDtypeStruct((4, HD, 4 * PART), BF16),
        in_specs=[smem, vmem, vmem],
        out_specs=vmem,
        scratch_shapes=[pltpu.VMEM((HD, 4 * PART), F32)],
        compiler_params=PARAMS,
        cost_estimate=cost(10**6, 2 * 10**6),
    )((2 * yl + core)[None], w_qkv, w_out)
    block = lax.all_to_all(unit, "zl", 0, 0, tiled=True).reshape(PART, 4 * PART)
    blocks = [block] + [
        lax.ppermute(block, "x", [(i, (i + 4 - step) % 4) for i in range(4)]) for step in (1, 2, 3)
    ]

    sent, sent_branch = pl.pallas_call(
        home_forward,
        out_shape=[jax.ShapeDtypeStruct((ZS, TOK, D), BF16)] * 2,
        in_specs=[smem, smem, vmem, vmem, vmem],
        out_specs=[vmem, vmem],
        scratch_shapes=[pltpu.VMEM((ROWS, D), F32)],
        compiler_params=PARAMS,
        cost_estimate=cost(20 * ROWS * D, 8 * ROWS * D),
    )(power, x_place, rows, cotangent, mod)

    def other_core(values):
        return lax.ppermute(values, "c", [(0, 1), (1, 0)])

    def other_y(values):
        return lax.ppermute(values, "yl", [(0, 1), (1, 0)])

    def from_frames(values):
        own = lax.all_to_all(values, "zh", 0, 0, tiled=True)
        across = other_y(own)
        return [own, other_core(own), across, other_core(across)]

    modded = from_frames(sent)
    branch = from_frames(sent_branch)
    w_back = pl.pallas_call(
        out_rows,
        out_shape=jax.ShapeDtypeStruct((4, PART, PART), BF16),
        in_specs=[smem] + [hbm] * 4,
        out_specs=vmem,
        scratch_shapes=[pltpu.VMEM((4, PART, 384), BF16), four],
        compiler_params=PARAMS,
        cost_estimate=cost(10**6, 2 * 10**6),
    )(x_place, *blocks)
    w_back = lax.all_to_all(w_back, ("yl", "c"), 0, 0, tiled=True)

    tables, tables_back = turn_tables(qk_gain, yl, core)
    wide = jax.ShapeDtypeStruct((ALL, WIDE), BF16)
    factors = jax.ShapeDtypeStruct((ALL, 128), F32)
    *kept, attended = pl.pallas_call(
        chip_forward,
        out_shape=[wide] * 5 + [factors] * 2 + [wide],
        in_specs=[vmem] * 4 + [hbm] * 4 + [vmem],
        out_specs=[vmem] * 8,
        scratch_shapes=[pltpu.VMEM((D, D), BF16), four],
        compiler_params=PARAMS,
        cost_estimate=cost(2 * ALL * D * 4 * PART, 12 * 10**6),
    )(*modded, *blocks, tables)
    part = pl.pallas_call(
        chip_term,
        out_shape=jax.ShapeDtypeStruct((PART, D), BF16),
        in_specs=[vmem] * 5,
        out_specs=vmem,
        compiler_params=PARAMS,
        cost_estimate=cost(2 * ALL * D * PART, 2 * 10**6),
    )(*branch, attended)

    plane = lax.all_to_all(part.reshape(8, 36, D), ("yh", "x"), 0, 0, tiled=True)
    plane = jnp.sum(plane.astype(F32), axis=0).astype(BF16)
    plane = jnp.pad(plane, ((0, 12), (0, 0))).reshape(16, 3, D)

    mine, theirs = pl.pallas_call(
        chip_backward,
        out_shape=[jax.ShapeDtypeStruct((2, ZS, TOK, D), F32), jax.ShapeDtypeStruct((2, ZS, TOK, D), BF16)],
        in_specs=[vmem] * 4 + [hbm] * 4 + [vmem] * 9,
        out_specs=[vmem] * 2,
        scratch_shapes=[
            pltpu.VMEM((ALL, WIDE), BF16),
            pltpu.VMEM((ALL, WIDE), F32),
            pltpu.VMEM((ALL, WIDE), F32),
            pltpu.VMEM((ALL, WIDE), F32),
            pltpu.VMEM((ALL, 7 * 128), F32),
            pltpu.VMEM((PART, D), F32),
            pltpu.VMEM((D, D), BF16),
            four,
        ],
        compiler_params=PARAMS,
        cost_estimate=cost(2 * ALL * D * 4 * PART, 14 * 10**6),
    )(*branch, *blocks, w_back, tables_back, *kept)
    arrived = other_core(theirs)
    across = (mine[1] + arrived[1].astype(F32)).astype(BF16)
    summed = (mine[0] + arrived[0].astype(F32) + other_y(across).astype(F32)).astype(BF16)
    back = lax.all_to_all(summed, "zh", 0, 0, tiled=True).reshape(ROWS, D)
    d_hidden = pl.pallas_call(
        home_backward,
        out_shape=jax.ShapeDtypeStruct((ROWS, D), BF16),
        in_specs=[smem, smem, vmem, vmem, vmem, vmem],
        out_specs=vmem,
        scratch_shapes=[pltpu.VMEM((ROWS, D), F32)],
        compiler_params=PARAMS,
        cost_estimate=cost(30 * ROWS * D, 8 * ROWS * D),
    )(power, x_place, rows, cotangent, mod, back)

    levels = lax.all_to_all(plane, ("zh", "zl"), 0, 0, tiled=True)
    level = jnp.sum(levels.astype(F32), axis=0).astype(BF16)
    spread = lax.all_to_all(jnp.broadcast_to(level[None], (8, 3, D)), ("c", "x"), 0, 0, tiled=True)
    wanted = lax.dynamic_index_in_dim(spread.reshape(4, 2, 3, D), core, 1, keepdims=False)
    wanted = jnp.broadcast_to(wanted[:, None], (4, 4, 3, D)).reshape(16, 3, D)
    final = lax.all_to_all(wanted, ("zh", "zl"), 0, 0, tiled=True).reshape(48, D)[:36]
    return d_hidden[None, None], final.astype(F32) / 32.0


def solution(mesh):
    fine = Mesh(mesh.devices.reshape([size for _, size in FINE]), [name for name, _ in FINE])
    placed = (
        P(CLIP, SEQ, None, None),
        P(CLIP, SEQ),
        P(CLIP, None, None, None),
        P(CLIP, SEQ, None, None),
        P(CLIP, None),
        P(CLIP, None),
        P(),
    )
    return jax.shard_map(
        on_device,
        mesh=fine,
        in_specs=placed,
        out_specs=(P(CLIP, SEQ, None, None), P(SEQ, None)),
        check_vma=False,
    )
```

time: 325 us -> 255 us (0.78)
  the two profiles are of different devices: /device:TPU:24 before, /device:TPU:32 now
where the time goes in v2:
time: 255 us; the launch traced here: 254 us
  waiting for transfers between devices  90.4 us (35%)
  starting transfers between devices  78.1 us (31%)
  blocking collectives  37.8 us (15%)
  Pallas kernels  33 us (13%)
  local copies, waits for them, and re-layouts  10.8 us (4%)
    all_to_all x2, waiting for transfers between devices, from_frames(): own = lax.all_to_all(values, 'zh', 0, 0, tiled=True)  28 us
    all_to_all x1, waiting for transfers between devices, on_device(): back = lax.all_to_all(summed, 'zh', 0, 0, tiled=True).reshape(ROWS, D)  20.8 us
    all_to_all x1, blocking collectives, on_device(): block = lax.all_to_all(unit, 'zl', 0, 0, tiled=True).reshape(PART, 4 * PART)  19.1 us
    all_to_all x1, blocking collectives, on_device(): lax.all_to_all(part.reshape(8, 36, D), ('yh', 'x'), 0, 0, tiled=True)  18.7 us
    all_to_all x2, starting transfers between devices, from_frames(): own = lax.all_to_all(values, 'zh', 0, 0, tiled=True)  17.6 us
    all_to_all x1, waiting for transfers between devices, on_device(): lax.all_to_all(wanted, ('zh', 'zl'), 0, 0, tiled=True).reshape(48, D)[:36]  13.7 us
    all_to_all x1, starting transfers between devices, on_device(): levels = lax.all_to_all(plane, ('zh', 'zl'), 0, 0, tiled=True)  12.9 us
    ppermute x3, waiting for transfers between devices, on_device(): lax.ppermute(block, 'x', [(i, (i + 4 - step) % 4) for i in range(4)])  12.4 us
  transfers between devices with their start and end apart: 18, of which 8 were waited for; matrix products, arithmetic and copies ran while one was open for 3% of the time, Pallas kernels for 6%

profile of v2, /device:TPU:32, one launch (start us, length us, event | category | flops | bytes accessed | tf_op | source)
XLA Modules:
  0.0 253.9 jit_solution(10714089985108812236)
XLA Ops:
  3.2 2.6 %shard_map.86 = (bf16[4,32,1152]{2,1,0:T(8,128)(2,1)}, bf16[4,32,1152]{2,1,0:T(8,128)(2,1)}) custom-call(f32[2]{0:T(128)} %pad_maximum_fusion.4.power_ref, s32[1]{0:T(128)} %bitcast.2.x_ref, bf16[128,1152]{1,0:T(8,128)(2,1)} %bitcast.38, bf16[128,1152]{1,0:T(8,128)(2,1)} %bitcast.40, f32[3,1152]{1,0:T(4,128)} %bitcast.45), custom_call_target="tpu_custom_call" | custom-call | flops 2949120 | bytes 1179648 | tf_op jit(solution)/shard_map/pallas_call | solution.py:356
  5.8 14.2 %all-to-all-start.3 = ((bf16[4,32,1152]{2,1,0:T(8,128)(2,1)}), bf16[4,32,1152]{2,1,0:T(8,128)(2,1)}, u32[]{:S(2)}, u32[]{:S(2)}) async-start(bf16[4,32,1152]{2,1,0:T(8,128)(2,1)} %get-tuple-element.15), calls=%async_computation.3 | async-start | bytes 589824 | tf_op jit(solution)/shard_map/all_to_all | solution.py:373
  22.2 20.1 %all-to-all-done.3.refs_0_ = bf16[4,32,1152]{2,1,0:T(8,128)(2,1)} async-done(((bf16[4,32,1152]{2,1,0:T(8,128)(2,1)}), bf16[4,32,1152]{2,1,0:T(8,128)(2,1)}, u32[]{:S(2)}, u32[]{:S(2)}) %all-to-all-start.3) | async-done | bytes 294944 | tf_op jit(solution)/shard_map/all_to_all | solution.py:373
  42.2 19.1 %all_to_all.45 = bf16[4,72,1152]{2,1,0:T(8,128)(2,1)S(1)} all-to-all(bf16[4,72,1152]{2,1,0:T(8,128)(2,1)} %shard_map.87), channel_id=1, replica_groups=mesh['yh'=2,'yl'=2,'zh'=4,'c'=2,'zl'=4,'x'=4] {'zl'}, dimensions={0} | all-to-all | bytes 1327104 | tf_op jit(solution)/shard_map/all_to_all | solution.py:351
  61.3 3.5 %all-to-all-start = ((bf16[4,32,1152]{2,1,0:T(8,128)(2,1)}), bf16[4,32,1152]{2,1,0:T(8,128)(2,1)S(1)}, u32[]{:S(2)}, u32[]{:S(2)}) async-start(bf16[4,32,1152]{2,1,0:T(8,128)(2,1)} %get-tuple-element.14), calls=%async_computation | async-start | bytes 589824 | tf_op jit(solution)/shard_map/all_to_all | solution.py:373
  64.8 4.8 %collective-permute-start.3 = (bf16[288,1152]{1,0:T(8,128)(2,1)S(1)}, bf16[288,1152]{1,0:T(8,128)(2,1)S(1)}, u32[]{:S(2)}, u32[]{:S(2)}) collective-permute-start(bf16[288,1152]{1,0:T(8,128)(2,1)S(1)} %bitcast.30), channel_id=1, source_target_pairs={{0,3},{1,0},{2,1},{3,2},{4,7},{5,4},{6,5},{7,6},{8,11},{9,8},{10,9... | collective-permute-start | bytes 1990664 | tf_op jit(solution)/shard_map/ppermute | solution.py:353
  69.6 2.7 %collective-permute-start.4 = (bf16[288,1152]{1,0:T(8,128)(2,1)S(1)}, bf16[288,1152]{1,0:T(8,128)(2,1)S(1)}, u32[]{:S(2)}, u32[]{:S(2)}) collective-permute-start(bf16[288,1152]{1,0:T(8,128)(2,1)S(1)} %bitcast.31), channel_id=1, source_target_pairs={{0,2},{1,3},{2,0},{3,1},{4,6},{5,7},{6,4},{7,5},{8,10},{9,11},{10,... | collective-permute-start | bytes 1990664 | tf_op jit(solution)/shard_map/ppermute | solution.py:353
  72.3 2.8 %collective-permute-start.5 = (bf16[288,1152]{1,0:T(8,128)(2,1)S(1)}, bf16[288,1152]{1,0:T(8,128)(2,1)S(1)}, u32[]{:S(2)}, u32[]{:S(2)}) collective-permute-start(bf16[288,1152]{1,0:T(8,128)(2,1)S(1)} %bitcast.32), channel_id=1, source_target_pairs={{0,1},{1,2},{2,3},{3,0},{4,5},{5,6},{6,7},{7,4},{8,9},{9,10},{10,1... | collective-permute-start | bytes 1990664 | tf_op jit(solution)/shard_map/ppermute | solution.py:353
  75.1 3.5 %collective-permute-start.7 = (bf16[4,32,1152]{2,1,0:T(8,128)(2,1)}, bf16[4,32,1152]{2,1,0:T(8,128)(2,1)}, u32[]{:S(2)}, u32[]{:S(2)}) collective-permute-start(bf16[4,32,1152]{2,1,0:T(8,128)(2,1)} %all-to-all-done.3.refs_0_), channel_id=1, source_target_pairs={{0,128},{128,0},{1,129},{129,1},{2,130},{130,2},{3,131},{131,3},{4... | collective-permute-start | bytes 884744 | tf_op jit(solution)/shard_map/ppermute | solution.py:370
  78.6 8.0 %all-to-all-done.refs_0_ = bf16[4,32,1152]{2,1,0:T(8,128)(2,1)S(1)} async-done(((bf16[4,32,1152]{2,1,0:T(8,128)(2,1)}), bf16[4,32,1152]{2,1,0:T(8,128)(2,1)S(1)}, u32[]{:S(2)}, u32[]{:S(2)}) %all-to-all-start) | async-done | bytes 294944 | tf_op jit(solution)/shard_map/all_to_all | solution.py:373
  86.6 3.5 %collective-permute-start.1 = (bf16[4,32,1152]{2,1,0:T(8,128)(2,1)S(1)}, bf16[4,32,1152]{2,1,0:T(8,128)(2,1)S(1)}, u32[]{:S(2)}, u32[]{:S(2)}) collective-permute-start(bf16[4,32,1152]{2,1,0:T(8,128)(2,1)S(1)} %all-to-all-done.refs_0_), channel_id=1, source_target_pairs={{0,128},{128,0},{1,129},{129,1},{2,130},{130,2},{3,131},{131,3},{4... | collective-permute-start | bytes 884744 | tf_op jit(solution)/shard_map/ppermute | solution.py:370
  90.1 6.8 %collective-permute-done.3.refs_1_.refs_5_ = bf16[288,1152]{1,0:T(8,128)(2,1)S(1)} collective-permute-done((bf16[288,1152]{1,0:T(8,128)(2,1)S(1)}, bf16[288,1152]{1,0:T(8,128)(2,1)S(1)}, u32[]{:S(2)}, u32[]{:S(2)}) %collective-permute-start.3) | collective-permute-done | bytes 663584 | tf_op jit(solution)/shard_map/ppermute | solution.py:353
  96.9 5.6 %collective-permute-done.5.refs_3_.refs_7_ = bf16[288,1152]{1,0:T(8,128)(2,1)S(1)} collective-permute-done((bf16[288,1152]{1,0:T(8,128)(2,1)S(1)}, bf16[288,1152]{1,0:T(8,128)(2,1)S(1)}, u32[]{:S(2)}, u32[]{:S(2)}) %collective-permute-start.5) | collective-permute-done | bytes 663584 | tf_op jit(solution)/shard_map/ppermute | solution.py:353
  103.4 2.6 %shard_map.88 = bf16[4,288,288]{2,1,0:T(8,128)(2,1)} custom-call(s32[1]{0:T(128)} %bitcast.2.x_ref, bf16[288,1152]{1,0:T(8,128)(2,1)} %bitcast.33, bf16[288,1152]{1,0:T(8,128)(2,1)} %copy-done.2, bf16[288,1152]{1,0:T(8,128)(2,1)} %copy-done.3, bf16[288,1152]{1,0:T(8,128)(2,1)} %copy-done.4), custom_call_target="tpu_custom_call" | custom-call | flops 1000000 | bytes 2000000 | tf_op jit(solution)/shard_map/pallas_call | solution.py:379
  106.0 3.5 %all-to-all-start.2 = ((bf16[4,288,288]{2,1,0:T(8,128)(2,1)}), bf16[4,288,288]{2,1,0:T(8,128)(2,1)S(1)}, u32[]{:S(2)}, u32[]{:S(2)}) async-start(bf16[4,288,288]{2,1,0:T(8,128)(2,1)} %shard_map.88), calls=%async_computation.2 | async-start | bytes 1769472 | tf_op jit(solution)/shard_map/all_to_all | solution.py:388
  110.2 2.4 collective-permute-start.6
  114.5 2.4 collective-permute-start.8
  121.0 8.1 %shard_map.89 = (bf16[512,384]{1,0:T(8,128)(2,1)}, bf16[512,384]{1,0:T(8,128)(2,1)}, bf16[512,384]{1,0:T(8,128)(2,1)}, bf16[512,384]{1,0:T(8,128)(2,1)}, bf16[51...) custom-call(bf16[4,32,1152]{2,1,0:T(8,128)(2,1)} %all-to-all-done.3.refs_0_, ...), custom_call_target="tpu_custom_call" | custom-call | flops 1358954496 | bytes 12000000 | tf_op jit(solution)/shard_map/pallas_call | solution.py:393
  130.7 11.9 %shard_map.90 = (f32[2,4,32,1152]{3,2,1,0:T(8,128)}, bf16[2,4,32,1152]{3,2,1,0:T(8,128)(2,1)}) custom-call(bf16[4,32,1152]{2,1,0:T(8,128)(2,1)} %copy-done.6, bf16[4,32,1152]{2,1,0:T(8,128)(2,1)} %copy-done.8, bf16[4,32,1152]{2,1,0:T(8,128)(2,1)} %copy-done.7, bf16[4,32,1152]{2,1,0:T(8,128)(2,1)} %copy-done.9, bf16[288,1152]{1,0:T(8,128)(2,1)} %bitcast.35, ...), custom_call_target="tpu_custom_call" | custom-call | flops 1358954496 | bytes 14000000 | tf_op jit(solution)/shard_map/pallas_call | solution.py:415
  142.6 2.4 collective-permute-start.9
  145.0 2.9 %shard_map.92 = bf16[288,1152]{1,0:T(8,128)(2,1)} custom-call(bf16[4,32,1152]{2,1,0:T(8,128)(2,1)} %copy-done.6, bf16[4,32,1152]{2,1,0:T(8,128)(2,1)} %copy-done.8, bf16[4,32,1152]{2,1,0:T(8,128)(2,1)} %copy-done.7, bf16[4,32,1152]{2,1,0:T(8,128)(2,1)} %copy-done.9, bf16[512,384]{1,0:T(8,128)(2,1)} %get-tuple-element.25.refs_4_), custom_call_target="tpu_custom_call" | custom-call | flops 339738624 | bytes 2000000 | tf_op jit(solution)/shard_map/pallas_call | solution.py:402
  149.1 18.7 %all_to_all.46 = bf16[8,36,1152]{2,1,0:T(8,128)(2,1)S(1)} all-to-all(bf16[8,36,1152]{2,1,0:T(8,128)(2,1)S(1)} %reshape.618), channel_id=1, replica_groups=mesh['yh'=2,'yl'=2,'zh'=4,'c'=2,'zl'=4,'x'=4] {'yh','x'}, dimensions={0} | all-to-all | bytes 1327104 | tf_op jit(solution)/shard_map/all_to_all | solution.py:411
  168.7 12.9 %all-to-all-start.6 = ((bf16[16,3,1152]{2,1,0:T(4,128)(2,1)}), bf16[16,3,1152]{2,1,0:T(4,128)(2,1)S(1)}, u32[]{:S(2)}, u32[]{:S(2)}) async-start(bf16[16,3,1152]{2,1,0:T(4,128)(2,1)} %reshape.619), calls=%async_computation.6 | async-start | bytes 294912 | tf_op jit(solution)/shard_map/all_to_all | solution.py:447
  181.7 3.3 %collective-permute-start.10 = (bf16[4,32,1152]{2,1,0:T(8,128)(2,1)S(1)}, bf16[4,32,1152]{2,1,0:T(8,128)(2,1)S(1)}, u32[]{:S(2)}, u32[]{:S(2)}) collective-permute-start(bf16[4,32,1152]{2,1,0:T(8,128)(2,1)S(1)} %fusion.1), channel_id=1, source_target_pairs={{0,128},{128,0},{1,129},{129,1},{2,130},{130,2},{3,131},{131,3},{4... | collective-permute-start | bytes 884744 | tf_op jit(solution)/shard_map/ppermute | solution.py:370
  185.0 10.2 %all-to-all-done.6 = bf16[16,3,1152]{2,1,0:T(4,128)(2,1)S(1)} async-done(((bf16[16,3,1152]{2,1,0:T(4,128)(2,1)}), bf16[16,3,1152]{2,1,0:T(4,128)(2,1)S(1)}, u32[]{:S(2)}, u32[]{:S(2)}) %all-to-all-start.6) | async-done | bytes 110624 | tf_op jit(solution)/shard_map/all_to_all | solution.py:447
  196.0 3.4 %all-to-all-start.7 = ((bf16[8,3,1152]{2,1,0:T(4,128)(2,1)}), bf16[8,3,1152]{2,1,0:T(4,128)(2,1)S(1)}, u32[]{:S(2)}, u32[]{:S(2)}) async-start(bf16[8,3,1152]{2,1,0:T(4,128)(2,1)} %broadcast_in_dim.52), calls=%async_computation.7 | async-start | bytes 147456 | tf_op jit(solution)/shard_map/all_to_all | solution.py:449
  199.3 5.3 %all-to-all-done.7 = bf16[8,3,1152]{2,1,0:T(4,128)(2,1)S(1)} async-done(((bf16[8,3,1152]{2,1,0:T(4,128)(2,1)}), bf16[8,3,1152]{2,1,0:T(4,128)(2,1)S(1)}, u32[]{:S(2)}, u32[]{:S(2)}) %all-to-all-start.7) | async-done | bytes 55328 | tf_op jit(solution)/shard_map/all_to_all | solution.py:449
  205.3 4.7 %all-to-all-start.8 = ((bf16[16,3,1152]{2,1,0:T(4,128)(2,1)}), bf16[16,3,1152]{2,1,0:T(4,128)(2,1)S(1)}, u32[]{:S(2)}, u32[]{:S(2)}) async-start(bf16[16,3,1152]{2,1,0:T(4,128)(2,1)} %bitcast.17), calls=%async_computation.8 | async-start | bytes 294912 | tf_op jit(solution)/shard_map/all_to_all | solution.py:452
  210.9 13.7 %all-to-all-done.8 = bf16[16,3,1152]{2,1,0:T(4,128)(2,1)S(1)} async-done(((bf16[16,3,1152]{2,1,0:T(4,128)(2,1)}), bf16[16,3,1152]{2,1,0:T(4,128)(2,1)S(1)}, u32[]{:S(2)}, u32[]{:S(2)}) %all-to-all-start.8) | async-done | bytes 110624 | tf_op jit(solution)/shard_map/all_to_all | solution.py:452
  224.6 4.3 %all-to-all-start.4 = ((bf16[4,32,1152]{2,1,0:T(8,128)(2,1)}), bf16[4,32,1152]{2,1,0:T(8,128)(2,1)S(1)}, u32[]{:S(2)}, u32[]{:S(2)}) async-start(bf16[4,32,1152]{2,1,0:T(8,128)(2,1)} %fusion), calls=%async_computation.4 | async-start | bytes 589824 | tf_op jit(solution)/shard_map/all_to_all | solution.py:436
  229.6 20.8 %all-to-all-done.4 = bf16[4,32,1152]{2,1,0:T(8,128)(2,1)S(1)} async-done(((bf16[4,32,1152]{2,1,0:T(8,128)(2,1)}), bf16[4,32,1152]{2,1,0:T(8,128)(2,1)S(1)}, u32[]{:S(2)}, u32[]{:S(2)}) %all-to-all-start.4) | async-done | bytes 294944 | tf_op jit(solution)/shard_map/all_to_all | solution.py:436
  251.2 2.7 %shard_map.91 = bf16[128,1152]{1,0:T(8,128)(2,1)} custom-call(f32[2]{0:T(128)} %pad_maximum_fusion.4.power_ref, s32[1]{0:T(128)} %bitcast.2.x_ref, bf16[128,1152]{1,0:T(8,128)(2,1)} %bitcast.39, bf16[128,1152]{1,0:T(8,128)(2,1)} %bitcast.41, f32[3,1152]{1,0:T(4,128)} %bitcast.46, bf16[128,1152]{1,0:T(8,128)(2,1)} %bitcast.42), custom_call_target="tpu_custom_call" | custom-call | flops 4423680 | bytes 1179648 | tf_op jit(solution)/shard_map/pallas_call | solution.py:437
  (80 shorter events, 19.0 us)
Async XLA Ops:
  0.6 0.8 copy-start
  5.8 36.4 %all-to-all-start.3 = ((bf16[4,32,1152]{2,1,0:T(8,128)(2,1)}), bf16[4,32,1152]{2,1,0:T(8,128)(2,1)}, u32[]{:S(2)}, u32[]{:S(2)}) async-start(bf16[4,32,1152]{2,1,0:T(8,128)(2,1)} %get-tuple-element.15), calls=%async_computation.3 | async-start | bytes 589824 | tf_op jit(solution)/shard_map/all_to_all | solution.py:373
  22.2 67.9 %copy-start.14 = (f32[2,72]{1,0:T(2,128)S(1)}, f32[2,72]{1,0:T(2,128)}, u32[]{:S(2)}) copy-start(f32[2,72]{1,0:T(2,128)} %param.13) | copy-start | bytes 1732
  61.3 41.2 %copy-start.1 = (bf16[4,72,1152]{2,1,0:T(8,128)(2,1)}, bf16[4,72,1152]{2,1,0:T(8,128)(2,1)S(1)}, u32[]{:S(2)}) copy-start(bf16[4,72,1152]{2,1,0:T(8,128)(2,1)S(1)} %all_to_all.45) | copy-start | bytes 1990660
  61.3 25.3 %all-to-all-start = ((bf16[4,32,1152]{2,1,0:T(8,128)(2,1)}), bf16[4,32,1152]{2,1,0:T(8,128)(2,1)S(1)}, u32[]{:S(2)}, u32[]{:S(2)}) async-start(bf16[4,32,1152]{2,1,0:T(8,128)(2,1)} %get-tuple-element.14), calls=%async_computation | async-start | bytes 589824 | tf_op jit(solution)/shard_map/all_to_all | solution.py:373
  64.8 32.1 %collective-permute-start.3 = (bf16[288,1152]{1,0:T(8,128)(2,1)S(1)}, bf16[288,1152]{1,0:T(8,128)(2,1)S(1)}, u32[]{:S(2)}, u32[]{:S(2)}) collective-permute-start(bf16[288,1152]{1,0:T(8,128)(2,1)S(1)} %bitcast.30), channel_id=1, source_target_pairs={{0,3},{1,0},{2,1},{3,2},{4,7},{5,4},{6,5},{7,6},{8,11},{9,8},{10,9... | collective-permute-start | bytes 1990664 | tf_op jit(solution)/shard_map/ppermute | solution.py:353
  69.6 27.3 %collective-permute-start.4 = (bf16[288,1152]{1,0:T(8,128)(2,1)S(1)}, bf16[288,1152]{1,0:T(8,128)(2,1)S(1)}, u32[]{:S(2)}, u32[]{:S(2)}) collective-permute-start(bf16[288,1152]{1,0:T(8,128)(2,1)S(1)} %bitcast.31), channel_id=1, source_target_pairs={{0,2},{1,3},{2,0},{3,1},{4,6},{5,7},{6,4},{7,5},{8,10},{9,11},{10,... | collective-permute-start | bytes 1990664 | tf_op jit(solution)/shard_map/ppermute | solution.py:353
  72.3 30.2 %collective-permute-start.5 = (bf16[288,1152]{1,0:T(8,128)(2,1)S(1)}, bf16[288,1152]{1,0:T(8,128)(2,1)S(1)}, u32[]{:S(2)}, u32[]{:S(2)}) collective-permute-start(bf16[288,1152]{1,0:T(8,128)(2,1)S(1)} %bitcast.32), channel_id=1, source_target_pairs={{0,1},{1,2},{2,3},{3,0},{4,5},{5,6},{6,7},{7,4},{8,9},{9,10},{10,1... | collective-permute-start | bytes 1990664 | tf_op jit(solution)/shard_map/ppermute | solution.py:353
  75.1 39.4 %collective-permute-start.7 = (bf16[4,32,1152]{2,1,0:T(8,128)(2,1)}, bf16[4,32,1152]{2,1,0:T(8,128)(2,1)}, u32[]{:S(2)}, u32[]{:S(2)}) collective-permute-start(bf16[4,32,1152]{2,1,0:T(8,128)(2,1)} %all-to-all-done.3.refs_0_), channel_id=1, source_target_pairs={{0,128},{128,0},{1,129},{129,1},{2,130},{130,2},{3,131},{131,3},{4... | collective-permute-start | bytes 884744 | tf_op jit(solution)/shard_map/ppermute | solution.py:370
  86.6 34.4 %copy-start.6 = (bf16[4,32,1152]{2,1,0:T(8,128)(2,1)}, bf16[4,32,1152]{2,1,0:T(8,128)(2,1)S(1)}, u32[]{:S(2)}) copy-start(bf16[4,32,1152]{2,1,0:T(8,128)(2,1)S(1)} %all-to-all-done.refs_0_) | copy-start | bytes 884740
  86.6 30.3 %collective-permute-start.1 = (bf16[4,32,1152]{2,1,0:T(8,128)(2,1)S(1)}, bf16[4,32,1152]{2,1,0:T(8,128)(2,1)S(1)}, u32[]{:S(2)}, u32[]{:S(2)}) collective-permute-start(bf16[4,32,1152]{2,1,0:T(8,128)(2,1)S(1)} %all-to-all-done.refs_0_), channel_id=1, source_target_pairs={{0,128},{128,0},{1,129},{129,1},{2,130},{130,2},{3,131},{131,3},{4... | collective-permute-start | bytes 884744 | tf_op jit(solution)/shard_map/ppermute | solution.py:370
  96.9 5.6 %copy-start.2 = (bf16[288,1152]{1,0:T(8,128)(2,1)}, bf16[288,1152]{1,0:T(8,128)(2,1)S(1)}, u32[]{:S(2)}) copy-start(bf16[288,1152]{1,0:T(8,128)(2,1)S(1)} %collective-permute-done.3.refs_1_.refs_5_) | copy-start | bytes 1990660
  96.9 5.6 %copy-start.3 = (bf16[288,1152]{1,0:T(8,128)(2,1)}, bf16[288,1152]{1,0:T(8,128)(2,1)S(1)}, u32[]{:S(2)}) copy-start(bf16[288,1152]{1,0:T(8,128)(2,1)S(1)} %collective-permute-done.4.refs_2_.refs_6_) | copy-start | bytes 1990660
  102.5 0.9 copy-start.4
  106.0 23.1 %all-to-all-start.2 = ((bf16[4,288,288]{2,1,0:T(8,128)(2,1)}), bf16[4,288,288]{2,1,0:T(8,128)(2,1)S(1)}, u32[]{:S(2)}, u32[]{:S(2)}) async-start(bf16[4,288,288]{2,1,0:T(8,128)(2,1)} %shard_map.88), calls=%async_computation.2 | async-start | bytes 1769472 | tf_op jit(solution)/shard_map/all_to_all | solution.py:388
  110.2 9.4 %collective-permute-start.6 = (bf16[4,32,1152]{2,1,0:T(8,128)(2,1)}, bf16[4,32,1152]{2,1,0:T(8,128)(2,1)S(1)}, u32[]{:S(2)}, u32[]{:S(2)}) collective-permute-start(bf16[4,32,1152]{2,1,0:T(8,128)(2,1)} %all-to-all-done.3.refs_0_), channel_id=1, source_target_pairs={{0,16},{16,0},{1,17},{17,1},{2,18},{18,2},{3,19},{19,3},{4,20},{20... | collective-permute-start | bytes 884744 | tf_op jit(solution)/shard_map/ppermute | solution.py:367
  112.6 16.5 %collective-permute-start = (bf16[4,32,1152]{2,1,0:T(8,128)(2,1)S(1)}, bf16[4,32,1152]{2,1,0:T(8,128)(2,1)S(1)}, u32[]{:S(2)}, u32[]{:S(2)}) collective-permute-start(bf16[4,32,1152]{2,1,0:T(8,128)(2,1)S(1)} %all-to-all-done.refs_0_), channel_id=1, source_target_pairs={{0,16},{16,0},{1,17},{17,1},{2,18},{18,2},{3,19},{19,3},{4,20},{20... | collective-permute-start | bytes 884744 | tf_op jit(solution)/shard_map/ppermute | solution.py:367
  114.5 5.1 %collective-permute-start.8 = (bf16[4,32,1152]{2,1,0:T(8,128)(2,1)}, bf16[4,32,1152]{2,1,0:T(8,128)(2,1)S(1)}, u32[]{:S(2)}, u32[]{:S(2)}) collective-permute-start(bf16[4,32,1152]{2,1,0:T(8,128)(2,1)} %collective-permute-done.7.refs_2_), channel_id=1, source_target_pairs={{0,16},{16,0},{1,17},{17,1},{2,18},{18,2},{3,19},{19,3},{4,20},{20... | collective-permute-start | bytes 884744 | tf_op jit(solution)/shard_map/ppermute | solution.py:367
  116.9 4.0 %copy-start.7 = (bf16[4,32,1152]{2,1,0:T(8,128)(2,1)}, bf16[4,32,1152]{2,1,0:T(8,128)(2,1)S(1)}, u32[]{:S(2)}) copy-start(bf16[4,32,1152]{2,1,0:T(8,128)(2,1)S(1)} %collective-permute-done.1.refs_2_) | copy-start | bytes 884740
  116.9 12.1 %collective-permute-start.2 = (bf16[4,32,1152]{2,1,0:T(8,128)(2,1)S(1)}, bf16[4,32,1152]{2,1,0:T(8,128)(2,1)S(1)}, u32[]{:S(2)}, u32[]{:S(2)}) collective-permute-start(bf16[4,32,1152]{2,1,0:T(8,128)(2,1)S(1)} %collective-permute-done.1.refs_2_), channel_id=1, source_target_pairs={{0,16},{16,0},{1,17},{17,1},{2,18},{18,2},{3,19},{19,3},{4,20},{20... | collective-permute-start | bytes 884744 | tf_op jit(solution)/shard_map/ppermute | solution.py:367
  119.6 1.4 copy-start.12
  119.6 1.3 copy-start.13
  129.1 1.4 copy-start.8
  129.1 1.4 copy-start.9
  129.1 1.6 copy-start.5
  142.6 39.0 %collective-permute-start.9 = (bf16[2,4,32,1152]{3,2,1,0:T(8,128)(2,1)}, bf16[2,4,32,1152]{3,2,1,0:T(8,128)(2,1)S(1)}, u32[]{:S(2)}, u32[]{:S(2)}) collective-permute-start(bf16[2,4,32,1152]{3,2,1,0:T(8,128)(2,1)} %get-tuple-element.24), channel_id=1, source_target_pairs={{0,16},{16,0},{1,17},{17,1},{2,18},{18,2},{3,19},{19,3},{4,20},{20... | collective-permute-start | bytes 1769480 | tf_op jit(solution)/shard_map/ppermute | solution.py:367
  149.1 32.5 %copy-start.10 = (f32[2,4,32,1152]{3,2,1,0:T(8,128)S(1)}, f32[2,4,32,1152]{3,2,1,0:T(8,128)}, u32[]{:S(2)}) copy-start(f32[2,4,32,1152]{3,2,1,0:T(8,128)} %get-tuple-element.23) | copy-start | bytes 3538948
  168.7 26.5 %all-to-all-start.6 = ((bf16[16,3,1152]{2,1,0:T(4,128)(2,1)}), bf16[16,3,1152]{2,1,0:T(4,128)(2,1)S(1)}, u32[]{:S(2)}, u32[]{:S(2)}) async-start(bf16[16,3,1152]{2,1,0:T(4,128)(2,1)} %reshape.619), calls=%async_computation.6 | async-start | bytes 294912 | tf_op jit(solution)/shard_map/all_to_all | solution.py:447
  181.7 28.4 %collective-permute-start.10 = (bf16[4,32,1152]{2,1,0:T(8,128)(2,1)S(1)}, bf16[4,32,1152]{2,1,0:T(8,128)(2,1)S(1)}, u32[]{:S(2)}, u32[]{:S(2)}) collective-permute-start(bf16[4,32,1152]{2,1,0:T(8,128)(2,1)S(1)} %fusion.1), channel_id=1, source_target_pairs={{0,128},{128,0},{1,129},{129,1},{2,130},{130,2},{3,131},{131,3},{4... | collective-permute-start | bytes 884744 | tf_op jit(solution)/shard_map/ppermute | solution.py:370
  196.0 8.6 %all-to-all-start.7 = ((bf16[8,3,1152]{2,1,0:T(4,128)(2,1)}), bf16[8,3,1152]{2,1,0:T(4,128)(2,1)S(1)}, u32[]{:S(2)}, u32[]{:S(2)}) async-start(bf16[8,3,1152]{2,1,0:T(4,128)(2,1)} %broadcast_in_dim.52), calls=%async_computation.7 | async-start | bytes 147456 | tf_op jit(solution)/shard_map/all_to_all | solution.py:449
  205.3 19.2 %all-to-all-start.8 = ((bf16[16,3,1152]{2,1,0:T(4,128)(2,1)}), bf16[16,3,1152]{2,1,0:T(4,128)(2,1)S(1)}, u32[]{:S(2)}, u32[]{:S(2)}) async-start(bf16[16,3,1152]{2,1,0:T(4,128)(2,1)} %bitcast.17), calls=%async_computation.8 | async-start | bytes 294912 | tf_op jit(solution)/shard_map/all_to_all | solution.py:452
  224.6 25.9 %all-to-all-start.4 = ((bf16[4,32,1152]{2,1,0:T(8,128)(2,1)}), bf16[4,32,1152]{2,1,0:T(8,128)(2,1)S(1)}, u32[]{:S(2)}, u32[]{:S(2)}) async-start(bf16[4,32,1152]{2,1,0:T(8,128)(2,1)} %fusion), calls=%async_computation.4 | async-start | bytes 589824 | tf_op jit(solution)/shard_map/all_to_all | solution.py:436
  (1 other events, 0.7 us)

commit v3 on v2

--- a/solution.py
+++ b/solution.py
@@ -52,9 +52,12 @@
     branch_ref[...] = (mod_ref[2:3, :] * grad_ref[...].astype(F32)).astype(BF16).reshape(ZS, TOK, D)
 
 
-def home_backward(power_ref, x_ref, hidden_ref, grad_ref, mod_ref, back_ref, out_ref, turned_ref):
+def home_backward(power_ref, x_ref, level_ref, hidden_ref, grad_ref, mod_ref, *refs):
+    *back_refs, out_ref, turned_ref, back_ref = refs
+    for step, piece_ref in enumerate(back_refs):
+        back_ref[lax.rem(level_ref[0] + ZS - step, ZS)] = piece_ref[...].astype(F32)
     normed, factor = normalise(hidden_ref[...], power_ref[0], power_ref[1])
-    back = back_ref[...].astype(F32)
+    back = back_ref[...].reshape(ROWS, D)
     for x in range(4):
 
         @pl.when(x_ref[0] == x)
@@ -190,6 +193,10 @@
     for copy in copies:
         copy.start()
     return copies
+
+
+def by_token(table):
+    return jnp.broadcast_to(table[:, None, :], (16, 16, WIDE)).reshape(BLOCK, WIDE)
 
 
 def widen(values):
@@ -214,9 +221,10 @@
         factor_ref[...] = factor
         wide = split_dot(nt, factor, members)
         swapped = swap_pairs(raw)
+        straight, ahead = by_token(tab_ref[2 * place]), by_token(tab_ref[2 * place + 1])
         for half in range(2):
             rows = slice(half * BLOCK, (half + 1) * BLOCK)
-            turned = raw[rows] * tab_ref[2 * place] + swapped[rows] * tab_ref[2 * place + 1]
+            turned = raw[rows] * straight + swapped[rows] * ahead
             hat_ref[rows, :] = (wide[rows] * turned).astype(BF16)
     v_ref[...] = widen(packed[:, 2 * PART : 3 * PART]).astype(BF16)
     same = same_token()
@@ -232,7 +240,9 @@
 
 def chip_term(*refs):
     row_refs, (att_ref, part_ref) = refs[:4], refs[4:]
-    part_ref[...] = tn(att_ref[...], gather_rows(row_refs))[:PART].astype(BF16)
+    total = tn(att_ref[...], gather_rows(row_refs))
+    for piece in range(8):
+        part_ref[piece] = total[36 * piece : 36 * (piece + 1)].astype(BF16)
 
 
 def chip_backward(*refs):
@@ -274,10 +284,10 @@
         factor = factor_ref[...]
         turned = turned_ref[...]
         swapped = swap_pairs(turned)
+        straight, back = by_token(tab_ref[2 * place]), by_token(tab_ref[2 * place + 1])
         scaled = jnp.concatenate(
             [
-                turned[first : first + BLOCK] * tab_ref[2 * place]
-                + swapped[first : first + BLOCK] * tab_ref[2 * place + 1]
+                turned[first : first + BLOCK] * straight + swapped[first : first + BLOCK] * back
                 for first in (0, BLOCK)
             ],
             axis=0,
@@ -310,8 +320,7 @@
     swapped = qk_gain.reshape(2, HD // 2, 2)[:, :, ::-1].reshape(2, HD)
 
     def spread(table):
-        table = jnp.pad(jnp.tile(table, (1, 1, HEADS)), ((0, 0), (0, 0), (0, WIDE - PART)))
-        return jnp.broadcast_to(table[:, :, None, :], (4, 16, 16, WIDE)).reshape(4, BLOCK, WIDE)
+        return jnp.pad(jnp.tile(table, (1, 1, HEADS)), ((0, 0), (0, 0), (0, WIDE - PART)))
 
     straight = [qk_gain[i] * cosine for i in range(2)]
     ahead = [jnp.where(even, -sine, sine) * swapped[i] for i in range(2)]
@@ -369,13 +378,17 @@
     def other_y(values):
         return lax.ppermute(values, "yl", [(0, 1), (1, 0)])
 
-    def from_frames(values):
-        own = lax.all_to_all(values, "zh", 0, 0, tiled=True)
+    def exchange(values):
+        return lax.all_to_all(values, "zh", 0, 0, tiled=True)
+
+    def from_frames(own):
         across = other_y(own)
         return [own, other_core(own), across, other_core(across)]
 
-    modded = from_frames(sent)
-    branch = from_frames(sent_branch)
+    sent, _ = lax.optimization_barrier((sent, block))
+    both = exchange(jnp.concatenate([sent, sent_branch], axis=1))
+    modded = from_frames(both[:, :TOK])
+    branch = from_frames(both[:, TOK:])
     w_back = pl.pallas_call(
         out_rows,
         out_shape=jax.ShapeDtypeStruct((4, PART, PART), BF16),
@@ -401,14 +414,16 @@
     )(*modded, *blocks, tables)
     part = pl.pallas_call(
         chip_term,
-        out_shape=jax.ShapeDtypeStruct((PART, D), BF16),
+        out_shape=jax.ShapeDtypeStruct((8, 36, D), BF16),
         in_specs=[vmem] * 5,
         out_specs=vmem,
         compiler_params=PARAMS,
         cost_estimate=cost(2 * ALL * D * PART, 2 * 10**6),
     )(*branch, attended)
 
-    plane = lax.all_to_all(part.reshape(8, 36, D), ("yh", "x"), 0, 0, tiled=True)
+    w_back, part = lax.optimization_barrier((w_back, part))
+
+    plane = lax.all_to_all(part, ("yh", "x"), 0, 0, tiled=True)
     plane = jnp.sum(plane.astype(F32), axis=0).astype(BF16)
     plane = jnp.pad(plane, ((0, 12), (0, 0))).reshape(16, 3, D)
 
@@ -430,19 +445,25 @@
         compiler_params=PARAMS,
         cost_estimate=cost(2 * ALL * D * 4 * PART, 14 * 10**6),
     )(*branch, *blocks, w_back, tables_back, *kept)
+    theirs, _ = lax.optimization_barrier((theirs, plane))
     arrived = other_core(theirs)
     across = (mine[1] + arrived[1].astype(F32)).astype(BF16)
     summed = (mine[0] + arrived[0].astype(F32) + other_y(across).astype(F32)).astype(BF16)
-    back = lax.all_to_all(summed, "zh", 0, 0, tiled=True).reshape(ROWS, D)
+    level = lax.axis_index("zh")
+    pieces = [lax.dynamic_index_in_dim(summed, level, 0, keepdims=False)]
+    for step in range(1, ZS):
+        piece = lax.dynamic_index_in_dim(summed, lax.rem(level + step, ZS), 0, keepdims=False)
+        pieces.append(lax.ppermute(piece, "zh", [(i, (i + step) % ZS) for i in range(ZS)]))
+    level = level[None]
     d_hidden = pl.pallas_call(
         home_backward,
         out_shape=jax.ShapeDtypeStruct((ROWS, D), BF16),
-        in_specs=[smem, smem, vmem, vmem, vmem, vmem],
+        in_specs=[smem, smem, smem] + [vmem] * 7,
         out_specs=vmem,
-        scratch_shapes=[pltpu.VMEM((ROWS, D), F32)],
+        scratch_shapes=[pltpu.VMEM((ROWS, D), F32), pltpu.VMEM((ZS, TOK, D), F32)],
         compiler_params=PARAMS,
         cost_estimate=cost(30 * ROWS * D, 8 * ROWS * D),
-    )(power, x_place, rows, cotangent, mod, back)
+    )(power, x_place, level, rows, cotangent, mod, *pieces)
 
     levels = lax.all_to_all(plane, ("zh", "zl"), 0, 0, tiled=True)
     level = jnp.sum(levels.astype(F32), axis=0).astype(BF16)

time: 255 us -> 209 us (0.82)
  the two profiles are of different devices: /device:TPU:32 before, /device:TPU:24 now
where the time goes in v3:
time: 209 us; the launch traced here: 207 us
  starting transfers between devices  99.4 us (48%)
  waiting for transfers between devices  58.4 us (28%)
  Pallas kernels  32.3 us (15%)
  local copies, waits for them, and re-layouts  12.1 us (6%)
  other arithmetic  3.47 us (2%)
    ppermute x3, starting transfers between devices, on_device(): lax.ppermute(piece, 'zh', [(i, (i + step) % ZS) for i in range(ZS)])  22.3 us
    all_to_all x1, waiting for transfers between devices, exchange(): return lax.all_to_all(values, 'zh', 0, 0, tiled=True)  19.9 us
    all_to_all x1, waiting for transfers between devices, on_device(): block = lax.all_to_all(unit, 'zl', 0, 0, tiled=True).reshape(PART, 4 * PART)  12.9 us
    all_to_all x1, starting transfers between devices, exchange(): return lax.all_to_all(values, 'zh', 0, 0, tiled=True)  12.9 us
    all_to_all x1, waiting for transfers between devices, on_device(): levels = lax.all_to_all(plane, ('zh', 'zl'), 0, 0, tiled=True)  12.3 us
    pallas_call x1, Pallas kernels, on_device(): pl.pallas_call(chip_backward, out_shape=[jax.ShapeDtypeStruct((2, ZS, TOK...  11.6 us
    ppermute x5, starting transfers between devices, other_core(): return lax.ppermute(values, 'c', [(0, 1), (1, 0)])  10.5 us
    ppermute x3, starting transfers between devices, on_device(): lax.ppermute(block, 'x', [(i, (i + 4 - step) % 4) for i in range(4)])  10.2 us
  transfers between devices with their start and end apart: 21, of which 6 were waited for; matrix products, arithmetic and copies ran while one was open for 4% of the time, Pallas kernels for 13%

profile of v3, /device:TPU:24, one launch (start us, length us, event | category | flops | bytes accessed | tf_op | source)
XLA Modules:
  0.0 207.5 jit_solution(8536631700167322402)
XLA Ops:
  0.7 2.1 %shard_map.87 = bf16[4,72,1152]{2,1,0:T(8,128)(2,1)} custom-call(s32[1]{0:T(128)} %bitcast.6.place_ref, bf16[72,3456]{1,0:T(8,128)(2,1)} %w_qkv_ref.1, bf16[72,1152]{1,0:T(8,128)(2,1)} %w_out_ref.1), custom_call_target="tpu_custom_call" | custom-call | flops 1000000 | bytes 2000000 | tf_op jit(solution)/shard_map/pallas_call | solution.py:351
  2.8 5.9 %all-to-all-start = ((bf16[4,72,1152]{2,1,0:T(8,128)(2,1)}), bf16[4,72,1152]{2,1,0:T(8,128)(2,1)S(1)}, u32[]{:S(2)}, u32[]{:S(2)}) async-start(bf16[4,72,1152]{2,1,0:T(8,128)(2,1)} %shard_map.87), calls=%async_computation | async-start | bytes 1327104 | tf_op jit(solution)/shard_map/all_to_all | solution.py:360
  10.6 2.6 %shard_map.86 = (bf16[4,32,1152]{2,1,0:T(8,128)(2,1)}, bf16[4,32,1152]{2,1,0:T(8,128)(2,1)}) custom-call(f32[2]{0:T(128)} %pad_maximum_fusion.5.power_ref, s32[1]{0:T(128)} %bitcast.2.x_ref, bf16[128,1152]{1,0:T(8,128)(2,1)} %bitcast.42, bf16[128,1152]{1,0:T(8,128)(2,1)} %bitcast.44, f32[3,1152]{1,0:T(4,128)} %bitcast.48), custom_call_target="tpu_custom_call" | custom-call | flops 2949120 | bytes 1179648 | tf_op jit(solution)/shard_map/pallas_call | solution.py:365
  13.2 12.9 %all-to-all-done = bf16[4,72,1152]{2,1,0:T(8,128)(2,1)S(1)} async-done(((bf16[4,72,1152]{2,1,0:T(8,128)(2,1)}), bf16[4,72,1152]{2,1,0:T(8,128)(2,1)S(1)}, u32[]{:S(2)}, u32[]{:S(2)}) %all-to-all-start) | async-done | bytes 663584 | tf_op jit(solution)/shard_map/all_to_all | solution.py:360
  26.2 2.2 %pad_maximum_fusion = bf16[4,64,1152]{2,1,0:T(8,128)(2,1)} fusion(bf16[4,32,1152]{2,1,0:T(8,128)(2,1)} %get-tuple-element.20, bf16[4,32,1152]{2,1,0:T(8,128)(2,1)} %get-tuple-element.19), kind=kLoop, calls=%fused_computation | loop fusion | flops 1179648 | bytes 1179648 | tf_op jit(solution)/shard_map/concatenate | solution.py:389
  28.3 12.9 %all-to-all-start.1 = ((bf16[4,64,1152]{2,1,0:T(8,128)(2,1)}), bf16[4,64,1152]{2,1,0:T(8,128)(2,1)}, u32[]{:S(2)}, u32[]{:S(2)}) async-start(bf16[4,64,1152]{2,1,0:T(8,128)(2,1)} %pad_maximum_fusion), calls=%async_computation.1 | async-start | bytes 1179648 | tf_op jit(solution)/shard_map/all_to_all | solution.py:382
  41.9 4.7 %collective-permute-start.3 = (bf16[288,1152]{1,0:T(8,128)(2,1)S(1)}, bf16[288,1152]{1,0:T(8,128)(2,1)S(1)}, u32[]{:S(2)}, u32[]{:S(2)}) collective-permute-start(bf16[288,1152]{1,0:T(8,128)(2,1)S(1)} %bitcast.36), channel_id=1, source_target_pairs={{0,3},{1,0},{2,1},{3,2},{4,7},{5,4},{6,5},{7,6},{8,11},{9,8},{10,9... | collective-permute-start | bytes 1990664 | tf_op jit(solution)/shard_map/ppermute | solution.py:362
  46.6 2.7 %collective-permute-start.4 = (bf16[288,1152]{1,0:T(8,128)(2,1)S(1)}, bf16[288,1152]{1,0:T(8,128)(2,1)S(1)}, u32[]{:S(2)}, u32[]{:S(2)}) collective-permute-start(bf16[288,1152]{1,0:T(8,128)(2,1)S(1)} %bitcast.37), channel_id=1, source_target_pairs={{0,2},{1,3},{2,0},{3,1},{4,6},{5,7},{6,4},{7,5},{8,10},{9,11},{10,... | collective-permute-start | bytes 1990664 | tf_op jit(solution)/shard_map/ppermute | solution.py:362
  49.3 2.8 %collective-permute-start.5 = (bf16[288,1152]{1,0:T(8,128)(2,1)S(1)}, bf16[288,1152]{1,0:T(8,128)(2,1)}, u32[]{:S(2)}, u32[]{:S(2)}) collective-permute-start(bf16[288,1152]{1,0:T(8,128)(2,1)S(1)} %bitcast.38), channel_id=1, source_target_pairs={{0,1},{1,2},{2,3},{3,0},{4,5},{5,6},{6,7},{7,4},{8,9},{9,10},{10,1... | collective-permute-start | bytes 1990664 | tf_op jit(solution)/shard_map/ppermute | solution.py:362
  52.1 19.9 %all-to-all-done.1 = bf16[4,64,1152]{2,1,0:T(8,128)(2,1)} async-done(((bf16[4,64,1152]{2,1,0:T(8,128)(2,1)}), bf16[4,64,1152]{2,1,0:T(8,128)(2,1)}, u32[]{:S(2)}, u32[]{:S(2)}) %all-to-all-start.1) | async-done | bytes 589856 | tf_op jit(solution)/shard_map/all_to_all | solution.py:382
  73.8 2.6 %collective-permute-start.7 = (bf16[4,32,1152]{2,1,0:T(8,128)(2,1)}, bf16[4,32,1152]{2,1,0:T(8,128)(2,1)S(1)}, u32[]{:S(2)}, u32[]{:S(2)}) collective-permute-start(bf16[4,32,1152]{2,1,0:T(8,128)(2,1)} %get-tuple-element.36.refs_0_), channel_id=1, source_target_pairs={{0,128},{128,0},{1,129},{129,1},{2,130},{130,2},{3,131},{131,3},{4... | collective-permute-start | bytes 884744 | tf_op jit(solution)/shard_map/ppermute | solution.py:379
  76.5 3.2 %collective-permute-start.1 = (bf16[4,32,1152]{2,1,0:T(8,128)(2,1)S(1)}, bf16[4,32,1152]{2,1,0:T(8,128)(2,1)S(1)}, u32[]{:S(2)}, u32[]{:S(2)}) collective-permute-start(bf16[4,32,1152]{2,1,0:T(8,128)(2,1)S(1)} %get-tuple-element.37.refs_0_), channel_id=1, source_target_pairs={{0,128},{128,0},{1,129},{129,1},{2,130},{130,2},{3,131},{131,3},{4... | collective-permute-start | bytes 884744 | tf_op jit(solution)/shard_map/ppermute | solution.py:379
  80.9 2.6 %shard_map.88 = bf16[4,288,288]{2,1,0:T(8,128)(2,1)} custom-call(s32[1]{0:T(128)} %bitcast.2.x_ref, bf16[288,1152]{1,0:T(8,128)(2,1)} %bitcast.39, bf16[288,1152]{1,0:T(8,128)(2,1)} %copy-done.4, bf16[288,1152]{1,0:T(8,128)(2,1)} %copy-done.5, bf16[288,1152]{1,0:T(8,128)(2,1)} %collective-permute-done.5.refs_3_.refs_7_), custom_call_target="tpu_custom_call" | custom-call | flops 1000000 | bytes 2000000 | tf_op jit(solution)/shard_map/pallas_call | solution.py:392
  83.5 4.2 %all-to-all-start.2 = ((bf16[4,288,288]{2,1,0:T(8,128)(2,1)}), bf16[4,288,288]{2,1,0:T(8,128)(2,1)S(1)}, u32[]{:S(2)}, u32[]{:S(2)}) async-start(bf16[4,288,288]{2,1,0:T(8,128)(2,1)} %shard_map.88), calls=%async_computation.2 | async-start | bytes 1769472 | tf_op jit(solution)/shard_map/all_to_all | solution.py:401
  87.8 2.0 collective-permute-start.6
  89.8 2.3 %collective-permute-start = (bf16[4,32,1152]{2,1,0:T(8,128)(2,1)S(1)}, bf16[4,32,1152]{2,1,0:T(8,128)(2,1)S(1)}, u32[]{:S(2)}, u32[]{:S(2)}) collective-permute-start(bf16[4,32,1152]{2,1,0:T(8,128)(2,1)S(1)} %get-tuple-element.37.refs_0_), channel_id=1, source_target_pairs={{0,16},{16,0},{1,17},{17,1},{2,18},{18,2},{3,19},{19,3},{4,20},{20... | collective-permute-start | bytes 884744 | tf_op jit(solution)/shard_map/ppermute | solution.py:376
  92.1 2.1 collective-permute-start.8
  94.2 2.3 %collective-permute-start.2 = (bf16[4,32,1152]{2,1,0:T(8,128)(2,1)S(1)}, bf16[4,32,1152]{2,1,0:T(8,128)(2,1)S(1)}, u32[]{:S(2)}, u32[]{:S(2)}) collective-permute-start(bf16[4,32,1152]{2,1,0:T(8,128)(2,1)S(1)} %collective-permute-done.1.refs_2_), channel_id=1, source_target_pairs={{0,16},{16,0},{1,17},{17,1},{2,18},{18,2},{3,19},{19,3},{4,20},{20... | collective-permute-start | bytes 884744 | tf_op jit(solution)/shard_map/ppermute | solution.py:376
  98.8 7.6 %shard_map.89 = (bf16[512,384]{1,0:T(8,128)(2,1)}, bf16[512,384]{1,0:T(8,128)(2,1)}, bf16[512,384]{1,0:T(8,128)(2,1)}, bf16[512,384]{1,0:T(8,128)(2,1)}, bf16[51...) custom-call(bf16[4,32,1152]{2,1,0:T(8,128)(2,1)} %get-tuple-element.36.refs_0_, ...), custom_call_target="tpu_custom_call" | custom-call | flops 1358954496 | bytes 12000000 | tf_op jit(solution)/shard_map/pallas_call | solution.py:406
  107.3 2.9 %shard_map.90 = bf16[8,36,1152]{2,1,0:T(8,128)(2,1)} custom-call(bf16[4,32,1152]{2,1,0:T(8,128)(2,1)} %copy-done.3, bf16[4,32,1152]{2,1,0:T(8,128)(2,1)} %copy-done.7, bf16[4,32,1152]{2,1,0:T(8,128)(2,1)} %copy-done.6, bf16[4,32,1152]{2,1,0:T(8,128)(2,1)} %copy-done.8, bf16[512,384]{1,0:T(8,128)(2,1)} %get-tuple-element.21.refs_4_), custom_call_target="tpu_custom_call" | custom-call | flops 339738624 | bytes 2000000 | tf_op jit(solution)/shard_map/pallas_call | solution.py:415
  110.3 7.3 %all-to-all-start.3 = ((bf16[8,36,1152]{2,1,0:T(8,128)(2,1)}), bf16[8,36,1152]{2,1,0:T(8,128)(2,1)S(1)}, u32[]{:S(2)}, u32[]{:S(2)}) async-start(bf16[8,36,1152]{2,1,0:T(8,128)(2,1)} %shard_map.90), calls=%async_computation.3 | async-start | bytes 1474560 | tf_op jit(solution)/shard_map/all_to_all | solution.py:426
  118.3 11.6 %shard_map.91 = (f32[2,4,32,1152]{3,2,1,0:T(8,128)}, bf16[2,4,32,1152]{3,2,1,0:T(8,128)(2,1)}) custom-call(bf16[4,32,1152]{2,1,0:T(8,128)(2,1)} %copy-done.3, bf16[4,32,1152]{2,1,0:T(8,128)(2,1)} %copy-done.7, bf16[4,32,1152]{2,1,0:T(8,128)(2,1)} %copy-done.6, bf16[4,32,1152]{2,1,0:T(8,128)(2,1)} %copy-done.8, bf16[288,1152]{1,0:T(8,128)(2,1)} %bitcast.41, ...), custom_call_target="tpu_custom_call" | custom-call | flops 1358954496 | bytes 14000000 | tf_op jit(solution)/shard_map/pallas_call | solution.py:430
  132.7 8.4 %all-to-all-start.4 = ((bf16[16,3,1152]{2,1,0:T(4,128)(2,1)}), bf16[16,3,1152]{2,1,0:T(4,128)(2,1)S(1)}, u32[]{:S(2)}, u32[]{:S(2)}) async-start(bf16[16,3,1152]{2,1,0:T(4,128)(2,1)} %reshape.601), calls=%async_computation.4 | async-start | bytes 294912 | tf_op jit(solution)/shard_map/all_to_all | solution.py:468
  143.2 12.3 %all-to-all-done.4 = bf16[16,3,1152]{2,1,0:T(4,128)(2,1)S(1)} async-done(((bf16[16,3,1152]{2,1,0:T(4,128)(2,1)}), bf16[16,3,1152]{2,1,0:T(4,128)(2,1)S(1)}, u32[]{:S(2)}, u32[]{:S(2)}) %all-to-all-start.4) | async-done | bytes 110624 | tf_op jit(solution)/shard_map/all_to_all | solution.py:468
  156.1 4.2 %all-to-all-start.5 = ((bf16[8,3,1152]{2,1,0:T(4,128)(2,1)}), bf16[8,3,1152]{2,1,0:T(4,128)(2,1)S(1)}, u32[]{:S(2)}, u32[]{:S(2)}) async-start(bf16[8,3,1152]{2,1,0:T(4,128)(2,1)} %broadcast_in_dim.42), calls=%async_computation.5 | async-start | bytes 147456 | tf_op jit(solution)/shard_map/all_to_all | solution.py:470
  160.4 5.4 %all-to-all-done.5 = bf16[8,3,1152]{2,1,0:T(4,128)(2,1)S(1)} async-done(((bf16[8,3,1152]{2,1,0:T(4,128)(2,1)}), bf16[8,3,1152]{2,1,0:T(4,128)(2,1)S(1)}, u32[]{:S(2)}, u32[]{:S(2)}) %all-to-all-start.5) | async-done | bytes 55328 | tf_op jit(solution)/shard_map/all_to_all | solution.py:470
  166.5 5.6 %all-to-all-start.6 = ((bf16[16,3,1152]{2,1,0:T(4,128)(2,1)}), bf16[16,3,1152]{2,1,0:T(4,128)(2,1)S(1)}, u32[]{:S(2)}, u32[]{:S(2)}) async-start(bf16[16,3,1152]{2,1,0:T(4,128)(2,1)} %bitcast.19), calls=%async_computation.6 | async-start | bytes 294912 | tf_op jit(solution)/shard_map/all_to_all | solution.py:473
  172.9 7.7 %collective-permute-start.11 = (bf16[32,1152]{1,0:T(8,128)(2,1)S(1)}, bf16[32,1152]{1,0:T(8,128)(2,1)S(1)}, u32[]{:S(2)}, u32[]{:S(2)}) collective-permute-start(bf16[32,1152]{1,0:T(8,128)(2,1)S(1)} %get-tuple-element.40), channel_id=1, source_target_pairs={{0,32},{32,64},{64,96},{96,0},{1,33},{33,65},{65,97},{97,1},{2,34}... | collective-permute-start | bytes 221192 | tf_op jit(solution)/shard_map/ppermute | solution.py:456
  180.6 7.3 %collective-permute-start.12 = (bf16[32,1152]{1,0:T(8,128)(2,1)S(1)}, bf16[32,1152]{1,0:T(8,128)(2,1)S(1)}, u32[]{:S(2)}, u32[]{:S(2)}) collective-permute-start(bf16[32,1152]{1,0:T(8,128)(2,1)S(1)} %get-tuple-element.39), channel_id=1, source_target_pairs={{0,64},{32,96},{64,0},{96,32},{1,65},{33,97},{65,1},{97,33},{2,66}... | collective-permute-start | bytes 221192 | tf_op jit(solution)/shard_map/ppermute | solution.py:456
  187.9 7.3 %collective-permute-start.13 = (bf16[32,1152]{1,0:T(8,128)(2,1)S(1)}, bf16[32,1152]{1,0:T(8,128)(2,1)S(1)}, u32[]{:S(2)}, u32[]{:S(2)}) collective-permute-start(bf16[32,1152]{1,0:T(8,128)(2,1)S(1)} %get-tuple-element.38), channel_id=1, source_target_pairs={{0,96},{32,0},{64,32},{96,64},{1,97},{33,1},{65,33},{97,65},{2,98}... | collective-permute-start | bytes 221192 | tf_op jit(solution)/shard_map/ppermute | solution.py:456
  196.0 6.0 %collective-permute-done.12.refs_2_ = bf16[32,1152]{1,0:T(8,128)(2,1)S(1)} collective-permute-done((bf16[32,1152]{1,0:T(8,128)(2,1)S(1)}, bf16[32,1152]{1,0:T(8,128)(2,1)S(1)}, u32[]{:S(2)}, u32[]{:S(2)}) %collective-permute-start.12) | collective-permute-done | bytes 73760 | tf_op jit(solution)/shard_map/ppermute | solution.py:456
  204.6 2.9 %shard_map.92 = bf16[128,1152]{1,0:T(8,128)(2,1)} custom-call(f32[2]{0:T(128)} %pad_maximum_fusion.5.power_ref, s32[1]{0:T(128)} %bitcast.2.x_ref, s32[1]{0:T(128)} %bitcast.3.level_ref, bf16[128,1152]{1,0:T(8,128)(2,1)} %bitcast.43, bf16[128,1152]{1,0:T(8,128)(2,1)} %bitcast.45, f32[3,1152]{1,0:T(4,128)} %bitcast.49, ...), custom_call_target="tpu_custom_call" | custom-call | flops 4423680 | bytes 1179648 | tf_op jit(solution)/shard_map/pallas_call | solution.py:458
  (88 shorter events, 19.3 us)
Async XLA Ops:
  0.6 8.1 %copy-start = (f32[1,2,3,1152]{3,1,2,0:T(2,128)S(1)}, f32[1,2,3,1152]{3,1,2,0:T(2,128)}, u32[]{:S(2)}) copy-start(f32[1,2,3,1152]{3,1,2,0:T(2,128)} %param.9) | copy-start | bytes 82948
  2.8 23.4 %all-to-all-start = ((bf16[4,72,1152]{2,1,0:T(8,128)(2,1)}), bf16[4,72,1152]{2,1,0:T(8,128)(2,1)S(1)}, u32[]{:S(2)}, u32[]{:S(2)}) async-start(bf16[4,72,1152]{2,1,0:T(8,128)(2,1)} %shard_map.87), calls=%async_computation | async-start | bytes 1327104 | tf_op jit(solution)/shard_map/all_to_all | solution.py:360
  26.2 23.2 %copy-start.1 = (bf16[4,72,1152]{2,1,0:T(8,128)(2,1)}, bf16[4,72,1152]{2,1,0:T(8,128)(2,1)S(1)}, u32[]{:S(2)}) copy-start(bf16[4,72,1152]{2,1,0:T(8,128)(2,1)S(1)} %all-to-all-done) | copy-start | bytes 1990660
  26.2 15.1 %copy-start.13 = (f32[2,72]{1,0:T(2,128)S(1)}, f32[2,72]{1,0:T(2,128)}, u32[]{:S(2)}) copy-start(f32[2,72]{1,0:T(2,128)} %param.13) | copy-start | bytes 1732
  28.3 43.6 %all-to-all-start.1 = ((bf16[4,64,1152]{2,1,0:T(8,128)(2,1)}), bf16[4,64,1152]{2,1,0:T(8,128)(2,1)}, u32[]{:S(2)}, u32[]{:S(2)}) async-start(bf16[4,64,1152]{2,1,0:T(8,128)(2,1)} %pad_maximum_fusion), calls=%async_computation.1 | async-start | bytes 1179648 | tf_op jit(solution)/shard_map/all_to_all | solution.py:382
  41.9 37.8 %collective-permute-start.3 = (bf16[288,1152]{1,0:T(8,128)(2,1)S(1)}, bf16[288,1152]{1,0:T(8,128)(2,1)S(1)}, u32[]{:S(2)}, u32[]{:S(2)}) collective-permute-start(bf16[288,1152]{1,0:T(8,128)(2,1)S(1)} %bitcast.36), channel_id=1, source_target_pairs={{0,3},{1,0},{2,1},{3,2},{4,7},{5,4},{6,5},{7,6},{8,11},{9,8},{10,9... | collective-permute-start | bytes 1990664 | tf_op jit(solution)/shard_map/ppermute | solution.py:362
  46.6 33.2 %collective-permute-start.4 = (bf16[288,1152]{1,0:T(8,128)(2,1)S(1)}, bf16[288,1152]{1,0:T(8,128)(2,1)S(1)}, u32[]{:S(2)}, u32[]{:S(2)}) collective-permute-start(bf16[288,1152]{1,0:T(8,128)(2,1)S(1)} %bitcast.37), channel_id=1, source_target_pairs={{0,2},{1,3},{2,0},{3,1},{4,6},{5,7},{6,4},{7,5},{8,10},{9,11},{10,... | collective-permute-start | bytes 1990664 | tf_op jit(solution)/shard_map/ppermute | solution.py:362
  49.3 30.5 %collective-permute-start.5 = (bf16[288,1152]{1,0:T(8,128)(2,1)S(1)}, bf16[288,1152]{1,0:T(8,128)(2,1)}, u32[]{:S(2)}, u32[]{:S(2)}) collective-permute-start(bf16[288,1152]{1,0:T(8,128)(2,1)S(1)} %bitcast.38), channel_id=1, source_target_pairs={{0,1},{1,2},{2,3},{3,0},{4,5},{5,6},{6,7},{7,4},{8,9},{9,10},{10,1... | collective-permute-start | bytes 1990664 | tf_op jit(solution)/shard_map/ppermute | solution.py:362
  73.8 16.0 %copy-start.3 = (bf16[4,32,1152]{2,1,0:T(8,128)(2,1)}, bf16[4,32,1152]{2,1,0:T(8,128)(2,1)S(1)}, u32[]{:S(2)}) copy-start(bf16[4,32,1152]{2,1,0:T(8,128)(2,1)S(1)} %get-tuple-element.37.refs_0_) | copy-start | bytes 884740
  73.8 18.3 %collective-permute-start.7 = (bf16[4,32,1152]{2,1,0:T(8,128)(2,1)}, bf16[4,32,1152]{2,1,0:T(8,128)(2,1)S(1)}, u32[]{:S(2)}, u32[]{:S(2)}) collective-permute-start(bf16[4,32,1152]{2,1,0:T(8,128)(2,1)} %get-tuple-element.36.refs_0_), channel_id=1, source_target_pairs={{0,128},{128,0},{1,129},{129,1},{2,130},{130,2},{3,131},{131,3},{4... | collective-permute-start | bytes 884744 | tf_op jit(solution)/shard_map/ppermute | solution.py:379
  76.5 17.7 %collective-permute-start.1 = (bf16[4,32,1152]{2,1,0:T(8,128)(2,1)S(1)}, bf16[4,32,1152]{2,1,0:T(8,128)(2,1)S(1)}, u32[]{:S(2)}, u32[]{:S(2)}) collective-permute-start(bf16[4,32,1152]{2,1,0:T(8,128)(2,1)S(1)} %get-tuple-element.37.refs_0_), channel_id=1, source_target_pairs={{0,128},{128,0},{1,129},{129,1},{2,130},{130,2},{3,131},{131,3},{4... | collective-permute-start | bytes 884744 | tf_op jit(solution)/shard_map/ppermute | solution.py:379
  79.8 1.1 copy-start.5
  83.5 26.7 %all-to-all-start.2 = ((bf16[4,288,288]{2,1,0:T(8,128)(2,1)}), bf16[4,288,288]{2,1,0:T(8,128)(2,1)S(1)}, u32[]{:S(2)}, u32[]{:S(2)}) async-start(bf16[4,288,288]{2,1,0:T(8,128)(2,1)} %shard_map.88), calls=%async_computation.2 | async-start | bytes 1769472 | tf_op jit(solution)/shard_map/all_to_all | solution.py:401
  87.8 9.7 %collective-permute-start.6 = (bf16[4,32,1152]{2,1,0:T(8,128)(2,1)}, bf16[4,32,1152]{2,1,0:T(8,128)(2,1)S(1)}, u32[]{:S(2)}, u32[]{:S(2)}) collective-permute-start(bf16[4,32,1152]{2,1,0:T(8,128)(2,1)} %get-tuple-element.36.refs_0_), channel_id=1, source_target_pairs={{0,16},{16,0},{1,17},{17,1},{2,18},{18,2},{3,19},{19,3},{4,20},{20... | collective-permute-start | bytes 884744 | tf_op jit(solution)/shard_map/ppermute | solution.py:376
  89.8 16.7 %collective-permute-start = (bf16[4,32,1152]{2,1,0:T(8,128)(2,1)S(1)}, bf16[4,32,1152]{2,1,0:T(8,128)(2,1)S(1)}, u32[]{:S(2)}, u32[]{:S(2)}) collective-permute-start(bf16[4,32,1152]{2,1,0:T(8,128)(2,1)S(1)} %get-tuple-element.37.refs_0_), channel_id=1, source_target_pairs={{0,16},{16,0},{1,17},{17,1},{2,18},{18,2},{3,19},{19,3},{4,20},{20... | collective-permute-start | bytes 884744 | tf_op jit(solution)/shard_map/ppermute | solution.py:376
  92.1 5.3 %copy-start.14 = (bf16[4,32,1152]{2,1,0:T(8,128)(2,1)}, bf16[4,32,1152]{2,1,0:T(8,128)(2,1)S(1)}, u32[]{:S(2)}) copy-start(bf16[4,32,1152]{2,1,0:T(8,128)(2,1)S(1)} %collective-permute-done.7.refs_2_) | copy-start | bytes 884740
  92.1 5.3 %collective-permute-start.8 = (bf16[4,32,1152]{2,1,0:T(8,128)(2,1)S(1)}, bf16[4,32,1152]{2,1,0:T(8,128)(2,1)S(1)}, u32[]{:S(2)}, u32[]{:S(2)}) collective-permute-start(bf16[4,32,1152]{2,1,0:T(8,128)(2,1)S(1)} %collective-permute-done.7.refs_2_), channel_id=1, source_target_pairs={{0,16},{16,0},{1,17},{17,1},{2,18},{18,2},{3,19},{19,3},{4,20},{20... | collective-permute-start | bytes 884744 | tf_op jit(solution)/shard_map/ppermute | solution.py:376
  94.2 12.3 %copy-start.6 = (bf16[4,32,1152]{2,1,0:T(8,128)(2,1)}, bf16[4,32,1152]{2,1,0:T(8,128)(2,1)S(1)}, u32[]{:S(2)}) copy-start(bf16[4,32,1152]{2,1,0:T(8,128)(2,1)S(1)} %collective-permute-done.1.refs_2_) | copy-start | bytes 884740
  94.2 12.3 %collective-permute-start.2 = (bf16[4,32,1152]{2,1,0:T(8,128)(2,1)S(1)}, bf16[4,32,1152]{2,1,0:T(8,128)(2,1)S(1)}, u32[]{:S(2)}, u32[]{:S(2)}) collective-permute-start(bf16[4,32,1152]{2,1,0:T(8,128)(2,1)S(1)} %collective-permute-done.1.refs_2_), channel_id=1, source_target_pairs={{0,16},{16,0},{1,17},{17,1},{2,18},{18,2},{3,19},{19,3},{4,20},{20... | collective-permute-start | bytes 884744 | tf_op jit(solution)/shard_map/ppermute | solution.py:376
  110.3 8.1 %copy-start.2 = (bf16[4,288,288]{2,1,0:T(8,128)(2,1)}, bf16[4,288,288]{2,1,0:T(8,128)(2,1)S(1)}, u32[]{:S(2)}) copy-start(bf16[4,288,288]{2,1,0:T(8,128)(2,1)S(1)} %all-to-all-done.2.refs_8_) | copy-start | bytes 1990660
  110.3 19.6 %all-to-all-start.3 = ((bf16[8,36,1152]{2,1,0:T(8,128)(2,1)}), bf16[8,36,1152]{2,1,0:T(8,128)(2,1)S(1)}, u32[]{:S(2)}, u32[]{:S(2)}) async-start(bf16[8,36,1152]{2,1,0:T(8,128)(2,1)} %shard_map.90), calls=%async_computation.3 | async-start | bytes 1474560 | tf_op jit(solution)/shard_map/all_to_all | solution.py:426
  129.9 11.2 %copy-start.9 = (f32[2,4,32,1152]{3,2,1,0:T(8,128)S(1)}, f32[2,4,32,1152]{3,2,1,0:T(8,128)}, u32[]{:S(2)}) copy-start(f32[2,4,32,1152]{3,2,1,0:T(8,128)} %get-tuple-element.30) | copy-start | bytes 3538948
  130.8 10.3 %collective-permute-start.9 = (bf16[2,4,32,1152]{3,2,1,0:T(8,128)(2,1)}, bf16[2,4,32,1152]{3,2,1,0:T(8,128)(2,1)S(1)}, u32[]{:S(2)}, u32[]{:S(2)}) collective-permute-start(bf16[2,4,32,1152]{3,2,1,0:T(8,128)(2,1)} %get-tuple-element.33), channel_id=1, source_target_pairs={{0,16},{16,0},{1,17},{17,1},{2,18},{18,2},{3,19},{19,3},{4,20},{20... | collective-permute-start | bytes 1769480 | tf_op jit(solution)/shard_map/ppermute | solution.py:376
  132.7 22.7 %all-to-all-start.4 = ((bf16[16,3,1152]{2,1,0:T(4,128)(2,1)}), bf16[16,3,1152]{2,1,0:T(4,128)(2,1)S(1)}, u32[]{:S(2)}, u32[]{:S(2)}) async-start(bf16[16,3,1152]{2,1,0:T(4,128)(2,1)} %reshape.601), calls=%async_computation.4 | async-start | bytes 294912 | tf_op jit(solution)/shard_map/all_to_all | solution.py:468
  141.2 30.9 %collective-permute-start.10 = (bf16[4,32,1152]{2,1,0:T(8,128)(2,1)S(1)}, bf16[4,32,1152]{2,1,0:T(8,128)(2,1)S(1)}, u32[]{:S(2)}, u32[]{:S(2)}) collective-permute-start(bf16[4,32,1152]{2,1,0:T(8,128)(2,1)S(1)} %fusion.1), channel_id=1, source_target_pairs={{0,128},{128,0},{1,129},{129,1},{2,130},{130,2},{3,131},{131,3},{4... | collective-permute-start | bytes 884744 | tf_op jit(solution)/shard_map/ppermute | solution.py:379
  156.1 9.6 %all-to-all-start.5 = ((bf16[8,3,1152]{2,1,0:T(4,128)(2,1)}), bf16[8,3,1152]{2,1,0:T(4,128)(2,1)S(1)}, u32[]{:S(2)}, u32[]{:S(2)}) async-start(bf16[8,3,1152]{2,1,0:T(4,128)(2,1)} %broadcast_in_dim.42), calls=%async_computation.5 | async-start | bytes 147456 | tf_op jit(solution)/shard_map/all_to_all | solution.py:470
  166.5 28.7 %all-to-all-start.6 = ((bf16[16,3,1152]{2,1,0:T(4,128)(2,1)}), bf16[16,3,1152]{2,1,0:T(4,128)(2,1)S(1)}, u32[]{:S(2)}, u32[]{:S(2)}) async-start(bf16[16,3,1152]{2,1,0:T(4,128)(2,1)} %bitcast.19), calls=%async_computation.6 | async-start | bytes 294912 | tf_op jit(solution)/shard_map/all_to_all | solution.py:473
  172.9 23.1 %collective-permute-start.11 = (bf16[32,1152]{1,0:T(8,128)(2,1)S(1)}, bf16[32,1152]{1,0:T(8,128)(2,1)S(1)}, u32[]{:S(2)}, u32[]{:S(2)}) collective-permute-start(bf16[32,1152]{1,0:T(8,128)(2,1)S(1)} %get-tuple-element.40), channel_id=1, source_target_pairs={{0,32},{32,64},{64,96},{96,0},{1,33},{33,65},{65,97},{97,1},{2,34}... | collective-permute-start | bytes 221192 | tf_op jit(solution)/shard_map/ppermute | solution.py:456
  180.6 21.4 %collective-permute-start.12 = (bf16[32,1152]{1,0:T(8,128)(2,1)S(1)}, bf16[32,1152]{1,0:T(8,128)(2,1)S(1)}, u32[]{:S(2)}, u32[]{:S(2)}) collective-permute-start(bf16[32,1152]{1,0:T(8,128)(2,1)S(1)} %get-tuple-element.39), channel_id=1, source_target_pairs={{0,64},{32,96},{64,0},{96,32},{1,65},{33,97},{65,1},{97,33},{2,66}... | collective-permute-start | bytes 221192 | tf_op jit(solution)/shard_map/ppermute | solution.py:456
  187.9 16.1 %collective-permute-start.13 = (bf16[32,1152]{1,0:T(8,128)(2,1)S(1)}, bf16[32,1152]{1,0:T(8,128)(2,1)S(1)}, u32[]{:S(2)}, u32[]{:S(2)}) collective-permute-start(bf16[32,1152]{1,0:T(8,128)(2,1)S(1)} %get-tuple-element.38), channel_id=1, source_target_pairs={{0,96},{32,0},{64,32},{96,64},{1,97},{33,1},{65,33},{97,65},{2,98}... | collective-permute-start | bytes 221192 | tf_op jit(solution)/shard_map/ppermute | solution.py:456
  196.0 8.0 %copy-start.10 = (bf16[32,1152]{1,0:T(8,128)(2,1)}, bf16[32,1152]{1,0:T(8,128)(2,1)S(1)}, u32[]{:S(2)}) copy-start(bf16[32,1152]{1,0:T(8,128)(2,1)S(1)} %collective-permute-done.11.refs_1_) | copy-start | bytes 221188
  202.0 2.0 copy-start.11
  (6 other events, 4.5 us)

commit v4 on v3

--- a/solution.py
+++ b/solution.py
@@ -38,7 +38,7 @@
     return centred * factor, factor
 
 
-def home_forward(power_ref, x_ref, hidden_ref, grad_ref, mod_ref, out_ref, branch_ref, turned_ref):
+def home_forward(power_ref, x_ref, hidden_ref, grad_ref, mod_ref, out_ref, turned_ref):
     normed, _ = normalise(hidden_ref[...], power_ref[0], power_ref[1])
     modded = normed * (1.0 + mod_ref[1:2, :]) + mod_ref[0:1, :]
     for x in range(4):
@@ -48,16 +48,13 @@
             for place, block in enumerate(block_order(x)):
                 turned_ref[:, place * HD : (place + 1) * HD] = modded[:, block * HD : (block + 1) * HD]
 
-    out_ref[...] = turned_ref[...].astype(BF16).reshape(ZS, TOK, D)
-    branch_ref[...] = (mod_ref[2:3, :] * grad_ref[...].astype(F32)).astype(BF16).reshape(ZS, TOK, D)
-
-
-def home_backward(power_ref, x_ref, level_ref, hidden_ref, grad_ref, mod_ref, *refs):
-    *back_refs, out_ref, turned_ref, back_ref = refs
-    for step, piece_ref in enumerate(back_refs):
-        back_ref[lax.rem(level_ref[0] + ZS - step, ZS)] = piece_ref[...].astype(F32)
+    out_ref[:, :TOK, :] = turned_ref[...].astype(BF16).reshape(ZS, TOK, D)
+    out_ref[:, TOK:, :] = (mod_ref[2:3, :] * grad_ref[...].astype(F32)).astype(BF16).reshape(ZS, TOK, D)
+
+
+def home_backward(power_ref, x_ref, hidden_ref, grad_ref, mod_ref, back_ref, out_ref, turned_ref):
     normed, factor = normalise(hidden_ref[...], power_ref[0], power_ref[1])
-    back = back_ref[...].reshape(ROWS, D)
+    back = back_ref[:, :TOK, :].reshape(ROWS, D).astype(F32)
     for x in range(4):
 
         @pl.when(x_ref[0] == x)
@@ -179,9 +176,9 @@
     return exps / jnp.sum(exps, axis=-1, keepdims=True)
 
 
-def gather_rows(refs):
+def gather_rows(refs, start):
     return jnp.concatenate(
-        [ref[:, first : first + 16, :].reshape(ZS * 16, D) for first in (0, 16) for ref in refs], axis=0
+        [ref[:, first : first + 16, :].reshape(ZS * 16, D) for first in (start, start + 16) for ref in refs], axis=0
     )
 
 
@@ -208,7 +205,7 @@
         refs[:4], refs[4:8], refs[8:]
     )
     copies = fetch_weights(block_refs, w_ref, sem)
-    modded = gather_rows(row_refs)
+    modded = gather_rows(row_refs, 0)
     members = head_members()
     for copy in copies:
         copy.wait()
@@ -240,7 +237,7 @@
 
 def chip_term(*refs):
     row_refs, (att_ref, part_ref) = refs[:4], refs[4:]
-    total = tn(att_ref[...], gather_rows(row_refs))
+    total = tn(att_ref[...], gather_rows(row_refs, TOK))
     for piece in range(8):
         part_ref[piece] = total[36 * piece : 36 * (piece + 1)].astype(BF16)
 
@@ -254,7 +251,7 @@
     copies = fetch_weights(block_refs, w_ref, sem)
     for place in range(4):
         wide_ref[:, place * PART : (place + 1) * PART] = wo_ref[place].astype(F32)
-    do_ref[...] = widen(nt(gather_rows(row_refs), wide_ref[...].astype(BF16))).astype(BF16)
+    do_ref[...] = widen(nt(gather_rows(row_refs, TOK), wide_ref[...].astype(BF16))).astype(BF16)
     same = same_token()
     members = head_members()
     for ref in (dv_ref, dqh_ref, dkh_ref):
@@ -362,11 +359,11 @@
         lax.ppermute(block, "x", [(i, (i + 4 - step) % 4) for i in range(4)]) for step in (1, 2, 3)
     ]
 
-    sent, sent_branch = pl.pallas_call(
+    sent = pl.pallas_call(
         home_forward,
-        out_shape=[jax.ShapeDtypeStruct((ZS, TOK, D), BF16)] * 2,
+        out_shape=jax.ShapeDtypeStruct((ZS, 2 * TOK, D), BF16),
         in_specs=[smem, smem, vmem, vmem, vmem],
-        out_specs=[vmem, vmem],
+        out_specs=vmem,
         scratch_shapes=[pltpu.VMEM((ROWS, D), F32)],
         compiler_params=PARAMS,
         cost_estimate=cost(20 * ROWS * D, 8 * ROWS * D),
@@ -381,14 +378,11 @@
     def exchange(values):
         return lax.all_to_all(values, "zh", 0, 0, tiled=True)
 
-    def from_frames(own):
-        across = other_y(own)
-        return [own, other_core(own), across, other_core(across)]
-
-    sent, _ = lax.optimization_barrier((sent, block))
-    both = exchange(jnp.concatenate([sent, sent_branch], axis=1))
-    modded = from_frames(both[:, :TOK])
-    branch = from_frames(both[:, TOK:])
+    tables, tables_back = turn_tables(qk_gain, yl, core)
+    sent, _, tables, tables_back = lax.optimization_barrier((sent, block, tables, tables_back))
+    own = exchange(sent)
+    across = other_y(own)
+    near = other_core(own)
     w_back = pl.pallas_call(
         out_rows,
         out_shape=jax.ShapeDtypeStruct((4, PART, PART), BF16),
@@ -398,9 +392,10 @@
         compiler_params=PARAMS,
         cost_estimate=cost(10**6, 2 * 10**6),
     )(x_place, *blocks)
+    across, w_back = lax.optimization_barrier((across, w_back))
+    arrays = [own, near, across, other_core(across)]
     w_back = lax.all_to_all(w_back, ("yl", "c"), 0, 0, tiled=True)
 
-    tables, tables_back = turn_tables(qk_gain, yl, core)
     wide = jax.ShapeDtypeStruct((ALL, WIDE), BF16)
     factors = jax.ShapeDtypeStruct((ALL, 128), F32)
     *kept, attended = pl.pallas_call(
@@ -411,7 +406,7 @@
         scratch_shapes=[pltpu.VMEM((D, D), BF16), four],
         compiler_params=PARAMS,
         cost_estimate=cost(2 * ALL * D * 4 * PART, 12 * 10**6),
-    )(*modded, *blocks, tables)
+    )(*arrays, *blocks, tables)
     part = pl.pallas_call(
         chip_term,
         out_shape=jax.ShapeDtypeStruct((8, 36, D), BF16),
@@ -419,13 +414,11 @@
         out_specs=vmem,
         compiler_params=PARAMS,
         cost_estimate=cost(2 * ALL * D * PART, 2 * 10**6),
-    )(*branch, attended)
+    )(*arrays, attended)
 
     w_back, part = lax.optimization_barrier((w_back, part))
 
     plane = lax.all_to_all(part, ("yh", "x"), 0, 0, tiled=True)
-    plane = jnp.sum(plane.astype(F32), axis=0).astype(BF16)
-    plane = jnp.pad(plane, ((0, 12), (0, 0))).reshape(16, 3, D)
 
     mine, theirs = pl.pallas_call(
         chip_backward,
@@ -444,33 +437,33 @@
         ],
         compiler_params=PARAMS,
         cost_estimate=cost(2 * ALL * D * 4 * PART, 14 * 10**6),
-    )(*branch, *blocks, w_back, tables_back, *kept)
-    theirs, _ = lax.optimization_barrier((theirs, plane))
+    )(*arrays, *blocks, w_back, tables_back, *kept)
+    theirs, plane = lax.optimization_barrier((theirs, plane))
+    plane = jnp.sum(plane.astype(F32), axis=0).astype(BF16)
+    plane = plane.reshape(4, 9, D)
     arrived = other_core(theirs)
     across = (mine[1] + arrived[1].astype(F32)).astype(BF16)
-    summed = (mine[0] + arrived[0].astype(F32) + other_y(across).astype(F32)).astype(BF16)
-    level = lax.axis_index("zh")
-    pieces = [lax.dynamic_index_in_dim(summed, level, 0, keepdims=False)]
-    for step in range(1, ZS):
-        piece = lax.dynamic_index_in_dim(summed, lax.rem(level + step, ZS), 0, keepdims=False)
-        pieces.append(lax.ppermute(piece, "zh", [(i, (i + step) % ZS) for i in range(ZS)]))
-    level = level[None]
+    from_y = other_y(across)
+    summed = (mine[0] + arrived[0].astype(F32) + from_y.astype(F32)).astype(BF16)
+
+    levels = lax.all_to_all(plane, "zl", 0, 0, tiled=True)
+    level = jnp.sum(levels.astype(F32), axis=0).astype(BF16)
+    level, summed = lax.optimization_barrier((level, summed))
+    spread = lax.all_to_all(jnp.broadcast_to(level[None], (8, 9, D)), ("c", "x"), 0, 0, tiled=True)
+    wanted = lax.dynamic_index_in_dim(spread.reshape(4, 2, 9, D), core, 1, keepdims=False)
+    joined = jnp.concatenate([summed, jnp.pad(wanted, ((0, 0), (0, 7), (0, 0)))], axis=1)
+    joined = exchange(joined)
     d_hidden = pl.pallas_call(
         home_backward,
         out_shape=jax.ShapeDtypeStruct((ROWS, D), BF16),
-        in_specs=[smem, smem, smem] + [vmem] * 7,
+        in_specs=[smem, smem, vmem, vmem, vmem, vmem],
         out_specs=vmem,
-        scratch_shapes=[pltpu.VMEM((ROWS, D), F32), pltpu.VMEM((ZS, TOK, D), F32)],
+        scratch_shapes=[pltpu.VMEM((ROWS, D), F32)],
         compiler_params=PARAMS,
         cost_estimate=cost(30 * ROWS * D, 8 * ROWS * D),
-    )(power, x_place, level, rows, cotangent, mod, *pieces)
-
-    levels = lax.all_to_all(plane, ("zh", "zl"), 0, 0, tiled=True)
-    level = jnp.sum(levels.astype(F32), axis=0).astype(BF16)
-    spread = lax.all_to_all(jnp.broadcast_to(level[None], (8, 3, D)), ("c", "x"), 0, 0, tiled=True)
-    wanted = lax.dynamic_index_in_dim(spread.reshape(4, 2, 3, D), core, 1, keepdims=False)
-    wanted = jnp.broadcast_to(wanted[:, None], (4, 4, 3, D)).reshape(16, 3, D)
-    final = lax.all_to_all(wanted, ("zh", "zl"), 0, 0, tiled=True).reshape(48, D)[:36]
+    )(power, x_place, rows, cotangent, mod, joined)
+    share = jnp.sum(joined[:, TOK : TOK + 9].astype(F32), axis=0).astype(BF16)
+    final = lax.all_to_all(jnp.broadcast_to(share[None], (4, 9, D)), "zl", 0, 0, tiled=True).reshape(36, D)
     return d_hidden[None, None], final.astype(F32) / 32.0
 
 

time: 209 us -> 202 us (0.967)
  blocking collectives: 0 us -> 44.8 us
  starting transfers between devices: 99.4 us -> 60 us
  waiting for transfers between devices: 58.4 us -> 49.7 us
  local copies, waits for them, and re-layouts: 12.1 us -> 7.54 us
    all_to_all x0 -> x2, blocking collectives: none -> 44.8 us  [the longest x1 34.7 us: exchange(): return lax.all_to_all(values, 'zh', 0, 0, tiled=True)]
    ppermute x3 -> x0, starting transfers between devices: 22.3 us -> none  [on_device(): lax.ppermute(piece, 'zh', [(i, (i + step) % ZS) for i in range(ZS)])]
    all_to_all x3 -> x2, starting transfers between devices: 18.3 us -> 7.95 us  [the longest x1 4.24 us: on_device(): lax.all_to_all(jnp.broadcast_to(level[None], (8, 9, D)), ('c', 'x'), 0, 0...]
    ppermute x3 -> x0, waiting for transfers between devices: 7.97 us -> none  [on_device(): lax.ppermute(piece, 'zh', [(i, (i + step) % ZS) for i in range(ZS)])]
    all_to_all x3 -> x2, waiting for transfers between devices: 17.6 us -> 10.5 us  [the longest x1 7.27 us: on_device(): lax.all_to_all(jnp.broadcast_to(level[None], (8, 9, D)), ('c', 'x'), 0, 0...]
    ppermute x3 -> x2, waiting for transfers between devices: 0.01 us -> 5.24 us  [other_y(): return lax.ppermute(values, 'yl', [(0, 1), (1, 0)])]
    ppermute x5 -> x3, starting transfers between devices: 10.5 us -> 5.75 us  [other_core(): return lax.ppermute(values, 'c', [(0, 1), (1, 0)])]
    ppermute x3 -> x2, starting transfers between devices: 7.77 us -> 4.6 us  [other_y(): return lax.ppermute(values, 'yl', [(0, 1), (1, 0)])]
  transfers between devices with their start and end apart: 21 -> 14, of which waited for: 6 -> 8; matrix products, arithmetic and copies ran while one was open for 4% -> 2% of each run, Pallas kernels for 13% -> 16%
where the time goes in v4:
time: 202 us; the launch traced here: 200 us
  starting transfers between devices  60 us (30%)
  waiting for transfers between devices  49.7 us (25%)
  blocking collectives  44.8 us (22%)
  Pallas kernels  33.5 us (17%)
  local copies, waits for them, and re-layouts  7.54 us (4%)
  other arithmetic  2.4 us (1%)
    all_to_all x1, blocking collectives, exchange(): return lax.all_to_all(values, 'zh', 0, 0, tiled=True)  34.7 us
    all_to_all x1, waiting for transfers between devices, exchange(): return lax.all_to_all(values, 'zh', 0, 0, tiled=True)  19.2 us
    all_to_all x1, starting transfers between devices, exchange(): return lax.all_to_all(values, 'zh', 0, 0, tiled=True)  12.9 us
    pallas_call x1, Pallas kernels, on_device(): pl.pallas_call(chip_backward, out_shape=[jax.ShapeDtypeStruct((2, ZS, TOK...  12 us
    ppermute x3, starting transfers between devices, on_device(): lax.ppermute(block, 'x', [(i, (i + 4 - step) % 4) for i in range(4)])  11.4 us
    all_to_all x1, waiting for transfers between devices, on_device(): block = lax.all_to_all(unit, 'zl', 0, 0, tiled=True).reshape(PART, 4 * PART)  10.4 us
    all_to_all x1, blocking collectives, on_device(): levels = lax.all_to_all(plane, 'zl', 0, 0, tiled=True)  10.2 us
    pallas_call x1, Pallas kernels, on_device(): pl.pallas_call(chip_forward, out_shape=[wide] * 5 + [factors] * 2 + [wide...  8.05 us
  transfers between devices with their start and end apart: 14, of which 8 were waited for; matrix products, arithmetic and copies ran while one was open for 2% of the time, Pallas kernels for 16%

profile of v4, /device:TPU:24, one launch (start us, length us, event | category | flops | bytes accessed | tf_op | source)
XLA Modules:
  0.0 199.6 jit_solution(6030808788393855945)
XLA Ops:
  0.7 2.2 %shard_map.87 = bf16[4,72,1152]{2,1,0:T(8,128)(2,1)} custom-call(s32[1]{0:T(128)} %bitcast.5.place_ref, bf16[72,3456]{1,0:T(8,128)(2,1)} %w_qkv_ref.1, bf16[72,1152]{1,0:T(8,128)(2,1)} %w_out_ref.1), custom_call_target="tpu_custom_call" | custom-call | flops 1000000 | bytes 2000000 | tf_op jit(solution)/shard_map/pallas_call | solution.py:348
  2.8 5.9 %all-to-all-start = ((bf16[4,72,1152]{2,1,0:T(8,128)(2,1)}), bf16[4,72,1152]{2,1,0:T(8,128)(2,1)S(1)}, u32[]{:S(2)}, u32[]{:S(2)}) async-start(bf16[4,72,1152]{2,1,0:T(8,128)(2,1)} %shard_map.87), calls=%async_computation | async-start | bytes 1327104 | tf_op jit(solution)/shard_map/all_to_all | solution.py:357
  13.1 2.6 %shard_map.86 = bf16[4,64,1152]{2,1,0:T(8,128)(2,1)} custom-call(f32[2]{0:T(128)} %pad_maximum_fusion.4.power_ref, s32[1]{0:T(128)} %bitcast.2.x_ref, bf16[128,1152]{1,0:T(8,128)(2,1)} %bitcast.32, bf16[128,1152]{1,0:T(8,128)(2,1)} %bitcast.34, f32[3,1152]{1,0:T(4,128)} %bitcast.38), custom_call_target="tpu_custom_call" | custom-call | flops 2949120 | bytes 1179648 | tf_op jit(solution)/shard_map/pallas_call | solution.py:362
  15.8 10.4 %all-to-all-done = bf16[4,72,1152]{2,1,0:T(8,128)(2,1)S(1)} async-done(((bf16[4,72,1152]{2,1,0:T(8,128)(2,1)}), bf16[4,72,1152]{2,1,0:T(8,128)(2,1)S(1)}, u32[]{:S(2)}, u32[]{:S(2)}) %all-to-all-start) | async-done | bytes 663584 | tf_op jit(solution)/shard_map/all_to_all | solution.py:357
  26.2 12.9 %all-to-all-start.1 = ((bf16[4,64,1152]{2,1,0:T(8,128)(2,1)}), bf16[4,64,1152]{2,1,0:T(8,128)(2,1)S(1)}, u32[]{:S(2)}, u32[]{:S(2)}) async-start(bf16[4,64,1152]{2,1,0:T(8,128)(2,1)} %shard_map.86), calls=%async_computation.1 | async-start | bytes 1179648 | tf_op jit(solution)/shard_map/all_to_all | solution.py:379
  39.1 3.4 %collective-permute-start.4 = (bf16[288,1152]{1,0:T(8,128)(2,1)S(1)}, bf16[288,1152]{1,0:T(8,128)(2,1)S(1)}, u32[]{:S(2)}, u32[]{:S(2)}) collective-permute-start(bf16[288,1152]{1,0:T(8,128)(2,1)S(1)} %bitcast.26), channel_id=1, source_target_pairs={{0,1},{1,2},{2,3},{3,0},{4,5},{5,6},{6,7},{7,4},{8,9},{9,10},{10,1... | collective-permute-start | bytes 1990664 | tf_op jit(solution)/shard_map/ppermute | solution.py:359
  42.5 4.6 %collective-permute-start.3 = (bf16[288,1152]{1,0:T(8,128)(2,1)S(1)}, bf16[288,1152]{1,0:T(8,128)(2,1)S(1)}, u32[]{:S(2)}, u32[]{:S(2)}) collective-permute-start(bf16[288,1152]{1,0:T(8,128)(2,1)S(1)} %bitcast.27), channel_id=1, source_target_pairs={{0,2},{1,3},{2,0},{3,1},{4,6},{5,7},{6,4},{7,5},{8,10},{9,11},{10,... | collective-permute-start | bytes 1990664 | tf_op jit(solution)/shard_map/ppermute | solution.py:359
  47.2 3.3 %collective-permute-start.2 = (bf16[288,1152]{1,0:T(8,128)(2,1)S(1)}, bf16[288,1152]{1,0:T(8,128)(2,1)S(1)}, u32[]{:S(2)}, u32[]{:S(2)}) collective-permute-start(bf16[288,1152]{1,0:T(8,128)(2,1)S(1)} %bitcast.28), channel_id=1, source_target_pairs={{0,3},{1,0},{2,1},{3,2},{4,7},{5,4},{6,5},{7,6},{8,11},{9,8},{10,9... | collective-permute-start | bytes 1990664 | tf_op jit(solution)/shard_map/ppermute | solution.py:359
  50.5 19.2 %all-to-all-done.1.refs_0_ = bf16[4,64,1152]{2,1,0:T(8,128)(2,1)S(1)} async-done(((bf16[4,64,1152]{2,1,0:T(8,128)(2,1)}), bf16[4,64,1152]{2,1,0:T(8,128)(2,1)S(1)}, u32[]{:S(2)}, u32[]{:S(2)}) %all-to-all-start.1) | async-done | bytes 589856 | tf_op jit(solution)/shard_map/all_to_all | solution.py:379
  69.7 2.6 %collective-permute-start.1 = (bf16[4,64,1152]{2,1,0:T(8,128)(2,1)S(1)}, bf16[4,64,1152]{2,1,0:T(8,128)(2,1)}, u32[]{:S(2)}, u32[]{:S(2)}) collective-permute-start(bf16[4,64,1152]{2,1,0:T(8,128)(2,1)S(1)} %all-to-all-done.1.refs_0_), channel_id=1, source_target_pairs={{0,128},{128,0},{1,129},{129,1},{2,130},{130,2},{3,131},{131,3},{4... | collective-permute-start | bytes 1769480 | tf_op jit(solution)/shard_map/ppermute | solution.py:376
  73.1 1.5 collective-permute-done.2.refs_1_.refs_5_
  74.6 0.8 copy-done.5
  75.5 2.6 %shard_map.88 = bf16[4,288,288]{2,1,0:T(8,128)(2,1)} custom-call(s32[1]{0:T(128)} %bitcast.2.x_ref, bf16[288,1152]{1,0:T(8,128)(2,1)} %bitcast.29, bf16[288,1152]{1,0:T(8,128)(2,1)} %copy-done.5, bf16[288,1152]{1,0:T(8,128)(2,1)} %copy-done.4, bf16[288,1152]{1,0:T(8,128)(2,1)} %copy-done.3), custom_call_target="tpu_custom_call" | custom-call | flops 1000000 | bytes 2000000 | tf_op jit(solution)/shard_map/pallas_call | solution.py:386
  78.1 1.9 collective-permute-start
  80.0 5.2 %collective-permute-done.1.refs_2_ = bf16[4,64,1152]{2,1,0:T(8,128)(2,1)} collective-permute-done((bf16[4,64,1152]{2,1,0:T(8,128)(2,1)S(1)}, bf16[4,64,1152]{2,1,0:T(8,128)(2,1)}, u32[]{:S(2)}, u32[]{:S(2)}) %collective-permute-start.1) | collective-permute-done | bytes 589856 | tf_op jit(solution)/shard_map/ppermute | solution.py:376
  85.3 1.9 collective-permute-start.5
  87.2 4.2 %all-to-all-start.2 = ((bf16[4,288,288]{2,1,0:T(8,128)(2,1)}), bf16[4,288,288]{2,1,0:T(8,128)(2,1)S(1)}, u32[]{:S(2)}, u32[]{:S(2)}) async-start(bf16[4,288,288]{2,1,0:T(8,128)(2,1)} %shard_map.88), calls=%async_computation.2 | async-start | bytes 1769472 | tf_op jit(solution)/shard_map/all_to_all | solution.py:397
  93.0 8.0 %shard_map.89 = (bf16[512,384]{1,0:T(8,128)(2,1)}, bf16[512,384]{1,0:T(8,128)(2,1)}, bf16[512,384]{1,0:T(8,128)(2,1)}, bf16[512,384]{1,0:T(8,128)(2,1)}, bf16[51...) custom-call(bf16[4,64,1152]{2,1,0:T(8,128)(2,1)} %copy-done.2, ...), custom_call_target="tpu_custom_call" | custom-call | flops 1358954496 | bytes 12000000 | tf_op jit(solution)/shard_map/pallas_call | solution.py:401
  101.1 3.3 %shard_map.90 = bf16[8,36,1152]{2,1,0:T(8,128)(2,1)} custom-call(bf16[4,64,1152]{2,1,0:T(8,128)(2,1)} %copy-done.2, bf16[4,64,1152]{2,1,0:T(8,128)(2,1)} %copy-done.6, bf16[4,64,1152]{2,1,0:T(8,128)(2,1)} %collective-permute-done.1.refs_2_, bf16[4,64,1152]{2,1,0:T(8,128)(2,1)} %copy-done.7, bf16[512,384]{1,0:T(8,128)(2,1)} %get-tuple-element.27.refs_4_), custom_call_target="tpu_custom_call" | custom-call | flops 339738624 | bytes 2000000 | tf_op jit(solution)/shard_map/pallas_call | solution.py:410
  104.4 7.3 %all-to-all-start.3 = ((bf16[8,36,1152]{2,1,0:T(8,128)(2,1)}), bf16[8,36,1152]{2,1,0:T(8,128)(2,1)S(1)}, u32[]{:S(2)}, u32[]{:S(2)}) async-start(bf16[8,36,1152]{2,1,0:T(8,128)(2,1)} %shard_map.90), calls=%async_computation.3 | async-start | bytes 1474560 | tf_op jit(solution)/shard_map/all_to_all | solution.py:421
  111.7 12.0 %shard_map.91 = (f32[2,4,32,1152]{3,2,1,0:T(8,128)}, bf16[2,4,32,1152]{3,2,1,0:T(8,128)(2,1)}) custom-call(bf16[4,64,1152]{2,1,0:T(8,128)(2,1)} %copy-done.2, bf16[4,64,1152]{2,1,0:T(8,128)(2,1)} %copy-done.6, bf16[4,64,1152]{2,1,0:T(8,128)(2,1)} %collective-permute-done.1.refs_2_, bf16[4,64,1152]{2,1,0:T(8,128)(2,1)} %copy-done.7, ...), custom_call_target="tpu_custom_call" | custom-call | flops 1358954496 | bytes 14000000 | tf_op jit(solution)/shard_map/pallas_call | solution.py:423
  123.6 1.9 collective-permute-start.6
  125.6 2.2 %collective-permute-done.6 = bf16[2,4,32,1152]{3,2,1,0:T(8,128)(2,1)S(1)} collective-permute-done((bf16[2,4,32,1152]{3,2,1,0:T(8,128)(2,1)}, bf16[2,4,32,1152]{3,2,1,0:T(8,128)(2,1)S(1)}, u32[]{:S(2)}, u32[]{:S(2)}) %collective-permute-start.6) | collective-permute-done | bytes 589856 | tf_op jit(solution)/shard_map/ppermute | solution.py:373
  127.7 1.2 fusion.3
  129.0 2.0 collective-permute-start.7
  131.1 10.2 %all_to_all.40 = bf16[4,9,1152]{2,1,0:T(8,128)(2,1)S(1)} all-to-all(bf16[4,9,1152]{2,1,0:T(8,128)(2,1)S(1)} %reshape.598), channel_id=1, replica_groups=mesh['yh'=2,'yl'=2,'zh'=4,'c'=2,'zl'=4,'x'=4] {'zl'}, dimensions={0} | all-to-all | bytes 165888 | tf_op jit(solution)/shard_map/all_to_all | solution.py:449
  142.2 4.2 %all-to-all-start.5 = ((bf16[8,9,1152]{2,1,0:T(8,128)(2,1)}), bf16[8,9,1152]{2,1,0:T(8,128)(2,1)S(1)}, u32[]{:S(2)}, u32[]{:S(2)}) async-start(bf16[8,9,1152]{2,1,0:T(8,128)(2,1)} %broadcast_in_dim.35), calls=%async_computation.5 | async-start | bytes 589824 | tf_op jit(solution)/shard_map/all_to_all | solution.py:452
  146.4 7.3 %all-to-all-done.5 = bf16[8,9,1152]{2,1,0:T(8,128)(2,1)S(1)} async-done(((bf16[8,9,1152]{2,1,0:T(8,128)(2,1)}), bf16[8,9,1152]{2,1,0:T(8,128)(2,1)S(1)}, u32[]{:S(2)}, u32[]{:S(2)}) %all-to-all-start.5) | async-done | bytes 165920 | tf_op jit(solution)/shard_map/all_to_all | solution.py:452
  153.7 34.7 %all_to_all.41.back_ref = bf16[4,48,1152]{2,1,0:T(8,128)(2,1)S(1)} all-to-all(bf16[4,48,1152]{2,1,0:T(8,128)(2,1)S(1)} %fusion.2), channel_id=1, replica_groups=mesh['yh'=2,'yl'=2,'zh'=4,'c'=2,'zl'=4,'x'=4] {'zh'}, dimensions={0} | all-to-all | bytes 884736 | tf_op jit(solution)/shard_map/all_to_all | solution.py:379
  189.2 3.7 %all-to-all-start.7 = ((bf16[4,9,1152]{2,1,0:T(8,128)(2,1)}), bf16[4,9,1152]{2,1,0:T(8,128)(2,1)S(1)}, u32[]{:S(2)}, u32[]{:S(2)}) async-start(bf16[4,9,1152]{2,1,0:T(8,128)(2,1)} %broadcast_in_dim.37), calls=%async_computation.7 | async-start | bytes 294912 | tf_op jit(solution)/shard_map/all_to_all | solution.py:466
  192.9 2.7 %shard_map.92 = bf16[128,1152]{1,0:T(8,128)(2,1)} custom-call(f32[2]{0:T(128)} %pad_maximum_fusion.4.power_ref, s32[1]{0:T(128)} %bitcast.2.x_ref, bf16[128,1152]{1,0:T(8,128)(2,1)} %bitcast.33, bf16[128,1152]{1,0:T(8,128)(2,1)} %bitcast.35, f32[3,1152]{1,0:T(4,128)} %bitcast.39, bf16[4,48,1152]{2,1,0:T(8,128)(2,1)} %copy-done.9), custom_call_target="tpu_custom_call" | custom-call | flops 4423680 | bytes 1179648 | tf_op jit(solution)/shard_map/pallas_call | solution.py:456
  195.6 3.2 %all-to-all-done.7 = bf16[4,9,1152]{2,1,0:T(8,128)(2,1)S(1)} async-done(((bf16[4,9,1152]{2,1,0:T(8,128)(2,1)}), bf16[4,9,1152]{2,1,0:T(8,128)(2,1)S(1)}, u32[]{:S(2)}, u32[]{:S(2)}) %all-to-all-start.7) | async-done | bytes 82976 | tf_op jit(solution)/shard_map/all_to_all | solution.py:466
  (64 shorter events, 8.5 us)
Async XLA Ops:
  0.6 8.7 %copy-start = (f32[1,2,3,1152]{3,1,2,0:T(2,128)S(1)}, f32[1,2,3,1152]{3,1,2,0:T(2,128)}, u32[]{:S(2)}) copy-start(f32[1,2,3,1152]{3,1,2,0:T(2,128)} %param.9) | copy-start | bytes 82948
  0.7 9.4 %copy-start.11 = (f32[2,72]{1,0:T(2,128)S(1)}, f32[2,72]{1,0:T(2,128)}, u32[]{:S(2)}) copy-start(f32[2,72]{1,0:T(2,128)} %param.13) | copy-start | bytes 1732
  2.8 23.4 %all-to-all-start = ((bf16[4,72,1152]{2,1,0:T(8,128)(2,1)}), bf16[4,72,1152]{2,1,0:T(8,128)(2,1)S(1)}, u32[]{:S(2)}, u32[]{:S(2)}) async-start(bf16[4,72,1152]{2,1,0:T(8,128)(2,1)} %shard_map.87), calls=%async_computation | async-start | bytes 1327104 | tf_op jit(solution)/shard_map/all_to_all | solution.py:357
  26.2 48.4 %copy-start.1 = (bf16[4,72,1152]{2,1,0:T(8,128)(2,1)}, bf16[4,72,1152]{2,1,0:T(8,128)(2,1)S(1)}, u32[]{:S(2)}) copy-start(bf16[4,72,1152]{2,1,0:T(8,128)(2,1)S(1)} %all-to-all-done) | copy-start | bytes 1990660
  26.2 43.5 %all-to-all-start.1 = ((bf16[4,64,1152]{2,1,0:T(8,128)(2,1)}), bf16[4,64,1152]{2,1,0:T(8,128)(2,1)S(1)}, u32[]{:S(2)}, u32[]{:S(2)}) async-start(bf16[4,64,1152]{2,1,0:T(8,128)(2,1)} %shard_map.86), calls=%async_computation.1 | async-start | bytes 1179648 | tf_op jit(solution)/shard_map/all_to_all | solution.py:379
  39.1 33.3 %collective-permute-start.4 = (bf16[288,1152]{1,0:T(8,128)(2,1)S(1)}, bf16[288,1152]{1,0:T(8,128)(2,1)S(1)}, u32[]{:S(2)}, u32[]{:S(2)}) collective-permute-start(bf16[288,1152]{1,0:T(8,128)(2,1)S(1)} %bitcast.26), channel_id=1, source_target_pairs={{0,1},{1,2},{2,3},{3,0},{4,5},{5,6},{6,7},{7,4},{8,9},{9,10},{10,1... | collective-permute-start | bytes 1990664 | tf_op jit(solution)/shard_map/ppermute | solution.py:359
  42.5 30.5 %collective-permute-start.3 = (bf16[288,1152]{1,0:T(8,128)(2,1)S(1)}, bf16[288,1152]{1,0:T(8,128)(2,1)S(1)}, u32[]{:S(2)}, u32[]{:S(2)}) collective-permute-start(bf16[288,1152]{1,0:T(8,128)(2,1)S(1)} %bitcast.27), channel_id=1, source_target_pairs={{0,2},{1,3},{2,0},{3,1},{4,6},{5,7},{6,4},{7,5},{8,10},{9,11},{10,... | collective-permute-start | bytes 1990664 | tf_op jit(solution)/shard_map/ppermute | solution.py:359
  47.2 27.4 %collective-permute-start.2 = (bf16[288,1152]{1,0:T(8,128)(2,1)S(1)}, bf16[288,1152]{1,0:T(8,128)(2,1)S(1)}, u32[]{:S(2)}, u32[]{:S(2)}) collective-permute-start(bf16[288,1152]{1,0:T(8,128)(2,1)S(1)} %bitcast.28), channel_id=1, source_target_pairs={{0,3},{1,0},{2,1},{3,2},{4,7},{5,4},{6,5},{7,6},{8,11},{9,8},{10,9... | collective-permute-start | bytes 1990664 | tf_op jit(solution)/shard_map/ppermute | solution.py:359
  69.7 8.3 %copy-start.2 = (bf16[4,64,1152]{2,1,0:T(8,128)(2,1)}, bf16[4,64,1152]{2,1,0:T(8,128)(2,1)S(1)}, u32[]{:S(2)}) copy-start(bf16[4,64,1152]{2,1,0:T(8,128)(2,1)S(1)} %all-to-all-done.1.refs_0_) | copy-start | bytes 1769476
  69.7 15.5 %collective-permute-start.1 = (bf16[4,64,1152]{2,1,0:T(8,128)(2,1)S(1)}, bf16[4,64,1152]{2,1,0:T(8,128)(2,1)}, u32[]{:S(2)}, u32[]{:S(2)}) collective-permute-start(bf16[4,64,1152]{2,1,0:T(8,128)(2,1)S(1)} %all-to-all-done.1.refs_0_), channel_id=1, source_target_pairs={{0,128},{128,0},{1,129},{129,1},{2,130},{130,2},{3,131},{131,3},{4... | collective-permute-start | bytes 1769480 | tf_op jit(solution)/shard_map/ppermute | solution.py:376
  72.4 2.2 %copy-start.3 = (bf16[288,1152]{1,0:T(8,128)(2,1)}, bf16[288,1152]{1,0:T(8,128)(2,1)S(1)}, u32[]{:S(2)}) copy-start(bf16[288,1152]{1,0:T(8,128)(2,1)S(1)} %collective-permute-done.4.refs_3_.refs_7_) | copy-start | bytes 1990660
  73.1 1.6 copy-start.4
  74.6 0.8 copy-start.5
  78.1 13.3 %collective-permute-start = (bf16[4,64,1152]{2,1,0:T(8,128)(2,1)S(1)}, bf16[4,64,1152]{2,1,0:T(8,128)(2,1)S(1)}, u32[]{:S(2)}, u32[]{:S(2)}) collective-permute-start(bf16[4,64,1152]{2,1,0:T(8,128)(2,1)S(1)} %all-to-all-done.1.refs_0_), channel_id=1, source_target_pairs={{0,16},{16,0},{1,17},{17,1},{2,18},{18,2},{3,19},{19,3},{4,20},{20... | collective-permute-start | bytes 1769480 | tf_op jit(solution)/shard_map/ppermute | solution.py:373
  85.3 6.1 %collective-permute-start.5 = (bf16[4,64,1152]{2,1,0:T(8,128)(2,1)}, bf16[4,64,1152]{2,1,0:T(8,128)(2,1)S(1)}, u32[]{:S(2)}, u32[]{:S(2)}) collective-permute-start(bf16[4,64,1152]{2,1,0:T(8,128)(2,1)} %collective-permute-done.1.refs_2_), channel_id=1, source_target_pairs={{0,16},{16,0},{1,17},{17,1},{2,18},{18,2},{3,19},{19,3},{4,20},{20... | collective-permute-start | bytes 1769480 | tf_op jit(solution)/shard_map/ppermute | solution.py:373
  87.2 17.2 %all-to-all-start.2 = ((bf16[4,288,288]{2,1,0:T(8,128)(2,1)}), bf16[4,288,288]{2,1,0:T(8,128)(2,1)S(1)}, u32[]{:S(2)}, u32[]{:S(2)}) async-start(bf16[4,288,288]{2,1,0:T(8,128)(2,1)} %shard_map.88), calls=%async_computation.2 | async-start | bytes 1769472 | tf_op jit(solution)/shard_map/all_to_all | solution.py:397
  91.4 0.8 copy-start.6
  92.2 0.8 copy-start.7
  104.4 7.3 %copy-start.8 = (bf16[4,288,288]{2,1,0:T(8,128)(2,1)}, bf16[4,288,288]{2,1,0:T(8,128)(2,1)S(1)}, u32[]{:S(2)}) copy-start(bf16[4,288,288]{2,1,0:T(8,128)(2,1)S(1)} %all-to-all-done.2.refs_8_) | copy-start | bytes 1990660
  104.4 19.2 %all-to-all-start.3 = ((bf16[8,36,1152]{2,1,0:T(8,128)(2,1)}), bf16[8,36,1152]{2,1,0:T(8,128)(2,1)S(1)}, u32[]{:S(2)}, u32[]{:S(2)}) async-start(bf16[8,36,1152]{2,1,0:T(8,128)(2,1)} %shard_map.90), calls=%async_computation.3 | async-start | bytes 1474560 | tf_op jit(solution)/shard_map/all_to_all | solution.py:421
  123.6 4.1 %collective-permute-start.6 = (bf16[2,4,32,1152]{3,2,1,0:T(8,128)(2,1)}, bf16[2,4,32,1152]{3,2,1,0:T(8,128)(2,1)S(1)}, u32[]{:S(2)}, u32[]{:S(2)}) collective-permute-start(bf16[2,4,32,1152]{3,2,1,0:T(8,128)(2,1)} %get-tuple-element.41), channel_id=1, source_target_pairs={{0,16},{16,0},{1,17},{17,1},{2,18},{18,2},{3,19},{19,3},{4,20},{20... | collective-permute-start | bytes 1769480 | tf_op jit(solution)/shard_map/ppermute | solution.py:373
  127.7 13.6 %copy-start.10 = (f32[2,4,32,1152]{3,2,1,0:T(8,128)S(1)}, f32[2,4,32,1152]{3,2,1,0:T(8,128)}, u32[]{:S(2)}) copy-start(f32[2,4,32,1152]{3,2,1,0:T(8,128)} %get-tuple-element.40) | copy-start | bytes 3538948
  129.0 12.3 %collective-permute-start.7 = (bf16[4,32,1152]{2,1,0:T(8,128)(2,1)S(1)}, bf16[4,32,1152]{2,1,0:T(8,128)(2,1)S(1)}, u32[]{:S(2)}, u32[]{:S(2)}) collective-permute-start(bf16[4,32,1152]{2,1,0:T(8,128)(2,1)S(1)} %fusion.3), channel_id=1, source_target_pairs={{0,128},{128,0},{1,129},{129,1},{2,130},{130,2},{3,131},{131,3},{4... | collective-permute-start | bytes 884744 | tf_op jit(solution)/shard_map/ppermute | solution.py:376
  142.2 11.5 %all-to-all-start.5 = ((bf16[8,9,1152]{2,1,0:T(8,128)(2,1)}), bf16[8,9,1152]{2,1,0:T(8,128)(2,1)S(1)}, u32[]{:S(2)}, u32[]{:S(2)}) async-start(bf16[8,9,1152]{2,1,0:T(8,128)(2,1)} %broadcast_in_dim.35), calls=%async_computation.5 | async-start | bytes 589824 | tf_op jit(solution)/shard_map/all_to_all | solution.py:452
  188.4 4.5 %copy-start.9 = (bf16[4,48,1152]{2,1,0:T(8,128)(2,1)}, bf16[4,48,1152]{2,1,0:T(8,128)(2,1)S(1)}, u32[]{:S(2)}) copy-start(bf16[4,48,1152]{2,1,0:T(8,128)(2,1)S(1)} %all_to_all.41.back_ref) | copy-start | bytes 1327108
  189.2 9.7 %all-to-all-start.7 = ((bf16[4,9,1152]{2,1,0:T(8,128)(2,1)}), bf16[4,9,1152]{2,1,0:T(8,128)(2,1)S(1)}, u32[]{:S(2)}, u32[]{:S(2)}) async-start(bf16[4,9,1152]{2,1,0:T(8,128)(2,1)} %broadcast_in_dim.37), calls=%async_computation.7 | async-start | bytes 294912 | tf_op jit(solution)/shard_map/all_to_all | solution.py:466

commit v5 on v4

--- a/solution.py
+++ b/solution.py
@@ -13,6 +13,7 @@
 HD = 72
 PART = 288
 WIDE = 384
+SPAN = 896
 HEADS = 4
 ZS = 4
 TOK = 32
@@ -184,7 +185,7 @@
 
 def fetch_weights(block_refs, w_ref, sem):
     copies = [
-        pltpu.make_async_copy(ref, w_ref.at[pl.ds(PART * step, PART), :], sem.at[step])
+        pltpu.make_async_copy(ref.at[:, pl.ds(0, SPAN)], w_ref.at[pl.ds(PART * step, PART), :], sem.at[step])
         for step, ref in enumerate(block_refs)
     ]
     for copy in copies:
@@ -201,7 +202,7 @@
 
 
 def chip_forward(*refs):
-    row_refs, block_refs, (tab_ref, q_ref, k_ref, v_ref, qh_ref, kh_ref, qf_ref, kf_ref, att_ref, w_ref, sem) = (
+    row_refs, block_refs, (tab_ref, q_ref, k_ref, v_ref, qh_ref, kh_ref, qf_ref, kf_ref, part_ref, att_ref, w_ref, sem) = (
         refs[:4], refs[4:8], refs[8:]
     )
     copies = fetch_weights(block_refs, w_ref, sem)
@@ -209,7 +210,7 @@
     members = head_members()
     for copy in copies:
         copy.wait()
-    packed = nn(modded, w_ref[:, : 7 * 128])
+    packed = nn(modded, w_ref[...])
     for place, (raw_ref, hat_ref, factor_ref) in enumerate(((q_ref, qh_ref, qf_ref), (k_ref, kh_ref, kf_ref))):
         raw = widen(packed[:, place * PART : (place + 1) * PART])
         raw_ref[...] = raw.astype(BF16)
@@ -234,9 +235,6 @@
             found = nn(probs, v_ref[rows, start:end]).astype(BF16)
             att_ref[rows, start:end] = jnp.where(mask, found, att_ref[rows, start:end])
 
-
-def chip_term(*refs):
-    row_refs, (att_ref, part_ref) = refs[:4], refs[4:]
     total = tn(att_ref[...], gather_rows(row_refs, TOK))
     for piece in range(8):
         part_ref[piece] = total[36 * piece : 36 * (piece + 1)].astype(BF16)
@@ -272,7 +270,7 @@
             dv_ref[rows, start:end] = jnp.where(mask, d_value, dv_ref[rows, start:end])
             dqh_ref[rows, start:end] = jnp.where(mask, d_q, dqh_ref[rows, start:end])
             dkh_ref[rows, start:end] = jnp.where(mask, d_k, dkh_ref[rows, start:end])
-    dqkv_ref[:, 3 * PART :] = jnp.zeros((ALL, 7 * 128 - 3 * PART), F32)
+    dqkv_ref[:, 3 * PART :] = jnp.zeros((ALL, SPAN - 3 * PART), F32)
     dqkv_ref[:, 2 * PART : 3 * PART] = dv_ref[:, :PART]
     for place, (raw_ref, factor_ref, turned_ref) in enumerate(
         ((q_ref, qf_ref, dqh_ref), (k_ref, kf_ref, dkh_ref))
@@ -295,7 +293,7 @@
         dqkv_ref[:, place * PART : (place + 1) * PART] = (wide * scaled - raw * pulled)[:, :PART]
     for copy in copies:
         copy.wait()
-    total = nt(dqkv_ref[...].astype(BF16), w_ref[:, : 7 * 128])
+    total = nt(dqkv_ref[...].astype(BF16), w_ref[...])
     for half in range(2):
         for device in range(4):
             first = half * BLOCK + device * ZS * 16
@@ -398,24 +396,15 @@
 
     wide = jax.ShapeDtypeStruct((ALL, WIDE), BF16)
     factors = jax.ShapeDtypeStruct((ALL, 128), F32)
-    *kept, attended = pl.pallas_call(
+    *kept, part = pl.pallas_call(
         chip_forward,
-        out_shape=[wide] * 5 + [factors] * 2 + [wide],
+        out_shape=[wide] * 5 + [factors] * 2 + [jax.ShapeDtypeStruct((8, 36, D), BF16)],
         in_specs=[vmem] * 4 + [hbm] * 4 + [vmem],
         out_specs=[vmem] * 8,
-        scratch_shapes=[pltpu.VMEM((D, D), BF16), four],
-        compiler_params=PARAMS,
-        cost_estimate=cost(2 * ALL * D * 4 * PART, 12 * 10**6),
+        scratch_shapes=[pltpu.VMEM((ALL, WIDE), BF16), pltpu.VMEM((D, SPAN), BF16), four],
+        compiler_params=PARAMS,
+        cost_estimate=cost(2 * ALL * D * 5 * PART, 12 * 10**6),
     )(*arrays, *blocks, tables)
-    part = pl.pallas_call(
-        chip_term,
-        out_shape=jax.ShapeDtypeStruct((8, 36, D), BF16),
-        in_specs=[vmem] * 5,
-        out_specs=vmem,
-        compiler_params=PARAMS,
-        cost_estimate=cost(2 * ALL * D * PART, 2 * 10**6),
-    )(*arrays, attended)
-
     w_back, part = lax.optimization_barrier((w_back, part))
 
     plane = lax.all_to_all(part, ("yh", "x"), 0, 0, tiled=True)
@@ -430,9 +419,9 @@
             pltpu.VMEM((ALL, WIDE), F32),
             pltpu.VMEM((ALL, WIDE), F32),
             pltpu.VMEM((ALL, WIDE), F32),
-            pltpu.VMEM((ALL, 7 * 128), F32),
+            pltpu.VMEM((ALL, SPAN), F32),
             pltpu.VMEM((PART, D), F32),
-            pltpu.VMEM((D, D), BF16),
+            pltpu.VMEM((D, SPAN), BF16),
             four,
         ],
         compiler_params=PARAMS,
@@ -449,9 +438,10 @@
     levels = lax.all_to_all(plane, "zl", 0, 0, tiled=True)
     level = jnp.sum(levels.astype(F32), axis=0).astype(BF16)
     level, summed = lax.optimization_barrier((level, summed))
-    spread = lax.all_to_all(jnp.broadcast_to(level[None], (8, 9, D)), ("c", "x"), 0, 0, tiled=True)
-    wanted = lax.dynamic_index_in_dim(spread.reshape(4, 2, 9, D), core, 1, keepdims=False)
-    joined = jnp.concatenate([summed, jnp.pad(wanted, ((0, 0), (0, 7), (0, 0)))], axis=1)
+    quarters = jnp.broadcast_to(jnp.pad(level, ((0, 3), (0, 0))).reshape(1, 4, 3, D), (2, 4, 3, D)).reshape(8, 3, D)
+    spread = lax.all_to_all(quarters, ("c", "x"), 0, 0, tiled=True)
+    wanted = lax.dynamic_index_in_dim(spread.reshape(4, 2, 3, D), core, 1, keepdims=False)
+    joined = jnp.concatenate([summed, jnp.pad(wanted, ((0, 0), (0, 5), (0, 0)))], axis=1)
     joined = exchange(joined)
     d_hidden = pl.pallas_call(
         home_backward,
@@ -462,8 +452,9 @@
         compiler_params=PARAMS,
         cost_estimate=cost(30 * ROWS * D, 8 * ROWS * D),
     )(power, x_place, rows, cotangent, mod, joined)
-    share = jnp.sum(joined[:, TOK : TOK + 9].astype(F32), axis=0).astype(BF16)
-    final = lax.all_to_all(jnp.broadcast_to(share[None], (4, 9, D)), "zl", 0, 0, tiled=True).reshape(36, D)
+    share = jnp.sum(joined[:, TOK : TOK + 3].astype(F32), axis=0).astype(BF16)
+    final = lax.all_to_all(jnp.broadcast_to(share[None], (16, 3, D)), CLIP, 0, 0, tiled=True)
+    final = final.reshape(4, 12, D)[:, :9].reshape(36, D)
     return d_hidden[None, None], final.astype(F32) / 32.0
 
 

time: 202 us -> 199 us (0.985)
  blocking collectives: 44.8 us -> 41.4 us
  Pallas kernels: 33.5 us -> 30.6 us
  waiting for transfers between devices: 49.7 us -> 52.1 us
    all_to_all x1, blocking collectives: 34.7 us -> 31.3 us  [exchange(): return lax.all_to_all(values, 'zh', 0, 0, tiled=True)]
    pallas_call x2 -> x1, Pallas kernels: 11.3 us -> 8.47 us  [on_device(): pl.pallas_call(chip_forward, out_shape=[wide] * 5 + [factors] * 2 + [jax....]
  transfers between devices with their start and end apart: 14 -> 14, of which waited for: 8 -> 9; matrix products, arithmetic and copies ran while one was open for 2% -> 2% of each run, Pallas kernels for 16% -> 14%
where the time goes in v5:
time: 199 us; the launch traced here: 198 us
  starting transfers between devices  61.9 us (31%)
  waiting for transfers between devices  52.1 us (26%)
  blocking collectives  41.4 us (21%)
  Pallas kernels  30.6 us (15%)
  local copies, waits for them, and re-layouts  7.6 us (4%)
  other arithmetic  2.39 us (1%)
    all_to_all x1, blocking collectives, exchange(): return lax.all_to_all(values, 'zh', 0, 0, tiled=True)  31.3 us
    all_to_all x1, waiting for transfers between devices, exchange(): return lax.all_to_all(values, 'zh', 0, 0, tiled=True)  19.3 us
    all_to_all x1, starting transfers between devices, exchange(): return lax.all_to_all(values, 'zh', 0, 0, tiled=True)  12.9 us
    pallas_call x1, Pallas kernels, on_device(): pl.pallas_call(chip_backward, out_shape=[jax.ShapeDtypeStruct((2, ZS, TOK...  12 us
    ppermute x3, starting transfers between devices, on_device(): lax.ppermute(block, 'x', [(i, (i + 4 - step) % 4) for i in range(4)])  11.4 us
    all_to_all x1, waiting for transfers between devices, on_device(): block = lax.all_to_all(unit, 'zl', 0, 0, tiled=True).reshape(PART, 4 * PART)  10.4 us
    all_to_all x1, blocking collectives, on_device(): levels = lax.all_to_all(plane, 'zl', 0, 0, tiled=True)  10.1 us
    pallas_call x1, Pallas kernels, on_device(): pl.pallas_call(chip_forward, out_shape=[wide] * 5 + [factors] * 2 + [jax....  8.47 us
  transfers between devices with their start and end apart: 14, of which 9 were waited for; matrix products, arithmetic and copies ran while one was open for 2% of the time, Pallas kernels for 14%

profile of v5, /device:TPU:24, one launch (start us, length us, event | category | flops | bytes accessed | tf_op | source)
XLA Modules:
  0.0 197.6 jit_solution(11866823851378910125)
XLA Ops:
  0.7 2.2 %shard_map.87 = bf16[4,72,1152]{2,1,0:T(8,128)(2,1)} custom-call(s32[1]{0:T(128)} %bitcast.5.place_ref, bf16[72,3456]{1,0:T(8,128)(2,1)} %w_qkv_ref.1, bf16[72,1152]{1,0:T(8,128)(2,1)} %w_out_ref.1), custom_call_target="tpu_custom_call" | custom-call | flops 1000000 | bytes 2000000 | tf_op jit(solution)/shard_map/pallas_call | solution.py:346
  2.8 5.9 %all-to-all-start = ((bf16[4,72,1152]{2,1,0:T(8,128)(2,1)}), bf16[4,72,1152]{2,1,0:T(8,128)(2,1)S(1)}, u32[]{:S(2)}, u32[]{:S(2)}) async-start(bf16[4,72,1152]{2,1,0:T(8,128)(2,1)} %shard_map.87), calls=%async_computation | async-start | bytes 1327104 | tf_op jit(solution)/shard_map/all_to_all | solution.py:355
  13.1 2.6 %shard_map.86 = bf16[4,64,1152]{2,1,0:T(8,128)(2,1)} custom-call(f32[2]{0:T(128)} %pad_maximum_fusion.4.power_ref, s32[1]{0:T(128)} %bitcast.2.x_ref, bf16[128,1152]{1,0:T(8,128)(2,1)} %bitcast.33, bf16[128,1152]{1,0:T(8,128)(2,1)} %bitcast.35, f32[3,1152]{1,0:T(4,128)} %bitcast.39), custom_call_target="tpu_custom_call" | custom-call | flops 2949120 | bytes 1179648 | tf_op jit(solution)/shard_map/pallas_call | solution.py:360
  15.8 10.4 %all-to-all-done = bf16[4,72,1152]{2,1,0:T(8,128)(2,1)S(1)} async-done(((bf16[4,72,1152]{2,1,0:T(8,128)(2,1)}), bf16[4,72,1152]{2,1,0:T(8,128)(2,1)S(1)}, u32[]{:S(2)}, u32[]{:S(2)}) %all-to-all-start) | async-done | bytes 663584 | tf_op jit(solution)/shard_map/all_to_all | solution.py:355
  26.2 12.9 %all-to-all-start.1 = ((bf16[4,64,1152]{2,1,0:T(8,128)(2,1)}), bf16[4,64,1152]{2,1,0:T(8,128)(2,1)}, u32[]{:S(2)}, u32[]{:S(2)}) async-start(bf16[4,64,1152]{2,1,0:T(8,128)(2,1)} %shard_map.86), calls=%async_computation.1 | async-start | bytes 1179648 | tf_op jit(solution)/shard_map/all_to_all | solution.py:377
  39.1 3.4 %collective-permute-start.4 = (bf16[288,1152]{1,0:T(8,128)(2,1)S(1)}, bf16[288,1152]{1,0:T(8,128)(2,1)S(1)}, u32[]{:S(2)}, u32[]{:S(2)}) collective-permute-start(bf16[288,1152]{1,0:T(8,128)(2,1)S(1)} %bitcast.27), channel_id=1, source_target_pairs={{0,1},{1,2},{2,3},{3,0},{4,5},{5,6},{6,7},{7,4},{8,9},{9,10},{10,1... | collective-permute-start | bytes 1990664 | tf_op jit(solution)/shard_map/ppermute | solution.py:357
  42.5 4.6 %collective-permute-start.3 = (bf16[288,1152]{1,0:T(8,128)(2,1)S(1)}, bf16[288,1152]{1,0:T(8,128)(2,1)S(1)}, u32[]{:S(2)}, u32[]{:S(2)}) collective-permute-start(bf16[288,1152]{1,0:T(8,128)(2,1)S(1)} %bitcast.28), channel_id=1, source_target_pairs={{0,2},{1,3},{2,0},{3,1},{4,6},{5,7},{6,4},{7,5},{8,10},{9,11},{10,... | collective-permute-start | bytes 1990664 | tf_op jit(solution)/shard_map/ppermute | solution.py:357
  47.2 3.3 %collective-permute-start.2 = (bf16[288,1152]{1,0:T(8,128)(2,1)S(1)}, bf16[288,1152]{1,0:T(8,128)(2,1)S(1)}, u32[]{:S(2)}, u32[]{:S(2)}) collective-permute-start(bf16[288,1152]{1,0:T(8,128)(2,1)S(1)} %bitcast.29), channel_id=1, source_target_pairs={{0,3},{1,0},{2,1},{3,2},{4,7},{5,4},{6,5},{7,6},{8,11},{9,8},{10,9... | collective-permute-start | bytes 1990664 | tf_op jit(solution)/shard_map/ppermute | solution.py:357
  50.5 19.3 %all-to-all-done.1.refs_0_ = bf16[4,64,1152]{2,1,0:T(8,128)(2,1)} async-done(((bf16[4,64,1152]{2,1,0:T(8,128)(2,1)}), bf16[4,64,1152]{2,1,0:T(8,128)(2,1)}, u32[]{:S(2)}, u32[]{:S(2)}) %all-to-all-start.1) | async-done | bytes 589856 | tf_op jit(solution)/shard_map/all_to_all | solution.py:377
  69.9 2.6 %collective-permute-start.1 = (bf16[4,64,1152]{2,1,0:T(8,128)(2,1)}, bf16[4,64,1152]{2,1,0:T(8,128)(2,1)S(1)}, u32[]{:S(2)}, u32[]{:S(2)}) collective-permute-start(bf16[4,64,1152]{2,1,0:T(8,128)(2,1)} %all-to-all-done.1.refs_0_), channel_id=1, source_target_pairs={{0,128},{128,0},{1,129},{129,1},{2,130},{130,2},{3,131},{131,3},{4... | collective-permute-start | bytes 1769480 | tf_op jit(solution)/shard_map/ppermute | solution.py:374
  73.1 1.5 collective-permute-done.2.refs_1_.refs_5_
  74.6 0.8 copy-done.5
  75.5 2.6 %shard_map.88 = bf16[4,288,288]{2,1,0:T(8,128)(2,1)} custom-call(s32[1]{0:T(128)} %bitcast.2.x_ref, bf16[288,1152]{1,0:T(8,128)(2,1)} %bitcast.30, bf16[288,1152]{1,0:T(8,128)(2,1)} %copy-done.5, bf16[288,1152]{1,0:T(8,128)(2,1)} %copy-done.4, bf16[288,1152]{1,0:T(8,128)(2,1)} %copy-done.3), custom_call_target="tpu_custom_call" | custom-call | flops 1000000 | bytes 2000000 | tf_op jit(solution)/shard_map/pallas_call | solution.py:384
  78.1 1.9 collective-permute-start
  80.0 5.5 %collective-permute-done.1.refs_2_ = bf16[4,64,1152]{2,1,0:T(8,128)(2,1)S(1)} collective-permute-done((bf16[4,64,1152]{2,1,0:T(8,128)(2,1)}, bf16[4,64,1152]{2,1,0:T(8,128)(2,1)S(1)}, u32[]{:S(2)}, u32[]{:S(2)}) %collective-permute-start.1) | collective-permute-done | bytes 589856 | tf_op jit(solution)/shard_map/ppermute | solution.py:374
  85.5 1.9 collective-permute-start.5
  87.4 4.2 %all-to-all-start.2 = ((bf16[4,288,288]{2,1,0:T(8,128)(2,1)}), bf16[4,288,288]{2,1,0:T(8,128)(2,1)S(1)}, u32[]{:S(2)}, u32[]{:S(2)}) async-start(bf16[4,288,288]{2,1,0:T(8,128)(2,1)} %shard_map.88), calls=%async_computation.2 | async-start | bytes 1769472 | tf_op jit(solution)/shard_map/all_to_all | solution.py:395
  93.3 8.5 %shard_map.89 = (bf16[512,384]{1,0:T(8,128)(2,1)}, bf16[512,384]{1,0:T(8,128)(2,1)}, bf16[512,384]{1,0:T(8,128)(2,1)}, bf16[512,384]{1,0:T(8,128)(2,1)}, bf16[51...) custom-call(bf16[4,64,1152]{2,1,0:T(8,128)(2,1)} %all-to-all-done.1.refs_0_, ...), custom_call_target="tpu_custom_call" | custom-call | flops 1698693120 | bytes 12000000 | tf_op jit(solution)/shard_map/pallas_call | solution.py:399
  101.7 0.9 all-to-all-done.2.refs_8_
  102.7 7.3 %all-to-all-start.3 = ((bf16[8,36,1152]{2,1,0:T(8,128)(2,1)}), bf16[8,36,1152]{2,1,0:T(8,128)(2,1)S(1)}, u32[]{:S(2)}, u32[]{:S(2)}) async-start(bf16[8,36,1152]{2,1,0:T(8,128)(2,1)} %get-tuple-element.38), calls=%async_computation.3 | async-start | bytes 1474560 | tf_op jit(solution)/shard_map/all_to_all | solution.py:410
  109.9 12.0 %shard_map.90 = (f32[2,4,32,1152]{3,2,1,0:T(8,128)}, bf16[2,4,32,1152]{3,2,1,0:T(8,128)(2,1)}) custom-call(bf16[4,64,1152]{2,1,0:T(8,128)(2,1)} %all-to-all-done.1.refs_0_, bf16[4,64,1152]{2,1,0:T(8,128)(2,1)} %copy-done.9, bf16[4,64,1152]{2,1,0:T(8,128)(2,1)} %copy-done.8, bf16[4,64,1152]{2,1,0:T(8,128)(2,1)} %copy-done.10, bf16[288,1152]{1,0:T(8,128)(2,1)} %bitcast.32, ...), custom_call_target="tpu_custom_call" | custom-call | flops 1358954496 | bytes 14000000 | tf_op jit(solution)/shard_map/pallas_call | solution.py:412
  121.9 1.9 collective-permute-start.6
  123.8 2.2 %collective-permute-done.6 = bf16[2,4,32,1152]{3,2,1,0:T(8,128)(2,1)S(1)} collective-permute-done((bf16[2,4,32,1152]{3,2,1,0:T(8,128)(2,1)}, bf16[2,4,32,1152]{3,2,1,0:T(8,128)(2,1)S(1)}, u32[]{:S(2)}, u32[]{:S(2)}) %collective-permute-start.6) | collective-permute-done | bytes 589856 | tf_op jit(solution)/shard_map/ppermute | solution.py:371
  126.0 1.2 fusion.3
  127.2 3.6 %collective-permute-start.7 = (bf16[4,32,1152]{2,1,0:T(8,128)(2,1)S(1)}, bf16[4,32,1152]{2,1,0:T(8,128)(2,1)S(1)}, u32[]{:S(2)}, u32[]{:S(2)}) collective-permute-start(bf16[4,32,1152]{2,1,0:T(8,128)(2,1)S(1)} %fusion.3), channel_id=1, source_target_pairs={{0,128},{128,0},{1,129},{129,1},{2,130},{130,2},{3,131},{131,3},{4... | collective-permute-start | bytes 884744 | tf_op jit(solution)/shard_map/ppermute | solution.py:374
  131.0 10.1 %all_to_all.40 = bf16[4,9,1152]{2,1,0:T(8,128)(2,1)S(1)} all-to-all(bf16[4,9,1152]{2,1,0:T(8,128)(2,1)S(1)} %reshape.605), channel_id=1, replica_groups=mesh['yh'=2,'yl'=2,'zh'=4,'c'=2,'zl'=4,'x'=4] {'zl'}, dimensions={0} | all-to-all | bytes 165888 | tf_op jit(solution)/shard_map/all_to_all | solution.py:438
  141.9 4.3 %all-to-all-start.5 = ((bf16[8,3,1152]{2,1,0:T(4,128)(2,1)}), bf16[8,3,1152]{2,1,0:T(4,128)(2,1)S(1)}, u32[]{:S(2)}, u32[]{:S(2)}) async-start(bf16[8,3,1152]{2,1,0:T(4,128)(2,1)} %bitcast.11), calls=%async_computation.5 | async-start | bytes 147456 | tf_op jit(solution)/shard_map/all_to_all | solution.py:442
  146.2 5.4 %all-to-all-done.5 = bf16[8,3,1152]{2,1,0:T(4,128)(2,1)S(1)} async-done(((bf16[8,3,1152]{2,1,0:T(4,128)(2,1)}), bf16[8,3,1152]{2,1,0:T(4,128)(2,1)S(1)}, u32[]{:S(2)}, u32[]{:S(2)}) %all-to-all-start.5) | async-done | bytes 55328 | tf_op jit(solution)/shard_map/all_to_all | solution.py:442
  151.6 31.3 %all_to_all.41.back_ref = bf16[4,40,1152]{2,1,0:T(8,128)(2,1)S(1)} all-to-all(bf16[4,40,1152]{2,1,0:T(8,128)(2,1)S(1)} %fusion.2), channel_id=1, replica_groups=mesh['yh'=2,'yl'=2,'zh'=4,'c'=2,'zl'=4,'x'=4] {'zh'}, dimensions={0} | all-to-all | bytes 737280 | tf_op jit(solution)/shard_map/all_to_all | solution.py:377
  183.7 4.0 %all-to-all-start.7 = ((bf16[16,3,1152]{2,1,0:T(4,128)(2,1)}), bf16[16,3,1152]{2,1,0:T(4,128)(2,1)S(1)}, u32[]{:S(2)}, u32[]{:S(2)}) async-start(bf16[16,3,1152]{2,1,0:T(4,128)(2,1)} %broadcast_in_dim.39), calls=%async_computation.7 | async-start | bytes 294912 | tf_op jit(solution)/shard_map/all_to_all | solution.py:456
  187.7 2.7 %shard_map.91 = bf16[128,1152]{1,0:T(8,128)(2,1)} custom-call(f32[2]{0:T(128)} %pad_maximum_fusion.4.power_ref, s32[1]{0:T(128)} %bitcast.2.x_ref, bf16[128,1152]{1,0:T(8,128)(2,1)} %bitcast.34, bf16[128,1152]{1,0:T(8,128)(2,1)} %bitcast.36, f32[3,1152]{1,0:T(4,128)} %bitcast.40, bf16[4,40,1152]{2,1,0:T(8,128)(2,1)} %copy-done.6), custom_call_target="tpu_custom_call" | custom-call | flops 4423680 | bytes 1179648 | tf_op jit(solution)/shard_map/pallas_call | solution.py:446
  190.4 6.3 %all-to-all-done.7 = bf16[16,3,1152]{2,1,0:T(4,128)(2,1)S(1)} async-done(((bf16[16,3,1152]{2,1,0:T(4,128)(2,1)}), bf16[16,3,1152]{2,1,0:T(4,128)(2,1)S(1)}, u32[]{:S(2)}, u32[]{:S(2)}) %all-to-all-start.7) | async-done | bytes 110624 | tf_op jit(solution)/shard_map/all_to_all | solution.py:456
  (66 shorter events, 8.5 us)
Async XLA Ops:
  0.6 8.7 %copy-start = (f32[1,2,3,1152]{3,1,2,0:T(2,128)S(1)}, f32[1,2,3,1152]{3,1,2,0:T(2,128)}, u32[]{:S(2)}) copy-start(f32[1,2,3,1152]{3,1,2,0:T(2,128)} %param.9) | copy-start | bytes 82948
  0.7 9.4 %copy-start.11 = (f32[2,72]{1,0:T(2,128)S(1)}, f32[2,72]{1,0:T(2,128)}, u32[]{:S(2)}) copy-start(f32[2,72]{1,0:T(2,128)} %param.13) | copy-start | bytes 1732
  2.8 23.4 %all-to-all-start = ((bf16[4,72,1152]{2,1,0:T(8,128)(2,1)}), bf16[4,72,1152]{2,1,0:T(8,128)(2,1)S(1)}, u32[]{:S(2)}, u32[]{:S(2)}) async-start(bf16[4,72,1152]{2,1,0:T(8,128)(2,1)} %shard_map.87), calls=%async_computation | async-start | bytes 1327104 | tf_op jit(solution)/shard_map/all_to_all | solution.py:355
  26.2 48.4 %copy-start.1 = (bf16[4,72,1152]{2,1,0:T(8,128)(2,1)}, bf16[4,72,1152]{2,1,0:T(8,128)(2,1)S(1)}, u32[]{:S(2)}) copy-start(bf16[4,72,1152]{2,1,0:T(8,128)(2,1)S(1)} %all-to-all-done) | copy-start | bytes 1990660
  26.2 43.6 %all-to-all-start.1 = ((bf16[4,64,1152]{2,1,0:T(8,128)(2,1)}), bf16[4,64,1152]{2,1,0:T(8,128)(2,1)}, u32[]{:S(2)}, u32[]{:S(2)}) async-start(bf16[4,64,1152]{2,1,0:T(8,128)(2,1)} %shard_map.86), calls=%async_computation.1 | async-start | bytes 1179648 | tf_op jit(solution)/shard_map/all_to_all | solution.py:377
  39.1 33.4 %collective-permute-start.4 = (bf16[288,1152]{1,0:T(8,128)(2,1)S(1)}, bf16[288,1152]{1,0:T(8,128)(2,1)S(1)}, u32[]{:S(2)}, u32[]{:S(2)}) collective-permute-start(bf16[288,1152]{1,0:T(8,128)(2,1)S(1)} %bitcast.27), channel_id=1, source_target_pairs={{0,1},{1,2},{2,3},{3,0},{4,5},{5,6},{6,7},{7,4},{8,9},{9,10},{10,1... | collective-permute-start | bytes 1990664 | tf_op jit(solution)/shard_map/ppermute | solution.py:357
  42.5 30.5 %collective-permute-start.3 = (bf16[288,1152]{1,0:T(8,128)(2,1)S(1)}, bf16[288,1152]{1,0:T(8,128)(2,1)S(1)}, u32[]{:S(2)}, u32[]{:S(2)}) collective-permute-start(bf16[288,1152]{1,0:T(8,128)(2,1)S(1)} %bitcast.28), channel_id=1, source_target_pairs={{0,2},{1,3},{2,0},{3,1},{4,6},{5,7},{6,4},{7,5},{8,10},{9,11},{10,... | collective-permute-start | bytes 1990664 | tf_op jit(solution)/shard_map/ppermute | solution.py:357
  47.2 27.4 %collective-permute-start.2 = (bf16[288,1152]{1,0:T(8,128)(2,1)S(1)}, bf16[288,1152]{1,0:T(8,128)(2,1)S(1)}, u32[]{:S(2)}, u32[]{:S(2)}) collective-permute-start(bf16[288,1152]{1,0:T(8,128)(2,1)S(1)} %bitcast.29), channel_id=1, source_target_pairs={{0,3},{1,0},{2,1},{3,2},{4,7},{5,4},{6,5},{7,6},{8,11},{9,8},{10,9... | collective-permute-start | bytes 1990664 | tf_op jit(solution)/shard_map/ppermute | solution.py:357
  69.9 15.6 %collective-permute-start.1 = (bf16[4,64,1152]{2,1,0:T(8,128)(2,1)}, bf16[4,64,1152]{2,1,0:T(8,128)(2,1)S(1)}, u32[]{:S(2)}, u32[]{:S(2)}) collective-permute-start(bf16[4,64,1152]{2,1,0:T(8,128)(2,1)} %all-to-all-done.1.refs_0_), channel_id=1, source_target_pairs={{0,128},{128,0},{1,129},{129,1},{2,130},{130,2},{3,131},{131,3},{4... | collective-permute-start | bytes 1769480 | tf_op jit(solution)/shard_map/ppermute | solution.py:374
  72.5 2.1 %copy-start.3 = (bf16[288,1152]{1,0:T(8,128)(2,1)}, bf16[288,1152]{1,0:T(8,128)(2,1)S(1)}, u32[]{:S(2)}) copy-start(bf16[288,1152]{1,0:T(8,128)(2,1)S(1)} %collective-permute-done.4.refs_3_.refs_7_) | copy-start | bytes 1990660
  73.1 1.6 copy-start.4
  74.6 0.8 copy-start.5
  78.1 13.5 %collective-permute-start = (bf16[4,64,1152]{2,1,0:T(8,128)(2,1)}, bf16[4,64,1152]{2,1,0:T(8,128)(2,1)S(1)}, u32[]{:S(2)}, u32[]{:S(2)}) collective-permute-start(bf16[4,64,1152]{2,1,0:T(8,128)(2,1)} %all-to-all-done.1.refs_0_), channel_id=1, source_target_pairs={{0,16},{16,0},{1,17},{17,1},{2,18},{18,2},{3,19},{19,3},{4,20},{20... | collective-permute-start | bytes 1769480 | tf_op jit(solution)/shard_map/ppermute | solution.py:371
  85.5 6.2 %copy-start.8 = (bf16[4,64,1152]{2,1,0:T(8,128)(2,1)}, bf16[4,64,1152]{2,1,0:T(8,128)(2,1)S(1)}, u32[]{:S(2)}) copy-start(bf16[4,64,1152]{2,1,0:T(8,128)(2,1)S(1)} %collective-permute-done.1.refs_2_) | copy-start | bytes 1769476
  85.5 6.1 %collective-permute-start.5 = (bf16[4,64,1152]{2,1,0:T(8,128)(2,1)S(1)}, bf16[4,64,1152]{2,1,0:T(8,128)(2,1)S(1)}, u32[]{:S(2)}, u32[]{:S(2)}) collective-permute-start(bf16[4,64,1152]{2,1,0:T(8,128)(2,1)S(1)} %collective-permute-done.1.refs_2_), channel_id=1, source_target_pairs={{0,16},{16,0},{1,17},{17,1},{2,18},{18,2},{3,19},{19,3},{4,20},{20... | collective-permute-start | bytes 1769480 | tf_op jit(solution)/shard_map/ppermute | solution.py:371
  87.4 15.3 %all-to-all-start.2 = ((bf16[4,288,288]{2,1,0:T(8,128)(2,1)}), bf16[4,288,288]{2,1,0:T(8,128)(2,1)S(1)}, u32[]{:S(2)}, u32[]{:S(2)}) async-start(bf16[4,288,288]{2,1,0:T(8,128)(2,1)} %shard_map.88), calls=%async_computation.2 | async-start | bytes 1769472 | tf_op jit(solution)/shard_map/all_to_all | solution.py:395
  91.6 0.8 copy-start.9
  92.5 0.8 copy-start.10
  102.7 7.3 %copy-start.2 = (bf16[4,288,288]{2,1,0:T(8,128)(2,1)}, bf16[4,288,288]{2,1,0:T(8,128)(2,1)S(1)}, u32[]{:S(2)}) copy-start(bf16[4,288,288]{2,1,0:T(8,128)(2,1)S(1)} %all-to-all-done.2.refs_8_) | copy-start | bytes 1990660
  102.7 19.2 %all-to-all-start.3 = ((bf16[8,36,1152]{2,1,0:T(8,128)(2,1)}), bf16[8,36,1152]{2,1,0:T(8,128)(2,1)S(1)}, u32[]{:S(2)}, u32[]{:S(2)}) async-start(bf16[8,36,1152]{2,1,0:T(8,128)(2,1)} %get-tuple-element.38), calls=%async_computation.3 | async-start | bytes 1474560 | tf_op jit(solution)/shard_map/all_to_all | solution.py:410
  121.9 4.1 %collective-permute-start.6 = (bf16[2,4,32,1152]{3,2,1,0:T(8,128)(2,1)}, bf16[2,4,32,1152]{3,2,1,0:T(8,128)(2,1)S(1)}, u32[]{:S(2)}, u32[]{:S(2)}) collective-permute-start(bf16[2,4,32,1152]{3,2,1,0:T(8,128)(2,1)} %get-tuple-element.41), channel_id=1, source_target_pairs={{0,16},{16,0},{1,17},{17,1},{2,18},{18,2},{3,19},{19,3},{4,20},{20... | collective-permute-start | bytes 1769480 | tf_op jit(solution)/shard_map/ppermute | solution.py:371
  126.0 15.1 %copy-start.7 = (f32[2,4,32,1152]{3,2,1,0:T(8,128)S(1)}, f32[2,4,32,1152]{3,2,1,0:T(8,128)}, u32[]{:S(2)}) copy-start(f32[2,4,32,1152]{3,2,1,0:T(8,128)} %get-tuple-element.40) | copy-start | bytes 3538948
  127.2 13.9 %collective-permute-start.7 = (bf16[4,32,1152]{2,1,0:T(8,128)(2,1)S(1)}, bf16[4,32,1152]{2,1,0:T(8,128)(2,1)S(1)}, u32[]{:S(2)}, u32[]{:S(2)}) collective-permute-start(bf16[4,32,1152]{2,1,0:T(8,128)(2,1)S(1)} %fusion.3), channel_id=1, source_target_pairs={{0,128},{128,0},{1,129},{129,1},{2,130},{130,2},{3,131},{131,3},{4... | collective-permute-start | bytes 884744 | tf_op jit(solution)/shard_map/ppermute | solution.py:374
  141.9 9.6 %all-to-all-start.5 = ((bf16[8,3,1152]{2,1,0:T(4,128)(2,1)}), bf16[8,3,1152]{2,1,0:T(4,128)(2,1)S(1)}, u32[]{:S(2)}, u32[]{:S(2)}) async-start(bf16[8,3,1152]{2,1,0:T(4,128)(2,1)} %bitcast.11), calls=%async_computation.5 | async-start | bytes 147456 | tf_op jit(solution)/shard_map/all_to_all | solution.py:442
  182.9 4.8 %copy-start.6 = (bf16[4,40,1152]{2,1,0:T(8,128)(2,1)}, bf16[4,40,1152]{2,1,0:T(8,128)(2,1)S(1)}, u32[]{:S(2)}) copy-start(bf16[4,40,1152]{2,1,0:T(8,128)(2,1)S(1)} %all_to_all.41.back_ref) | copy-start | bytes 1105924
  183.7 13.0 %all-to-all-start.7 = ((bf16[16,3,1152]{2,1,0:T(4,128)(2,1)}), bf16[16,3,1152]{2,1,0:T(4,128)(2,1)S(1)}, u32[]{:S(2)}, u32[]{:S(2)}) async-start(bf16[16,3,1152]{2,1,0:T(4,128)(2,1)} %broadcast_in_dim.39), calls=%async_computation.7 | async-start | bytes 294912 | tf_op jit(solution)/shard_map/all_to_all | solution.py:456

commit v6 on v5

--- a/solution.py
+++ b/solution.py
@@ -25,6 +25,9 @@
 EPS = 1e-06
 TEMPER = HD ** (-0.5)
 PARAMS = pltpu.CompilerParams(vmem_limit_bytes=56 * 1024 * 1024)
+
+
+SMALL = pltpu.CompilerParams(vmem_limit_bytes=24 * 1024 * 1024)
 
 
 def cost(flops, nbytes):
@@ -363,7 +366,7 @@
         in_specs=[smem, smem, vmem, vmem, vmem],
         out_specs=vmem,
         scratch_shapes=[pltpu.VMEM((ROWS, D), F32)],
-        compiler_params=PARAMS,
+        compiler_params=SMALL,
         cost_estimate=cost(20 * ROWS * D, 8 * ROWS * D),
     )(power, x_place, rows, cotangent, mod)
 
@@ -432,12 +435,12 @@
     plane = plane.reshape(4, 9, D)
     arrived = other_core(theirs)
     across = (mine[1] + arrived[1].astype(F32)).astype(BF16)
+
+    levels = lax.all_to_all(plane, "zl", 0, 0, tiled=True)
+    across, levels = lax.optimization_barrier((across, levels))
     from_y = other_y(across)
     summed = (mine[0] + arrived[0].astype(F32) + from_y.astype(F32)).astype(BF16)
-
-    levels = lax.all_to_all(plane, "zl", 0, 0, tiled=True)
     level = jnp.sum(levels.astype(F32), axis=0).astype(BF16)
-    level, summed = lax.optimization_barrier((level, summed))
     quarters = jnp.broadcast_to(jnp.pad(level, ((0, 3), (0, 0))).reshape(1, 4, 3, D), (2, 4, 3, D)).reshape(8, 3, D)
     spread = lax.all_to_all(quarters, ("c", "x"), 0, 0, tiled=True)
     wanted = lax.dynamic_index_in_dim(spread.reshape(4, 2, 3, D), core, 1, keepdims=False)
@@ -449,7 +452,7 @@
         in_specs=[smem, smem, vmem, vmem, vmem, vmem],
         out_specs=vmem,
         scratch_shapes=[pltpu.VMEM((ROWS, D), F32)],
-        compiler_params=PARAMS,
+        compiler_params=SMALL,
         cost_estimate=cost(30 * ROWS * D, 8 * ROWS * D),
     )(power, x_place, rows, cotangent, mod, joined)
     share = jnp.sum(joined[:, TOK : TOK + 3].astype(F32), axis=0).astype(BF16)

time: 199 us -> 197 us (0.990)
  blocking collectives: 41.4 us -> 28.5 us
  starting transfers between devices: 61.9 us -> 69 us
  waiting for transfers between devices: 52.1 us -> 57.8 us
    all_to_all x1 -> x0, blocking collectives: 10.1 us -> none  [on_device(): levels = lax.all_to_all(plane, 'zl', 0, 0, tiled=True)]
    all_to_all x0 -> x1, waiting for transfers between devices: none -> 5.54 us  [on_device(): levels = lax.all_to_all(plane, 'zl', 0, 0, tiled=True)]
    all_to_all x0 -> x1, starting transfers between devices: none -> 3.61 us  [on_device(): levels = lax.all_to_all(plane, 'zl', 0, 0, tiled=True)]
    all_to_all x1, starting transfers between devices: 3.98 us -> 7.43 us  [on_device(): lax.all_to_all(jnp.broadcast_to(share[None], (16, 3, D)), CLIP, 0, 0, til...]
    all_to_all x1, blocking collectives: 31.3 us -> 28.5 us  [exchange(): return lax.all_to_all(values, 'zh', 0, 0, tiled=True)]
    ppermute x3, waiting for transfers between devices: 2.19 us -> 0.01 us  [other_core(): return lax.ppermute(values, 'c', [(0, 1), (1, 0)])]
  transfers between devices with their start and end apart: 14 -> 15, of which waited for: 9 -> 9; matrix products, arithmetic and copies ran while one was open for 2% -> 3% of each run, Pallas kernels for 14% -> 14%
where the time goes in v6:
time: 197 us; the launch traced here: 196 us
  starting transfers between devices  69 us (35%)
  waiting for transfers between devices  57.8 us (29%)
  Pallas kernels  29.4 us (15%)
  blocking collectives  28.5 us (14%)
  local copies, waits for them, and re-layouts  7.62 us (4%)
    all_to_all x1, blocking collectives, exchange(): return lax.all_to_all(values, 'zh', 0, 0, tiled=True)  28.5 us
    all_to_all x1, waiting for transfers between devices, exchange(): return lax.all_to_all(values, 'zh', 0, 0, tiled=True)  19.3 us
    all_to_all x1, starting transfers between devices, exchange(): return lax.all_to_all(values, 'zh', 0, 0, tiled=True)  12.9 us
    all_to_all x1, waiting for transfers between devices, on_device(): block = lax.all_to_all(unit, 'zl', 0, 0, tiled=True).reshape(PART, 4 * PART)  12 us
    pallas_call x1, Pallas kernels, on_device(): pl.pallas_call(chip_backward, out_shape=[jax.ShapeDtypeStruct((2, ZS, TOK...  12 us
    ppermute x3, starting transfers between devices, on_device(): lax.ppermute(block, 'x', [(i, (i + 4 - step) % 4) for i in range(4)])  11.4 us
    pallas_call x1, Pallas kernels, on_device(): pl.pallas_call(chip_forward, out_shape=[wide] * 5 + [factors] * 2 + [jax....  8.47 us
    all_to_all x1, starting transfers between devices, on_device(): lax.all_to_all(jnp.broadcast_to(share[None], (16, 3, D)), CLIP, 0, 0, til...  7.43 us
  transfers between devices with their start and end apart: 15, of which 9 were waited for; matrix products, arithmetic and copies ran while one was open for 3% of the time, Pallas kernels for 14%

profile of v6, /device:TPU:24, one launch (start us, length us, event | category | flops | bytes accessed | tf_op | source)
XLA Modules:
  0.0 195.9 jit_solution(11298240754882291931)
XLA Ops:
  0.7 2.2 %shard_map.87 = bf16[4,72,1152]{2,1,0:T(8,128)(2,1)} custom-call(s32[1]{0:T(128)} %bitcast.5.place_ref, bf16[72,3456]{1,0:T(8,128)(2,1)} %w_qkv_ref.1, bf16[72,1152]{1,0:T(8,128)(2,1)} %w_out_ref.1), custom_call_target="tpu_custom_call" | custom-call | flops 1000000 | bytes 2000000 | tf_op jit(solution)/shard_map/pallas_call | solution.py:349
  2.8 6.0 %all-to-all-start = ((bf16[4,72,1152]{2,1,0:T(8,128)(2,1)}), bf16[4,72,1152]{2,1,0:T(8,128)(2,1)S(1)}, u32[]{:S(2)}, u32[]{:S(2)}) async-start(bf16[4,72,1152]{2,1,0:T(8,128)(2,1)} %shard_map.87), calls=%async_computation | async-start | bytes 1327104 | tf_op jit(solution)/shard_map/all_to_all | solution.py:358
  12.2 2.1 %shard_map.86 = bf16[4,64,1152]{2,1,0:T(8,128)(2,1)} custom-call(f32[2]{0:T(128)S(1)} %pad_maximum_fusion.4.power_ref, s32[1]{0:T(128)} %bitcast.2.x_ref, bf16[128,1152]{1,0:T(8,128)(2,1)S(1)} %bitcast.27, bf16[128,1152]{1,0:T(8,128)(2,1)S(1)} %bitcast.29, f32[3,1152]{1,0:T(4,128)S(1)} %bitcast.31), custom_call_target="tpu_custom_call" | custom-call | flops 2949120 | bytes 1179648 | tf_op jit(solution)/shard_map/pallas_call | solution.py:363
  14.3 12.0 %all-to-all-done = bf16[4,72,1152]{2,1,0:T(8,128)(2,1)S(1)} async-done(((bf16[4,72,1152]{2,1,0:T(8,128)(2,1)}), bf16[4,72,1152]{2,1,0:T(8,128)(2,1)S(1)}, u32[]{:S(2)}, u32[]{:S(2)}) %all-to-all-start) | async-done | bytes 663584 | tf_op jit(solution)/shard_map/all_to_all | solution.py:358
  26.3 12.9 %all-to-all-start.1 = ((bf16[4,64,1152]{2,1,0:T(8,128)(2,1)}), bf16[4,64,1152]{2,1,0:T(8,128)(2,1)}, u32[]{:S(2)}, u32[]{:S(2)}) async-start(bf16[4,64,1152]{2,1,0:T(8,128)(2,1)} %shard_map.86), calls=%async_computation.1 | async-start | bytes 1179648 | tf_op jit(solution)/shard_map/all_to_all | solution.py:380
  39.3 3.4 %collective-permute-start.4 = (bf16[288,1152]{1,0:T(8,128)(2,1)S(1)}, bf16[288,1152]{1,0:T(8,128)(2,1)S(1)}, u32[]{:S(2)}, u32[]{:S(2)}) collective-permute-start(bf16[288,1152]{1,0:T(8,128)(2,1)S(1)} %bitcast.33), channel_id=1, source_target_pairs={{0,1},{1,2},{2,3},{3,0},{4,5},{5,6},{6,7},{7,4},{8,9},{9,10},{10,1... | collective-permute-start | bytes 1990664 | tf_op jit(solution)/shard_map/ppermute | solution.py:360
  42.6 4.6 %collective-permute-start.3 = (bf16[288,1152]{1,0:T(8,128)(2,1)S(1)}, bf16[288,1152]{1,0:T(8,128)(2,1)S(1)}, u32[]{:S(2)}, u32[]{:S(2)}) collective-permute-start(bf16[288,1152]{1,0:T(8,128)(2,1)S(1)} %bitcast.34), channel_id=1, source_target_pairs={{0,2},{1,3},{2,0},{3,1},{4,6},{5,7},{6,4},{7,5},{8,10},{9,11},{10,... | collective-permute-start | bytes 1990664 | tf_op jit(solution)/shard_map/ppermute | solution.py:360
  47.3 3.3 %collective-permute-start.2 = (bf16[288,1152]{1,0:T(8,128)(2,1)S(1)}, bf16[288,1152]{1,0:T(8,128)(2,1)S(1)}, u32[]{:S(2)}, u32[]{:S(2)}) collective-permute-start(bf16[288,1152]{1,0:T(8,128)(2,1)S(1)} %bitcast.35), channel_id=1, source_target_pairs={{0,3},{1,0},{2,1},{3,2},{4,7},{5,4},{6,5},{7,6},{8,11},{9,8},{10,9... | collective-permute-start | bytes 1990664 | tf_op jit(solution)/shard_map/ppermute | solution.py:360
  50.6 19.3 %all-to-all-done.1.refs_0_ = bf16[4,64,1152]{2,1,0:T(8,128)(2,1)} async-done(((bf16[4,64,1152]{2,1,0:T(8,128)(2,1)}), bf16[4,64,1152]{2,1,0:T(8,128)(2,1)}, u32[]{:S(2)}, u32[]{:S(2)}) %all-to-all-start.1) | async-done | bytes 589856 | tf_op jit(solution)/shard_map/all_to_all | solution.py:380
  70.0 2.6 %collective-permute-start.1 = (bf16[4,64,1152]{2,1,0:T(8,128)(2,1)}, bf16[4,64,1152]{2,1,0:T(8,128)(2,1)}, u32[]{:S(2)}, u32[]{:S(2)}) collective-permute-start(bf16[4,64,1152]{2,1,0:T(8,128)(2,1)} %all-to-all-done.1.refs_0_), channel_id=1, source_target_pairs={{0,128},{128,0},{1,129},{129,1},{2,130},{130,2},{3,131},{131,3},{4... | collective-permute-start | bytes 1769480 | tf_op jit(solution)/shard_map/ppermute | solution.py:377
  73.2 1.5 collective-permute-done.2.refs_1_.refs_5_
  74.8 0.8 copy-done.7
  75.6 2.6 %shard_map.88 = bf16[4,288,288]{2,1,0:T(8,128)(2,1)} custom-call(s32[1]{0:T(128)} %bitcast.2.x_ref, bf16[288,1152]{1,0:T(8,128)(2,1)} %bitcast.36, bf16[288,1152]{1,0:T(8,128)(2,1)} %copy-done.7, bf16[288,1152]{1,0:T(8,128)(2,1)} %copy-done.6, bf16[288,1152]{1,0:T(8,128)(2,1)} %copy-done.5), custom_call_target="tpu_custom_call" | custom-call | flops 1000000 | bytes 2000000 | tf_op jit(solution)/shard_map/pallas_call | solution.py:387
  78.2 1.9 collective-permute-start
  80.1 5.6 %collective-permute-done.1.refs_2_ = bf16[4,64,1152]{2,1,0:T(8,128)(2,1)} collective-permute-done((bf16[4,64,1152]{2,1,0:T(8,128)(2,1)}, bf16[4,64,1152]{2,1,0:T(8,128)(2,1)}, u32[]{:S(2)}, u32[]{:S(2)}) %collective-permute-start.1) | collective-permute-done | bytes 589856 | tf_op jit(solution)/shard_map/ppermute | solution.py:377
  85.7 1.9 collective-permute-start.5
  87.6 4.2 %all-to-all-start.2 = ((bf16[4,288,288]{2,1,0:T(8,128)(2,1)}), bf16[4,288,288]{2,1,0:T(8,128)(2,1)S(1)}, u32[]{:S(2)}, u32[]{:S(2)}) async-start(bf16[4,288,288]{2,1,0:T(8,128)(2,1)} %shard_map.88), calls=%async_computation.2 | async-start | bytes 1769472 | tf_op jit(solution)/shard_map/all_to_all | solution.py:398
  93.5 8.5 %shard_map.89 = (bf16[512,384]{1,0:T(8,128)(2,1)}, bf16[512,384]{1,0:T(8,128)(2,1)}, bf16[512,384]{1,0:T(8,128)(2,1)}, bf16[512,384]{1,0:T(8,128)(2,1)}, bf16[51...) custom-call(bf16[4,64,1152]{2,1,0:T(8,128)(2,1)} %all-to-all-done.1.refs_0_, ...), custom_call_target="tpu_custom_call" | custom-call | flops 1698693120 | bytes 12000000 | tf_op jit(solution)/shard_map/pallas_call | solution.py:402
  102.0 0.9 all-to-all-done.2.refs_8_
  102.9 7.3 %all-to-all-start.3 = ((bf16[8,36,1152]{2,1,0:T(8,128)(2,1)}), bf16[8,36,1152]{2,1,0:T(8,128)(2,1)S(1)}, u32[]{:S(2)}, u32[]{:S(2)}) async-start(bf16[8,36,1152]{2,1,0:T(8,128)(2,1)} %get-tuple-element.39), calls=%async_computation.3 | async-start | bytes 1474560 | tf_op jit(solution)/shard_map/all_to_all | solution.py:413
  110.2 12.0 %shard_map.90 = (f32[2,4,32,1152]{3,2,1,0:T(8,128)}, bf16[2,4,32,1152]{3,2,1,0:T(8,128)(2,1)}) custom-call(bf16[4,64,1152]{2,1,0:T(8,128)(2,1)} %all-to-all-done.1.refs_0_, bf16[4,64,1152]{2,1,0:T(8,128)(2,1)} %copy-done.9, bf16[4,64,1152]{2,1,0:T(8,128)(2,1)} %collective-permute-done.1.refs_2_, bf16[4,64,1152]{2,1,0:T(8,128)(2,1)} %copy-done.10, ...), custom_call_target="tpu_custom_call" | custom-call | flops 1358954496 | bytes 14000000 | tf_op jit(solution)/shard_map/pallas_call | solution.py:415
  122.1 1.9 collective-permute-start.6
  124.9 3.6 %all-to-all-start.4 = ((bf16[4,9,1152]{2,1,0:T(8,128)(2,1)}), bf16[4,9,1152]{2,1,0:T(8,128)(2,1)S(1)}, u32[]{:S(2)}, u32[]{:S(2)}) async-start(bf16[4,9,1152]{2,1,0:T(8,128)(2,1)} %reshape.605), calls=%async_computation.4 | async-start | bytes 294912 | tf_op jit(solution)/shard_map/all_to_all | solution.py:439
  128.5 1.1 fusion.3
  129.7 5.5 %all-to-all-done.4 = bf16[4,9,1152]{2,1,0:T(8,128)(2,1)S(1)} async-done(((bf16[4,9,1152]{2,1,0:T(8,128)(2,1)}), bf16[4,9,1152]{2,1,0:T(8,128)(2,1)S(1)}, u32[]{:S(2)}, u32[]{:S(2)}) %all-to-all-start.4) | async-done | bytes 82976 | tf_op jit(solution)/shard_map/all_to_all | solution.py:439
  135.2 3.6 %collective-permute-start.7 = (bf16[4,32,1152]{2,1,0:T(8,128)(2,1)S(1)}, bf16[4,32,1152]{2,1,0:T(8,128)(2,1)S(1)}, u32[]{:S(2)}, u32[]{:S(2)}) collective-permute-start(bf16[4,32,1152]{2,1,0:T(8,128)(2,1)S(1)} %fusion.3), channel_id=1, source_target_pairs={{0,128},{128,0},{1,129},{129,1},{2,130},{130,2},{3,131},{131,3},{4... | collective-permute-start | bytes 884744 | tf_op jit(solution)/shard_map/ppermute | solution.py:377
  139.5 4.2 %all-to-all-start.5 = ((bf16[8,3,1152]{2,1,0:T(4,128)(2,1)}), bf16[8,3,1152]{2,1,0:T(4,128)(2,1)S(1)}, u32[]{:S(2)}, u32[]{:S(2)}) async-start(bf16[8,3,1152]{2,1,0:T(4,128)(2,1)} %bitcast.11), calls=%async_computation.5 | async-start | bytes 147456 | tf_op jit(solution)/shard_map/all_to_all | solution.py:445
  143.7 5.4 %all-to-all-done.5 = bf16[8,3,1152]{2,1,0:T(4,128)(2,1)S(1)} async-done(((bf16[8,3,1152]{2,1,0:T(4,128)(2,1)}), bf16[8,3,1152]{2,1,0:T(4,128)(2,1)S(1)}, u32[]{:S(2)}, u32[]{:S(2)}) %all-to-all-start.5) | async-done | bytes 55328 | tf_op jit(solution)/shard_map/all_to_all | solution.py:445
  149.3 28.5 %all_to_all.40.back_ref = bf16[4,40,1152]{2,1,0:T(8,128)(2,1)S(1)} all-to-all(bf16[4,40,1152]{2,1,0:T(8,128)(2,1)S(1)} %fusion.2), channel_id=1, replica_groups=mesh['yh'=2,'yl'=2,'zh'=4,'c'=2,'zl'=4,'x'=4] {'zh'}, dimensions={0} | all-to-all | bytes 737280 | tf_op jit(solution)/shard_map/all_to_all | solution.py:380
  178.6 7.4 %all-to-all-start.7 = ((bf16[16,3,1152]{2,1,0:T(4,128)(2,1)}), bf16[16,3,1152]{2,1,0:T(4,128)(2,1)S(1)}, u32[]{:S(2)}, u32[]{:S(2)}) async-start(bf16[16,3,1152]{2,1,0:T(4,128)(2,1)} %broadcast_in_dim.39), calls=%async_computation.7 | async-start | bytes 294912 | tf_op jit(solution)/shard_map/all_to_all | solution.py:459
  186.0 2.1 %shard_map.91 = bf16[128,1152]{1,0:T(8,128)(2,1)} custom-call(f32[2]{0:T(128)S(1)} %pad_maximum_fusion.4.power_ref, s32[1]{0:T(128)} %bitcast.2.x_ref, bf16[128,1152]{1,0:T(8,128)(2,1)S(1)} %bitcast.28, bf16[128,1152]{1,0:T(8,128)(2,1)S(1)} %bitcast.30, f32[3,1152]{1,0:T(4,128)S(1)} %bitcast.32, bf16[4,40,1152]{2,1,0:T(8,128)(2,1)S(1)} %all_to_all.40.back_ref), custom_call_target="tpu_custom_call" | custom-call | flops 4423680 | bytes 1179648 | tf_op jit(solution)/shard_map/pallas_call | solution.py:449
  188.1 7.0 %all-to-all-done.7 = bf16[16,3,1152]{2,1,0:T(4,128)(2,1)S(1)} async-done(((bf16[16,3,1152]{2,1,0:T(4,128)(2,1)}), bf16[16,3,1152]{2,1,0:T(4,128)(2,1)S(1)}, u32[]{:S(2)}, u32[]{:S(2)}) %all-to-all-start.7) | async-done | bytes 110624 | tf_op jit(solution)/shard_map/all_to_all | solution.py:459
  (67 shorter events, 8.0 us)
Async XLA Ops:
  0.6 8.9 %copy-start = (f32[1,2,3,1152]{3,1,2,0:T(2,128)S(1)}, f32[1,2,3,1152]{3,1,2,0:T(2,128)}, u32[]{:S(2)}) copy-start(f32[1,2,3,1152]{3,1,2,0:T(2,128)} %param.9) | copy-start | bytes 82948
  0.7 8.9 %copy-start.11 = (f32[2,72]{1,0:T(2,128)S(1)}, f32[2,72]{1,0:T(2,128)}, u32[]{:S(2)}) copy-start(f32[2,72]{1,0:T(2,128)} %param.13) | copy-start | bytes 1732
  2.8 9.4 %copy-start.1 = (bf16[1,1,128,1152]{3,2,1,0:T(8,128)(2,1)S(1)}, bf16[1,1,128,1152]{3,2,1,0:T(8,128)(2,1)}, u32[]{:S(2)}) copy-start(bf16[1,1,128,1152]{3,2,1,0:T(8,128)(2,1)} %param.7) | copy-start | bytes 884740
  2.8 9.4 %copy-start.2 = (bf16[1,1,128,1152]{3,2,1,0:T(8,128)(2,1)S(1)}, bf16[1,1,128,1152]{3,2,1,0:T(8,128)(2,1)}, u32[]{:S(2)}) copy-start(bf16[1,1,128,1152]{3,2,1,0:T(8,128)(2,1)} %param.10) | copy-start | bytes 884740
  2.8 23.5 %all-to-all-start = ((bf16[4,72,1152]{2,1,0:T(8,128)(2,1)}), bf16[4,72,1152]{2,1,0:T(8,128)(2,1)S(1)}, u32[]{:S(2)}, u32[]{:S(2)}) async-start(bf16[4,72,1152]{2,1,0:T(8,128)(2,1)} %shard_map.87), calls=%async_computation | async-start | bytes 1327104 | tf_op jit(solution)/shard_map/all_to_all | solution.py:358
  26.3 48.4 %copy-start.3 = (bf16[4,72,1152]{2,1,0:T(8,128)(2,1)}, bf16[4,72,1152]{2,1,0:T(8,128)(2,1)S(1)}, u32[]{:S(2)}) copy-start(bf16[4,72,1152]{2,1,0:T(8,128)(2,1)S(1)} %all-to-all-done) | copy-start | bytes 1990660
  26.3 43.6 %all-to-all-start.1 = ((bf16[4,64,1152]{2,1,0:T(8,128)(2,1)}), bf16[4,64,1152]{2,1,0:T(8,128)(2,1)}, u32[]{:S(2)}, u32[]{:S(2)}) async-start(bf16[4,64,1152]{2,1,0:T(8,128)(2,1)} %shard_map.86), calls=%async_computation.1 | async-start | bytes 1179648 | tf_op jit(solution)/shard_map/all_to_all | solution.py:380
  39.3 33.4 %collective-permute-start.4 = (bf16[288,1152]{1,0:T(8,128)(2,1)S(1)}, bf16[288,1152]{1,0:T(8,128)(2,1)S(1)}, u32[]{:S(2)}, u32[]{:S(2)}) collective-permute-start(bf16[288,1152]{1,0:T(8,128)(2,1)S(1)} %bitcast.33), channel_id=1, source_target_pairs={{0,1},{1,2},{2,3},{3,0},{4,5},{5,6},{6,7},{7,4},{8,9},{9,10},{10,1... | collective-permute-start | bytes 1990664 | tf_op jit(solution)/shard_map/ppermute | solution.py:360
  42.6 30.5 %collective-permute-start.3 = (bf16[288,1152]{1,0:T(8,128)(2,1)S(1)}, bf16[288,1152]{1,0:T(8,128)(2,1)S(1)}, u32[]{:S(2)}, u32[]{:S(2)}) collective-permute-start(bf16[288,1152]{1,0:T(8,128)(2,1)S(1)} %bitcast.34), channel_id=1, source_target_pairs={{0,2},{1,3},{2,0},{3,1},{4,6},{5,7},{6,4},{7,5},{8,10},{9,11},{10,... | collective-permute-start | bytes 1990664 | tf_op jit(solution)/shard_map/ppermute | solution.py:360
  47.3 27.4 %collective-permute-start.2 = (bf16[288,1152]{1,0:T(8,128)(2,1)S(1)}, bf16[288,1152]{1,0:T(8,128)(2,1)S(1)}, u32[]{:S(2)}, u32[]{:S(2)}) collective-permute-start(bf16[288,1152]{1,0:T(8,128)(2,1)S(1)} %bitcast.35), channel_id=1, source_target_pairs={{0,3},{1,0},{2,1},{3,2},{4,7},{5,4},{6,5},{7,6},{8,11},{9,8},{10,9... | collective-permute-start | bytes 1990664 | tf_op jit(solution)/shard_map/ppermute | solution.py:360
  70.0 15.7 %collective-permute-start.1 = (bf16[4,64,1152]{2,1,0:T(8,128)(2,1)}, bf16[4,64,1152]{2,1,0:T(8,128)(2,1)}, u32[]{:S(2)}, u32[]{:S(2)}) collective-permute-start(bf16[4,64,1152]{2,1,0:T(8,128)(2,1)} %all-to-all-done.1.refs_0_), channel_id=1, source_target_pairs={{0,128},{128,0},{1,129},{129,1},{2,130},{130,2},{3,131},{131,3},{4... | collective-permute-start | bytes 1769480 | tf_op jit(solution)/shard_map/ppermute | solution.py:377
  72.6 2.1 %copy-start.5 = (bf16[288,1152]{1,0:T(8,128)(2,1)}, bf16[288,1152]{1,0:T(8,128)(2,1)S(1)}, u32[]{:S(2)}) copy-start(bf16[288,1152]{1,0:T(8,128)(2,1)S(1)} %collective-permute-done.4.refs_3_.refs_7_) | copy-start | bytes 1990660
  73.2 1.6 copy-start.6
  74.7 0.8 copy-start.7
  78.2 13.6 %collective-permute-start = (bf16[4,64,1152]{2,1,0:T(8,128)(2,1)}, bf16[4,64,1152]{2,1,0:T(8,128)(2,1)S(1)}, u32[]{:S(2)}, u32[]{:S(2)}) collective-permute-start(bf16[4,64,1152]{2,1,0:T(8,128)(2,1)} %all-to-all-done.1.refs_0_), channel_id=1, source_target_pairs={{0,16},{16,0},{1,17},{17,1},{2,18},{18,2},{3,19},{19,3},{4,20},{20... | collective-permute-start | bytes 1769480 | tf_op jit(solution)/shard_map/ppermute | solution.py:374
  85.7 6.1 %collective-permute-start.5 = (bf16[4,64,1152]{2,1,0:T(8,128)(2,1)}, bf16[4,64,1152]{2,1,0:T(8,128)(2,1)S(1)}, u32[]{:S(2)}, u32[]{:S(2)}) collective-permute-start(bf16[4,64,1152]{2,1,0:T(8,128)(2,1)} %collective-permute-done.1.refs_2_), channel_id=1, source_target_pairs={{0,16},{16,0},{1,17},{17,1},{2,18},{18,2},{3,19},{19,3},{4,20},{20... | collective-permute-start | bytes 1769480 | tf_op jit(solution)/shard_map/ppermute | solution.py:374
  87.6 15.3 %all-to-all-start.2 = ((bf16[4,288,288]{2,1,0:T(8,128)(2,1)}), bf16[4,288,288]{2,1,0:T(8,128)(2,1)S(1)}, u32[]{:S(2)}, u32[]{:S(2)}) async-start(bf16[4,288,288]{2,1,0:T(8,128)(2,1)} %shard_map.88), calls=%async_computation.2 | async-start | bytes 1769472 | tf_op jit(solution)/shard_map/all_to_all | solution.py:398
  91.8 0.8 copy-start.9
  92.7 0.8 copy-start.10
  102.9 7.3 %copy-start.4 = (bf16[4,288,288]{2,1,0:T(8,128)(2,1)}, bf16[4,288,288]{2,1,0:T(8,128)(2,1)S(1)}, u32[]{:S(2)}) copy-start(bf16[4,288,288]{2,1,0:T(8,128)(2,1)S(1)} %all-to-all-done.2.refs_8_) | copy-start | bytes 1990660
  102.9 19.2 %all-to-all-start.3 = ((bf16[8,36,1152]{2,1,0:T(8,128)(2,1)}), bf16[8,36,1152]{2,1,0:T(8,128)(2,1)S(1)}, u32[]{:S(2)}, u32[]{:S(2)}) async-start(bf16[8,36,1152]{2,1,0:T(8,128)(2,1)} %get-tuple-element.39), calls=%async_computation.3 | async-start | bytes 1474560 | tf_op jit(solution)/shard_map/all_to_all | solution.py:413
  122.1 6.4 %collective-permute-start.6 = (bf16[2,4,32,1152]{3,2,1,0:T(8,128)(2,1)}, bf16[2,4,32,1152]{3,2,1,0:T(8,128)(2,1)S(1)}, u32[]{:S(2)}, u32[]{:S(2)}) collective-permute-start(bf16[2,4,32,1152]{3,2,1,0:T(8,128)(2,1)} %get-tuple-element.40), channel_id=1, source_target_pairs={{0,16},{16,0},{1,17},{17,1},{2,18},{18,2},{3,19},{19,3},{4,20},{20... | collective-permute-start | bytes 1769480 | tf_op jit(solution)/shard_map/ppermute | solution.py:374
  124.2 25.0 %copy-start.8 = (f32[2,4,32,1152]{3,2,1,0:T(8,128)S(1)}, f32[2,4,32,1152]{3,2,1,0:T(8,128)}, u32[]{:S(2)}) copy-start(f32[2,4,32,1152]{3,2,1,0:T(8,128)} %get-tuple-element.37) | copy-start | bytes 3538948
  124.9 10.3 %all-to-all-start.4 = ((bf16[4,9,1152]{2,1,0:T(8,128)(2,1)}), bf16[4,9,1152]{2,1,0:T(8,128)(2,1)S(1)}, u32[]{:S(2)}, u32[]{:S(2)}) async-start(bf16[4,9,1152]{2,1,0:T(8,128)(2,1)} %reshape.605), calls=%async_computation.4 | async-start | bytes 294912 | tf_op jit(solution)/shard_map/all_to_all | solution.py:439
  135.2 13.9 %collective-permute-start.7 = (bf16[4,32,1152]{2,1,0:T(8,128)(2,1)S(1)}, bf16[4,32,1152]{2,1,0:T(8,128)(2,1)S(1)}, u32[]{:S(2)}, u32[]{:S(2)}) collective-permute-start(bf16[4,32,1152]{2,1,0:T(8,128)(2,1)S(1)} %fusion.3), channel_id=1, source_target_pairs={{0,128},{128,0},{1,129},{129,1},{2,130},{130,2},{3,131},{131,3},{4... | collective-permute-start | bytes 884744 | tf_op jit(solution)/shard_map/ppermute | solution.py:377
  139.5 9.6 %all-to-all-start.5 = ((bf16[8,3,1152]{2,1,0:T(4,128)(2,1)}), bf16[8,3,1152]{2,1,0:T(4,128)(2,1)S(1)}, u32[]{:S(2)}, u32[]{:S(2)}) async-start(bf16[8,3,1152]{2,1,0:T(4,128)(2,1)} %bitcast.11), calls=%async_computation.5 | async-start | bytes 147456 | tf_op jit(solution)/shard_map/all_to_all | solution.py:445
  178.6 16.5 %all-to-all-start.7 = ((bf16[16,3,1152]{2,1,0:T(4,128)(2,1)}), bf16[16,3,1152]{2,1,0:T(4,128)(2,1)S(1)}, u32[]{:S(2)}, u32[]{:S(2)}) async-start(bf16[16,3,1152]{2,1,0:T(4,128)(2,1)} %broadcast_in_dim.39), calls=%async_computation.7 | async-start | bytes 294912 | tf_op jit(solution)/shard_map/all_to_all | solution.py:459

commit v7 on v6

--- a/solution.py
+++ b/solution.py
@@ -42,30 +42,28 @@
     return centred * factor, factor
 
 
-def home_forward(power_ref, x_ref, hidden_ref, grad_ref, mod_ref, out_ref, turned_ref):
+def block_at(place, spot_ref):
+    return 4 * lax.rem(spot_ref[1] + place % 4, 4) + lax.rem(spot_ref[0] + place // 4, 4)
+
+
+def home_forward(power_ref, spot_ref, hidden_ref, grad_ref, mod_ref, out_ref, turned_ref, block_ref):
     normed, _ = normalise(hidden_ref[...], power_ref[0], power_ref[1])
     modded = normed * (1.0 + mod_ref[1:2, :]) + mod_ref[0:1, :]
-    for x in range(4):
-
-        @pl.when(x_ref[0] == x)
-        def _(x=x):
-            for place, block in enumerate(block_order(x)):
-                turned_ref[:, place * HD : (place + 1) * HD] = modded[:, block * HD : (block + 1) * HD]
-
+    for block in range(16):
+        block_ref[block] = modded[:, block * HD : (block + 1) * HD]
+    for place in range(16):
+        turned_ref[:, place * HD : (place + 1) * HD] = block_ref[block_at(place, spot_ref)]
     out_ref[:, :TOK, :] = turned_ref[...].astype(BF16).reshape(ZS, TOK, D)
     out_ref[:, TOK:, :] = (mod_ref[2:3, :] * grad_ref[...].astype(F32)).astype(BF16).reshape(ZS, TOK, D)
 
 
-def home_backward(power_ref, x_ref, hidden_ref, grad_ref, mod_ref, back_ref, out_ref, turned_ref):
+def home_backward(power_ref, spot_ref, hidden_ref, grad_ref, mod_ref, back_ref, out_ref, turned_ref, block_ref):
     normed, factor = normalise(hidden_ref[...], power_ref[0], power_ref[1])
     back = back_ref[:, :TOK, :].reshape(ROWS, D).astype(F32)
-    for x in range(4):
-
-        @pl.when(x_ref[0] == x)
-        def _(x=x):
-            for place, block in enumerate(block_order(x)):
-                turned_ref[:, block * HD : (block + 1) * HD] = back[:, place * HD : (place + 1) * HD]
-
+    for place in range(16):
+        block_ref[block_at(place, spot_ref)] = back[:, place * HD : (place + 1) * HD]
+    for block in range(16):
+        turned_ref[:, block * HD : (block + 1) * HD] = block_ref[block]
     d_normed = turned_ref[...] * (1.0 + mod_ref[1:2, :])
     d_rows = factor * (
         d_normed
@@ -73,10 +71,6 @@
         - normed * jnp.mean(d_normed * normed, axis=-1, keepdims=True)
     )
     out_ref[...] = (grad_ref[...].astype(F32) + d_rows.astype(BF16).astype(F32)).astype(BF16)
-
-
-def block_order(x):
-    return [4 * zl + (x + step) % 4 for step in range(4) for zl in range(4)]
 
 
 def pick_weights(place_ref, w_qkv_ref, w_out_ref, out_ref, unit_ref):
@@ -94,34 +88,30 @@
                     unit_ref[:, to : to + 2 * HD] = qkv[:, first : first + 2 * HD]
             unit_ref[:, 3 * PART :] = out[:, place * PART : (place + 1) * PART]
 
-    unit = unit_ref[...].astype(BF16)
-    for copy in range(4):
-        out_ref[copy] = unit
-
-
-def out_rows(x_ref, *refs):
-    *block_refs, send_ref, rows_ref, sem = refs
+    out_ref[...] = unit_ref[...].astype(BF16)
+
+
+def out_rows(spot_ref, *refs):
+    *block_refs, send_ref, rows_ref, head_ref, sem = refs
     copies = [
         pltpu.make_async_copy(ref.at[:, pl.ds(768, 384)], rows_ref.at[step], sem.at[step])
         for step, ref in enumerate(block_refs)
     ]
     for copy in copies:
         copy.start()
-    for copy in copies:
+    for step, copy in enumerate(copies):
         copy.wait()
-    blocks = [rows_ref[step].astype(F32)[:, 96:384] for step in range(4)]
-    for x in range(4):
-
-        @pl.when(x_ref[0] == x)
-        def _(x=x):
-            for place in range(4):
-                yl, core = place // 2, place % 2
-                pieces = []
-                for high in range(2):
-                    for low in range(2):
-                        first = (2 * high + yl) * HD
-                        pieces.append(blocks[(2 * core + low - x) % 4][first : first + HD])
-                send_ref[place] = jnp.concatenate(pieces, axis=0).astype(BF16)
+        rows = rows_ref[step].astype(F32)[:, 96:384]
+        for level in range(4):
+            head_ref[4 * step + level] = rows[level * HD : (level + 1) * HD]
+    for place in range(4):
+        yl, core = place // 2, place % 2
+        pieces = [
+            head_ref[4 * lax.rem(2 * core + low + 4 - spot_ref[0], 4) + lax.rem(2 * high + yl + 4 - spot_ref[1], 4)]
+            for high in range(2)
+            for low in range(2)
+        ]
+        send_ref[place] = jnp.concatenate(pieces, axis=0).astype(BF16)
 
 
 def nt(left, right):
@@ -340,7 +330,7 @@
         ]
     )
     mod = lax.dynamic_index_in_dim(modulation[0], lax.axis_index("yh"), 0, keepdims=False)
-    x_place = x[None]
+    spot = jnp.stack([x, lax.axis_index("zl")])
     smem = pl.BlockSpec(memory_space=pltpu.SMEM)
     vmem = pl.BlockSpec(memory_space=pltpu.VMEM)
     hbm = pl.BlockSpec(memory_space=pl.ANY)
@@ -348,14 +338,17 @@
 
     unit = pl.pallas_call(
         pick_weights,
-        out_shape=jax.ShapeDtypeStruct((4, HD, 4 * PART), BF16),
+        out_shape=jax.ShapeDtypeStruct((HD, 4 * PART), BF16),
         in_specs=[smem, vmem, vmem],
         out_specs=vmem,
         scratch_shapes=[pltpu.VMEM((HD, 4 * PART), F32)],
         compiler_params=PARAMS,
         cost_estimate=cost(10**6, 2 * 10**6),
     )((2 * yl + core)[None], w_qkv, w_out)
-    block = lax.all_to_all(unit, "zl", 0, 0, tiled=True).reshape(PART, 4 * PART)
+    block = jnp.concatenate(
+        [unit]
+        + [lax.ppermute(unit, ("zh", "zl"), [(i, (i + 16 - step) % 16) for i in range(16)]) for step in (1, 2, -1)]
+    )
     blocks = [block] + [
         lax.ppermute(block, "x", [(i, (i + 4 - step) % 4) for i in range(4)]) for step in (1, 2, 3)
     ]
@@ -365,10 +358,10 @@
         out_shape=jax.ShapeDtypeStruct((ZS, 2 * TOK, D), BF16),
         in_specs=[smem, smem, vmem, vmem, vmem],
         out_specs=vmem,
-        scratch_shapes=[pltpu.VMEM((ROWS, D), F32)],
+        scratch_shapes=[pltpu.VMEM((ROWS, D), F32), pltpu.VMEM((16, ROWS, HD), F32)],
         compiler_params=SMALL,
         cost_estimate=cost(20 * ROWS * D, 8 * ROWS * D),
-    )(power, x_place, rows, cotangent, mod)
+    )(power, spot, rows, cotangent, mod)
 
     def other_core(values):
         return lax.ppermute(values, "c", [(0, 1), (1, 0)])
@@ -380,8 +373,9 @@
         return lax.all_to_all(values, "zh", 0, 0, tiled=True)
 
     tables, tables_back = turn_tables(qk_gain, yl, core)
-    sent, _, tables, tables_back = lax.optimization_barrier((sent, block, tables, tables_back))
+    sent, _ = lax.optimization_barrier((sent, block))
     own = exchange(sent)
+    own, tables, tables_back = lax.optimization_barrier((own, tables, tables_back))
     across = other_y(own)
     near = other_core(own)
     w_back = pl.pallas_call(
@@ -389,10 +383,10 @@
         out_shape=jax.ShapeDtypeStruct((4, PART, PART), BF16),
         in_specs=[smem] + [hbm] * 4,
         out_specs=vmem,
-        scratch_shapes=[pltpu.VMEM((4, PART, 384), BF16), four],
+        scratch_shapes=[pltpu.VMEM((4, PART, 384), BF16), pltpu.VMEM((16, HD, PART), F32), four],
         compiler_params=PARAMS,
         cost_estimate=cost(10**6, 2 * 10**6),
-    )(x_place, *blocks)
+    )(spot, *blocks)
     across, w_back = lax.optimization_barrier((across, w_back))
     arrays = [own, near, across, other_core(across)]
     w_back = lax.all_to_all(w_back, ("yl", "c"), 0, 0, tiled=True)
@@ -451,10 +445,10 @@
         out_shape=jax.ShapeDtypeStruct((ROWS, D), BF16),
         in_specs=[smem, smem, vmem, vmem, vmem, vmem],
         out_specs=vmem,
-        scratch_shapes=[pltpu.VMEM((ROWS, D), F32)],
+        scratch_shapes=[pltpu.VMEM((ROWS, D), F32), pltpu.VMEM((16, ROWS, HD), F32)],
         compiler_params=SMALL,
         cost_estimate=cost(30 * ROWS * D, 8 * ROWS * D),
-    )(power, x_place, rows, cotangent, mod, joined)
+    )(power, spot, rows, cotangent, mod, joined)
     share = jnp.sum(joined[:, TOK : TOK + 3].astype(F32), axis=0).astype(BF16)
     final = lax.all_to_all(jnp.broadcast_to(share[None], (16, 3, D)), CLIP, 0, 0, tiled=True)
     final = final.reshape(4, 12, D)[:, :9].reshape(36, D)

time: 197 us -> 197 us (level)
  waiting for transfers between devices: 57.8 us -> 46.6 us
  starting transfers between devices: 69 us -> 76.4 us
    ppermute x0 -> x3, starting transfers between devices: none -> 17.7 us  [on_device(): lax.ppermute(unit, ('zh', 'zl'), [(i, (i + 16 - step) % 16) for i in rang...]
    all_to_all x1 -> x0, waiting for transfers between devices: 12 us -> none  [on_device(): block = lax.all_to_all(unit, 'zl', 0, 0, tiled=True).reshape(PART, 4 * PART)]
    all_to_all x1 -> x0, starting transfers between devices: 6.03 us -> none  [on_device(): block = lax.all_to_all(unit, 'zl', 0, 0, tiled=True).reshape(PART, 4 * PART)]
    all_to_all x1, starting transfers between devices: 12.9 us -> 8.91 us  [exchange(): return lax.all_to_all(values, 'zh', 0, 0, tiled=True)]
    all_to_all x1, waiting for transfers between devices: 19.3 us -> 16.2 us  [exchange(): return lax.all_to_all(values, 'zh', 0, 0, tiled=True)]
    ppermute x0 -> x3, waiting for transfers between devices: none -> 2.23 us  [on_device(): lax.ppermute(unit, ('zh', 'zl'), [(i, (i + 16 - step) % 16) for i in rang...]
    unnamed x25 -> x37, local copies, waits for them, and re-layouts: 2.5 us -> 4.49 us
  transfers between devices with their start and end apart: 15 -> 17, of which waited for: 9 -> 9; matrix products, arithmetic and copies ran while one was open for 3% -> 2% of each run, Pallas kernels for 14% -> 14%
where the time goes in v7:
time: 197 us; the launch traced here: 196 us
  starting transfers between devices  76.4 us (39%)
  waiting for transfers between devices  46.6 us (24%)
  blocking collectives  30.3 us (15%)
  Pallas kernels  30.2 us (15%)
  local copies, waits for them, and re-layouts  9.59 us (5%)
    all_to_all x1, blocking collectives, exchange(): return lax.all_to_all(values, 'zh', 0, 0, tiled=True)  30.3 us
    ppermute x3, starting transfers between devices, on_device(): lax.ppermute(unit, ('zh', 'zl'), [(i, (i + 16 - step) % 16) for i in rang...  17.7 us
    all_to_all x1, waiting for transfers between devices, exchange(): return lax.all_to_all(values, 'zh', 0, 0, tiled=True)  16.2 us
    pallas_call x1, Pallas kernels, on_device(): pl.pallas_call(chip_backward, out_shape=[jax.ShapeDtypeStruct((2, ZS, TOK...  11.9 us
    ppermute x3, starting transfers between devices, on_device(): lax.ppermute(block, 'x', [(i, (i + 4 - step) % 4) for i in range(4)])  11.4 us
    all_to_all x1, starting transfers between devices, exchange(): return lax.all_to_all(values, 'zh', 0, 0, tiled=True)  8.91 us
    pallas_call x1, Pallas kernels, on_device(): pl.pallas_call(chip_forward, out_shape=[wide] * 5 + [factors] * 2 + [jax....  8.47 us
    all_to_all x1, starting transfers between devices, on_device(): plane = lax.all_to_all(part, ('yh', 'x'), 0, 0, tiled=True)  7.26 us
  transfers between devices with their start and end apart: 17, of which 9 were waited for; matrix products, arithmetic and copies ran while one was open for 2% of the time, Pallas kernels for 14%

profile of v7, /device:TPU:24, one launch (start us, length us, event | category | flops | bytes accessed | tf_op | source)
XLA Modules:
  0.0 195.6 jit_solution(8820022434846637767)
XLA Ops:
  0.7 1.9 shard_map.87
  2.6 3.8 %collective-permute-start.2 = (bf16[72,1152]{1,0:T(8,128)(2,1)}, bf16[72,1152]{1,0:T(8,128)(2,1)S(1)}, u32[]{:S(2)}, u32[]{:S(2)}) collective-permute-start(bf16[72,1152]{1,0:T(8,128)(2,1)} %shard_map.87), channel_id=1, source_target_pairs={{0,4},{4,8},{8,12},{12,32},{32,36},{36,40},{40,44},{44,64},{64,68}... | collective-permute-start | bytes 497672 | tf_op jit(solution)/shard_map/ppermute | solution.py:350
  6.4 10.9 %collective-permute-start.1 = (bf16[72,1152]{1,0:T(8,128)(2,1)}, bf16[72,1152]{1,0:T(8,128)(2,1)S(1)}, u32[]{:S(2)}, u32[]{:S(2)}) collective-permute-start(bf16[72,1152]{1,0:T(8,128)(2,1)} %shard_map.87), channel_id=1, source_target_pairs={{0,104},{4,108},{8,0},{12,4},{32,8},{36,12},{40,32},{44,36},{64,40... | collective-permute-start | bytes 497672 | tf_op jit(solution)/shard_map/ppermute | solution.py:350
  17.4 2.9 %collective-permute-start = (bf16[72,1152]{1,0:T(8,128)(2,1)}, bf16[72,1152]{1,0:T(8,128)(2,1)S(1)}, u32[]{:S(2)}, u32[]{:S(2)}) collective-permute-start(bf16[72,1152]{1,0:T(8,128)(2,1)} %shard_map.87), channel_id=1, source_target_pairs={{0,108},{4,0},{8,4},{12,8},{32,12},{36,32},{40,36},{44,40},{64,44}... | collective-permute-start | bytes 497672 | tf_op jit(solution)/shard_map/ppermute | solution.py:350
  23.1 2.4 %shard_map.86 = bf16[4,64,1152]{2,1,0:T(8,128)(2,1)} custom-call(f32[2]{0:T(128)S(1)} %pad_maximum_fusion.5.power_ref, s32[2]{0:T(128)S(1)} %pad_add_fusion.spot_ref, bf16[128,1152]{1,0:T(8,128)(2,1)S(1)} %bitcast.27, bf16[128,1152]{1,0:T(8,128)(2,1)S(1)} %bitcast.29, f32[3,1152]{1,0:T(4,128)S(1)} %bitcast.31), custom_call_target="tpu_custom_call" | custom-call | flops 2949120 | bytes 1179648 | tf_op jit(solution)/shard_map/pallas_call | solution.py:356
  25.5 2.2 %collective-permute-done = bf16[72,1152]{1,0:T(8,128)(2,1)S(1)} collective-permute-done((bf16[72,1152]{1,0:T(8,128)(2,1)}, bf16[72,1152]{1,0:T(8,128)(2,1)S(1)}, u32[]{:S(2)}, u32[]{:S(2)}) %collective-permute-start) | collective-permute-done | bytes 165920 | tf_op jit(solution)/shard_map/ppermute | solution.py:350
  27.9 8.9 %all-to-all-start = ((bf16[4,64,1152]{2,1,0:T(8,128)(2,1)}), bf16[4,64,1152]{2,1,0:T(8,128)(2,1)}, u32[]{:S(2)}, u32[]{:S(2)}) async-start(bf16[4,64,1152]{2,1,0:T(8,128)(2,1)} %shard_map.86), calls=%async_computation | async-start | bytes 1179648 | tf_op jit(solution)/shard_map/all_to_all | solution.py:373
  37.7 3.4 %collective-permute-start.7 = (bf16[288,1152]{1,0:T(8,128)(2,1)S(1)}, bf16[288,1152]{1,0:T(8,128)(2,1)S(1)}, u32[]{:S(2)}, u32[]{:S(2)}) collective-permute-start(bf16[288,1152]{1,0:T(8,128)(2,1)S(1)} %pad_maximum_fusion.refs_0_.refs_4_), channel_id=1, source_target_pairs={{0,1},{1,2},{2,3},{3,0},{4,5},{5,6},{6,7},{7,4},{8,9},{9,10},{10,1... | collective-permute-start | bytes 1990664 | tf_op jit(solution)/shard_map/ppermute | solution.py:353
  41.1 4.6 %collective-permute-start.6 = (bf16[288,1152]{1,0:T(8,128)(2,1)S(1)}, bf16[288,1152]{1,0:T(8,128)(2,1)S(1)}, u32[]{:S(2)}, u32[]{:S(2)}) collective-permute-start(bf16[288,1152]{1,0:T(8,128)(2,1)S(1)} %pad_maximum_fusion.refs_0_.refs_4_), channel_id=1, source_target_pairs={{0,2},{1,3},{2,0},{3,1},{4,6},{5,7},{6,4},{7,5},{8,10},{9,11},{10,... | collective-permute-start | bytes 1990664 | tf_op jit(solution)/shard_map/ppermute | solution.py:353
  45.7 3.3 %collective-permute-start.5 = (bf16[288,1152]{1,0:T(8,128)(2,1)S(1)}, bf16[288,1152]{1,0:T(8,128)(2,1)S(1)}, u32[]{:S(2)}, u32[]{:S(2)}) collective-permute-start(bf16[288,1152]{1,0:T(8,128)(2,1)S(1)} %pad_maximum_fusion.refs_0_.refs_4_), channel_id=1, source_target_pairs={{0,3},{1,0},{2,1},{3,2},{4,7},{5,4},{6,5},{7,6},{8,11},{9,8},{10,9... | collective-permute-start | bytes 1990664 | tf_op jit(solution)/shard_map/ppermute | solution.py:353
  50.7 16.2 %all-to-all-done.refs_0_ = bf16[4,64,1152]{2,1,0:T(8,128)(2,1)} async-done(((bf16[4,64,1152]{2,1,0:T(8,128)(2,1)}), bf16[4,64,1152]{2,1,0:T(8,128)(2,1)}, u32[]{:S(2)}, u32[]{:S(2)}) %all-to-all-start) | async-done | bytes 589856 | tf_op jit(solution)/shard_map/all_to_all | solution.py:373
  66.9 2.6 %collective-permute-start.4 = (bf16[4,64,1152]{2,1,0:T(8,128)(2,1)}, bf16[4,64,1152]{2,1,0:T(8,128)(2,1)S(1)}, u32[]{:S(2)}, u32[]{:S(2)}) collective-permute-start(bf16[4,64,1152]{2,1,0:T(8,128)(2,1)} %all-to-all-done.refs_0_), channel_id=1, source_target_pairs={{0,128},{128,0},{1,129},{129,1},{2,130},{130,2},{3,131},{131,3},{4... | collective-permute-start | bytes 1769480 | tf_op jit(solution)/shard_map/ppermute | solution.py:370
  69.5 1.6 collective-permute-done.6.refs_2_.refs_6_
  71.2 1.5 collective-permute-done.5.refs_1_.refs_5_
  73.6 3.2 %shard_map.88 = bf16[4,288,288]{2,1,0:T(8,128)(2,1)} custom-call(s32[2]{0:T(128)} %copy-done.5, bf16[288,1152]{1,0:T(8,128)(2,1)} %copy-done.7, bf16[288,1152]{1,0:T(8,128)(2,1)} %copy-done.11, bf16[288,1152]{1,0:T(8,128)(2,1)} %copy-done.10, bf16[288,1152]{1,0:T(8,128)(2,1)} %copy-done.9), custom_call_target="tpu_custom_call" | custom-call | flops 1000000 | bytes 2000000 | tf_op jit(solution)/shard_map/pallas_call | solution.py:381
  76.8 1.9 collective-permute-start.3
  78.7 5.3 %collective-permute-done.4.refs_2_ = bf16[4,64,1152]{2,1,0:T(8,128)(2,1)S(1)} collective-permute-done((bf16[4,64,1152]{2,1,0:T(8,128)(2,1)}, bf16[4,64,1152]{2,1,0:T(8,128)(2,1)S(1)}, u32[]{:S(2)}, u32[]{:S(2)}) %collective-permute-start.4) | collective-permute-done | bytes 589856 | tf_op jit(solution)/shard_map/ppermute | solution.py:370
  84.0 1.9 collective-permute-start.8
  85.9 4.1 %all-to-all-start.1 = ((bf16[4,288,288]{2,1,0:T(8,128)(2,1)}), bf16[4,288,288]{2,1,0:T(8,128)(2,1)S(1)}, u32[]{:S(2)}, u32[]{:S(2)}) async-start(bf16[4,288,288]{2,1,0:T(8,128)(2,1)} %shard_map.88), calls=%async_computation.1 | async-start | bytes 1769472 | tf_op jit(solution)/shard_map/all_to_all | solution.py:392
  91.7 8.5 %shard_map.89 = (bf16[512,384]{1,0:T(8,128)(2,1)}, bf16[512,384]{1,0:T(8,128)(2,1)}, bf16[512,384]{1,0:T(8,128)(2,1)}, bf16[512,384]{1,0:T(8,128)(2,1)}, bf16[51...) custom-call(bf16[4,64,1152]{2,1,0:T(8,128)(2,1)} %all-to-all-done.refs_0_, ...), custom_call_target="tpu_custom_call" | custom-call | flops 1698693120 | bytes 12000000 | tf_op jit(solution)/shard_map/pallas_call | solution.py:396
  101.0 7.3 %all-to-all-start.2 = ((bf16[8,36,1152]{2,1,0:T(8,128)(2,1)}), bf16[8,36,1152]{2,1,0:T(8,128)(2,1)S(1)}, u32[]{:S(2)}, u32[]{:S(2)}) async-start(bf16[8,36,1152]{2,1,0:T(8,128)(2,1)} %get-tuple-element.41), calls=%async_computation.2 | async-start | bytes 1474560 | tf_op jit(solution)/shard_map/all_to_all | solution.py:407
  108.3 11.9 %shard_map.90 = (f32[2,4,32,1152]{3,2,1,0:T(8,128)}, bf16[2,4,32,1152]{3,2,1,0:T(8,128)(2,1)}) custom-call(bf16[4,64,1152]{2,1,0:T(8,128)(2,1)} %all-to-all-done.refs_0_, bf16[4,64,1152]{2,1,0:T(8,128)(2,1)} %copy-done.15, bf16[4,64,1152]{2,1,0:T(8,128)(2,1)} %copy-done.14, bf16[4,64,1152]{2,1,0:T(8,128)(2,1)} %copy-done.16, bf16[288,1152]{1,0:T(8,128)(2,1)} %copy-done.7, ...), custom_call_target="tpu_custom_call" | custom-call | flops 1358954496 | bytes 14000000 | tf_op jit(solution)/shard_map/pallas_call | solution.py:409
  120.3 2.1 %collective-permute-start.9 = (bf16[2,4,32,1152]{3,2,1,0:T(8,128)(2,1)}, bf16[2,4,32,1152]{3,2,1,0:T(8,128)(2,1)S(1)}, u32[]{:S(2)}, u32[]{:S(2)}) collective-permute-start(bf16[2,4,32,1152]{3,2,1,0:T(8,128)(2,1)} %get-tuple-element.42), channel_id=1, source_target_pairs={{0,16},{16,0},{1,17},{17,1},{2,18},{18,2},{3,19},{19,3},{4,20},{20... | collective-permute-start | bytes 1769480 | tf_op jit(solution)/shard_map/ppermute | solution.py:367
  123.1 3.6 %all-to-all-start.3 = ((bf16[4,9,1152]{2,1,0:T(8,128)(2,1)}), bf16[4,9,1152]{2,1,0:T(8,128)(2,1)S(1)}, u32[]{:S(2)}, u32[]{:S(2)}) async-start(bf16[4,9,1152]{2,1,0:T(8,128)(2,1)} %reshape.601), calls=%async_computation.3 | async-start | bytes 294912 | tf_op jit(solution)/shard_map/all_to_all | solution.py:433
  126.8 6.6 %all-to-all-done.3 = bf16[4,9,1152]{2,1,0:T(8,128)(2,1)S(1)} async-done(((bf16[4,9,1152]{2,1,0:T(8,128)(2,1)}), bf16[4,9,1152]{2,1,0:T(8,128)(2,1)S(1)}, u32[]{:S(2)}, u32[]{:S(2)}) %all-to-all-start.3) | async-done | bytes 82976 | tf_op jit(solution)/shard_map/all_to_all | solution.py:433
  133.4 3.6 %collective-permute-start.10 = (bf16[4,32,1152]{2,1,0:T(8,128)(2,1)S(1)}, bf16[4,32,1152]{2,1,0:T(8,128)(2,1)S(1)}, u32[]{:S(2)}, u32[]{:S(2)}) collective-permute-start(bf16[4,32,1152]{2,1,0:T(8,128)(2,1)S(1)} %fusion.3), channel_id=1, source_target_pairs={{0,128},{128,0},{1,129},{129,1},{2,130},{130,2},{3,131},{131,3},{4... | collective-permute-start | bytes 884744 | tf_op jit(solution)/shard_map/ppermute | solution.py:370
  137.7 4.2 %all-to-all-start.4 = ((bf16[8,3,1152]{2,1,0:T(4,128)(2,1)}), bf16[8,3,1152]{2,1,0:T(4,128)(2,1)S(1)}, u32[]{:S(2)}, u32[]{:S(2)}) async-start(bf16[8,3,1152]{2,1,0:T(4,128)(2,1)} %bitcast.11), calls=%async_computation.4 | async-start | bytes 147456 | tf_op jit(solution)/shard_map/all_to_all | solution.py:439
  142.0 5.4 %all-to-all-done.4 = bf16[8,3,1152]{2,1,0:T(4,128)(2,1)S(1)} async-done(((bf16[8,3,1152]{2,1,0:T(4,128)(2,1)}), bf16[8,3,1152]{2,1,0:T(4,128)(2,1)S(1)}, u32[]{:S(2)}, u32[]{:S(2)}) %all-to-all-start.4) | async-done | bytes 55328 | tf_op jit(solution)/shard_map/all_to_all | solution.py:439
  147.6 30.3 %all_to_all.35.back_ref = bf16[4,40,1152]{2,1,0:T(8,128)(2,1)S(1)} all-to-all(bf16[4,40,1152]{2,1,0:T(8,128)(2,1)S(1)} %fusion.2), channel_id=1, replica_groups=mesh['yh'=2,'yl'=2,'zh'=4,'c'=2,'zl'=4,'x'=4] {'zh'}, dimensions={0} | all-to-all | bytes 737280 | tf_op jit(solution)/shard_map/all_to_all | solution.py:373
  178.6 7.2 %all-to-all-start.6 = ((bf16[16,3,1152]{2,1,0:T(4,128)(2,1)}), bf16[16,3,1152]{2,1,0:T(4,128)(2,1)S(1)}, u32[]{:S(2)}, u32[]{:S(2)}) async-start(bf16[16,3,1152]{2,1,0:T(4,128)(2,1)} %broadcast_in_dim.35), calls=%async_computation.6 | async-start | bytes 294912 | tf_op jit(solution)/shard_map/all_to_all | solution.py:453
  185.8 2.3 %shard_map.91 = bf16[128,1152]{1,0:T(8,128)(2,1)} custom-call(f32[2]{0:T(128)S(1)} %pad_maximum_fusion.5.power_ref, s32[2]{0:T(128)S(1)} %copy-done.6, bf16[128,1152]{1,0:T(8,128)(2,1)S(1)} %bitcast.28, bf16[128,1152]{1,0:T(8,128)(2,1)S(1)} %bitcast.30, f32[3,1152]{1,0:T(4,128)S(1)} %bitcast.32, bf16[4,40,1152]{2,1,0:T(8,128)(2,1)S(1)} %all_to_all.35.back_ref), custom_call_target="tpu_custom_call" | custom-call | flops 4423680 | bytes 1179648 | tf_op jit(solution)/shard_map/pallas_call | solution.py:443
  188.1 6.7 %all-to-all-done.6 = bf16[16,3,1152]{2,1,0:T(4,128)(2,1)S(1)} async-done(((bf16[16,3,1152]{2,1,0:T(4,128)(2,1)}), bf16[16,3,1152]{2,1,0:T(4,128)(2,1)S(1)}, u32[]{:S(2)}, u32[]{:S(2)}) %all-to-all-start.6) | async-done | bytes 110624 | tf_op jit(solution)/shard_map/all_to_all | solution.py:453
  (85 shorter events, 11.3 us)
Async XLA Ops:
  0.6 19.7 %copy-start = (f32[1,2,3,1152]{3,1,2,0:T(2,128)S(1)}, f32[1,2,3,1152]{3,1,2,0:T(2,128)}, u32[]{:S(2)}) copy-start(f32[1,2,3,1152]{3,1,2,0:T(2,128)} %param.9) | copy-start | bytes 82948
  2.6 22.9 %collective-permute-start.2 = (bf16[72,1152]{1,0:T(8,128)(2,1)}, bf16[72,1152]{1,0:T(8,128)(2,1)S(1)}, u32[]{:S(2)}, u32[]{:S(2)}) collective-permute-start(bf16[72,1152]{1,0:T(8,128)(2,1)} %shard_map.87), channel_id=1, source_target_pairs={{0,4},{4,8},{8,12},{12,32},{32,36},{36,40},{40,44},{44,64},{64,68}... | collective-permute-start | bytes 497672 | tf_op jit(solution)/shard_map/ppermute | solution.py:350
  6.4 19.1 %collective-permute-start.1 = (bf16[72,1152]{1,0:T(8,128)(2,1)}, bf16[72,1152]{1,0:T(8,128)(2,1)S(1)}, u32[]{:S(2)}, u32[]{:S(2)}) collective-permute-start(bf16[72,1152]{1,0:T(8,128)(2,1)} %shard_map.87), channel_id=1, source_target_pairs={{0,104},{4,108},{8,0},{12,4},{32,8},{36,12},{40,32},{44,36},{64,40... | collective-permute-start | bytes 497672 | tf_op jit(solution)/shard_map/ppermute | solution.py:350
  17.4 10.4 %collective-permute-start = (bf16[72,1152]{1,0:T(8,128)(2,1)}, bf16[72,1152]{1,0:T(8,128)(2,1)S(1)}, u32[]{:S(2)}, u32[]{:S(2)}) collective-permute-start(bf16[72,1152]{1,0:T(8,128)(2,1)} %shard_map.87), channel_id=1, source_target_pairs={{0,108},{4,0},{8,4},{12,8},{32,12},{36,32},{40,36},{44,40},{64,44}... | collective-permute-start | bytes 497672 | tf_op jit(solution)/shard_map/ppermute | solution.py:350
  20.4 7.4 %copy-start.5 = (s32[2]{0:T(128)}, s32[2]{0:T(128)S(1)}, u32[]{:S(2)}) copy-start(s32[2]{0:T(128)S(1)} %pad_add_fusion.spot_ref) | copy-start | bytes 28
  21.2 1.0 copy-start.1
  22.1 1.0 copy-start.3
  23.1 4.7 %copy-start.13 = (bf16[72,1152]{1,0:T(8,128)(2,1)S(1)}, bf16[72,1152]{1,0:T(8,128)(2,1)}, u32[]{:S(2)}) copy-start(bf16[72,1152]{1,0:T(8,128)(2,1)} %shard_map.87) | copy-start | bytes 497668
  25.5 11.2 %copy-start.17 = (f32[2,72]{1,0:T(2,128)S(1)}, f32[2,72]{1,0:T(2,128)}, u32[]{:S(2)}) copy-start(f32[2,72]{1,0:T(2,128)} %param.13) | copy-start | bytes 1732
  27.8 22.2 %copy-start.7 = (bf16[288,1152]{1,0:T(8,128)(2,1)}, bf16[288,1152]{1,0:T(8,128)(2,1)S(1)}, u32[]{:S(2)}) copy-start(bf16[288,1152]{1,0:T(8,128)(2,1)S(1)} %pad_maximum_fusion.refs_0_.refs_4_) | copy-start | bytes 1990660
  27.9 39.1 %all-to-all-start = ((bf16[4,64,1152]{2,1,0:T(8,128)(2,1)}), bf16[4,64,1152]{2,1,0:T(8,128)(2,1)}, u32[]{:S(2)}, u32[]{:S(2)}) async-start(bf16[4,64,1152]{2,1,0:T(8,128)(2,1)} %shard_map.86), calls=%async_computation | async-start | bytes 1179648 | tf_op jit(solution)/shard_map/all_to_all | solution.py:373
  37.7 31.9 %collective-permute-start.7 = (bf16[288,1152]{1,0:T(8,128)(2,1)S(1)}, bf16[288,1152]{1,0:T(8,128)(2,1)S(1)}, u32[]{:S(2)}, u32[]{:S(2)}) collective-permute-start(bf16[288,1152]{1,0:T(8,128)(2,1)S(1)} %pad_maximum_fusion.refs_0_.refs_4_), channel_id=1, source_target_pairs={{0,1},{1,2},{2,3},{3,0},{4,5},{5,6},{6,7},{7,4},{8,9},{9,10},{10,1... | collective-permute-start | bytes 1990664 | tf_op jit(solution)/shard_map/ppermute | solution.py:353
  41.1 30.1 %collective-permute-start.6 = (bf16[288,1152]{1,0:T(8,128)(2,1)S(1)}, bf16[288,1152]{1,0:T(8,128)(2,1)S(1)}, u32[]{:S(2)}, u32[]{:S(2)}) collective-permute-start(bf16[288,1152]{1,0:T(8,128)(2,1)S(1)} %pad_maximum_fusion.refs_0_.refs_4_), channel_id=1, source_target_pairs={{0,2},{1,3},{2,0},{3,1},{4,6},{5,7},{6,4},{7,5},{8,10},{9,11},{10,... | collective-permute-start | bytes 1990664 | tf_op jit(solution)/shard_map/ppermute | solution.py:353
  45.7 27.0 %collective-permute-start.5 = (bf16[288,1152]{1,0:T(8,128)(2,1)S(1)}, bf16[288,1152]{1,0:T(8,128)(2,1)S(1)}, u32[]{:S(2)}, u32[]{:S(2)}) collective-permute-start(bf16[288,1152]{1,0:T(8,128)(2,1)S(1)} %pad_maximum_fusion.refs_0_.refs_4_), channel_id=1, source_target_pairs={{0,3},{1,0},{2,1},{3,2},{4,7},{5,4},{6,5},{7,6},{8,11},{9,8},{10,9... | collective-permute-start | bytes 1990664 | tf_op jit(solution)/shard_map/ppermute | solution.py:353
  66.9 17.1 %collective-permute-start.4 = (bf16[4,64,1152]{2,1,0:T(8,128)(2,1)}, bf16[4,64,1152]{2,1,0:T(8,128)(2,1)S(1)}, u32[]{:S(2)}, u32[]{:S(2)}) collective-permute-start(bf16[4,64,1152]{2,1,0:T(8,128)(2,1)} %all-to-all-done.refs_0_), channel_id=1, source_target_pairs={{0,128},{128,0},{1,129},{129,1},{2,130},{130,2},{3,131},{131,3},{4... | collective-permute-start | bytes 1769480 | tf_op jit(solution)/shard_map/ppermute | solution.py:370
  69.5 3.2 %copy-start.9 = (bf16[288,1152]{1,0:T(8,128)(2,1)}, bf16[288,1152]{1,0:T(8,128)(2,1)S(1)}, u32[]{:S(2)}) copy-start(bf16[288,1152]{1,0:T(8,128)(2,1)S(1)} %collective-permute-done.7.refs_3_.refs_7_) | copy-start | bytes 1990660
  71.2 1.6 copy-start.10
  76.8 13.2 %collective-permute-start.3 = (bf16[4,64,1152]{2,1,0:T(8,128)(2,1)}, bf16[4,64,1152]{2,1,0:T(8,128)(2,1)S(1)}, u32[]{:S(2)}, u32[]{:S(2)}) collective-permute-start(bf16[4,64,1152]{2,1,0:T(8,128)(2,1)} %all-to-all-done.refs_0_), channel_id=1, source_target_pairs={{0,16},{16,0},{1,17},{17,1},{2,18},{18,2},{3,19},{19,3},{4,20},{20... | collective-permute-start | bytes 1769480 | tf_op jit(solution)/shard_map/ppermute | solution.py:367
  84.0 6.0 %copy-start.14 = (bf16[4,64,1152]{2,1,0:T(8,128)(2,1)}, bf16[4,64,1152]{2,1,0:T(8,128)(2,1)S(1)}, u32[]{:S(2)}) copy-start(bf16[4,64,1152]{2,1,0:T(8,128)(2,1)S(1)} %collective-permute-done.4.refs_2_) | copy-start | bytes 1769476
  84.0 6.0 %collective-permute-start.8 = (bf16[4,64,1152]{2,1,0:T(8,128)(2,1)S(1)}, bf16[4,64,1152]{2,1,0:T(8,128)(2,1)S(1)}, u32[]{:S(2)}, u32[]{:S(2)}) collective-permute-start(bf16[4,64,1152]{2,1,0:T(8,128)(2,1)S(1)} %collective-permute-done.4.refs_2_), channel_id=1, source_target_pairs={{0,16},{16,0},{1,17},{17,1},{2,18},{18,2},{3,19},{19,3},{4,20},{20... | collective-permute-start | bytes 1769480 | tf_op jit(solution)/shard_map/ppermute | solution.py:367
  85.9 15.1 %all-to-all-start.1 = ((bf16[4,288,288]{2,1,0:T(8,128)(2,1)}), bf16[4,288,288]{2,1,0:T(8,128)(2,1)S(1)}, u32[]{:S(2)}, u32[]{:S(2)}) async-start(bf16[4,288,288]{2,1,0:T(8,128)(2,1)} %shard_map.88), calls=%async_computation.1 | async-start | bytes 1769472 | tf_op jit(solution)/shard_map/all_to_all | solution.py:392
  101.0 7.3 %copy-start.8 = (bf16[4,288,288]{2,1,0:T(8,128)(2,1)}, bf16[4,288,288]{2,1,0:T(8,128)(2,1)S(1)}, u32[]{:S(2)}) copy-start(bf16[4,288,288]{2,1,0:T(8,128)(2,1)S(1)} %all-to-all-done.1.refs_8_) | copy-start | bytes 1990660
  101.0 19.2 %all-to-all-start.2 = ((bf16[8,36,1152]{2,1,0:T(8,128)(2,1)}), bf16[8,36,1152]{2,1,0:T(8,128)(2,1)S(1)}, u32[]{:S(2)}, u32[]{:S(2)}) async-start(bf16[8,36,1152]{2,1,0:T(8,128)(2,1)} %get-tuple-element.41), calls=%async_computation.2 | async-start | bytes 1474560 | tf_op jit(solution)/shard_map/all_to_all | solution.py:407
  120.2 6.5 %copy-start.12 = (f32[2,4,32,1152]{3,2,1,0:T(8,128)S(1)}, f32[2,4,32,1152]{3,2,1,0:T(8,128)}, u32[]{:S(2)}) copy-start(f32[2,4,32,1152]{3,2,1,0:T(8,128)} %get-tuple-element.39) | copy-start | bytes 3538948
  120.3 6.5 %collective-permute-start.9 = (bf16[2,4,32,1152]{3,2,1,0:T(8,128)(2,1)}, bf16[2,4,32,1152]{3,2,1,0:T(8,128)(2,1)S(1)}, u32[]{:S(2)}, u32[]{:S(2)}) collective-permute-start(bf16[2,4,32,1152]{3,2,1,0:T(8,128)(2,1)} %get-tuple-element.42), channel_id=1, source_target_pairs={{0,16},{16,0},{1,17},{17,1},{2,18},{18,2},{3,19},{19,3},{4,20},{20... | collective-permute-start | bytes 1769480 | tf_op jit(solution)/shard_map/ppermute | solution.py:367
  123.1 10.3 %all-to-all-start.3 = ((bf16[4,9,1152]{2,1,0:T(8,128)(2,1)}), bf16[4,9,1152]{2,1,0:T(8,128)(2,1)S(1)}, u32[]{:S(2)}, u32[]{:S(2)}) async-start(bf16[4,9,1152]{2,1,0:T(8,128)(2,1)} %reshape.601), calls=%async_computation.3 | async-start | bytes 294912 | tf_op jit(solution)/shard_map/all_to_all | solution.py:433
  133.4 13.9 %collective-permute-start.10 = (bf16[4,32,1152]{2,1,0:T(8,128)(2,1)S(1)}, bf16[4,32,1152]{2,1,0:T(8,128)(2,1)S(1)}, u32[]{:S(2)}, u32[]{:S(2)}) collective-permute-start(bf16[4,32,1152]{2,1,0:T(8,128)(2,1)S(1)} %fusion.3), channel_id=1, source_target_pairs={{0,128},{128,0},{1,129},{129,1},{2,130},{130,2},{3,131},{131,3},{4... | collective-permute-start | bytes 884744 | tf_op jit(solution)/shard_map/ppermute | solution.py:370
  137.7 9.6 %all-to-all-start.4 = ((bf16[8,3,1152]{2,1,0:T(4,128)(2,1)}), bf16[8,3,1152]{2,1,0:T(4,128)(2,1)S(1)}, u32[]{:S(2)}, u32[]{:S(2)}) async-start(bf16[8,3,1152]{2,1,0:T(4,128)(2,1)} %bitcast.11), calls=%async_computation.4 | async-start | bytes 147456 | tf_op jit(solution)/shard_map/all_to_all | solution.py:439
  147.5 38.3 %copy-start.2 = (bf16[1,1,128,1152]{3,2,1,0:T(8,128)(2,1)S(1)}, bf16[1,1,128,1152]{3,2,1,0:T(8,128)(2,1)}, u32[]{:S(2)}) copy-start(bf16[1,1,128,1152]{3,2,1,0:T(8,128)(2,1)} %param.7) | copy-start | bytes 884740
  147.5 38.3 %copy-start.4 = (bf16[1,1,128,1152]{3,2,1,0:T(8,128)(2,1)S(1)}, bf16[1,1,128,1152]{3,2,1,0:T(8,128)(2,1)}, u32[]{:S(2)}) copy-start(bf16[1,1,128,1152]{3,2,1,0:T(8,128)(2,1)} %param.10) | copy-start | bytes 884740
  147.5 38.3 %copy-start.6 = (s32[2]{0:T(128)S(1)}, s32[2]{0:T(128)}, u32[]{:S(2)}) copy-start(s32[2]{0:T(128)} %copy-done.5) | copy-start | bytes 28
  178.6 16.3 %all-to-all-start.6 = ((bf16[16,3,1152]{2,1,0:T(4,128)(2,1)}), bf16[16,3,1152]{2,1,0:T(4,128)(2,1)S(1)}, u32[]{:S(2)}, u32[]{:S(2)}) async-start(bf16[16,3,1152]{2,1,0:T(4,128)(2,1)} %broadcast_in_dim.35), calls=%async_computation.6 | async-start | bytes 294912 | tf_op jit(solution)/shard_map/all_to_all | solution.py:453
  (3 other events, 2.5 us)

commit v8 on v7

--- a/solution.py
+++ b/solution.py
@@ -373,9 +373,8 @@
         return lax.all_to_all(values, "zh", 0, 0, tiled=True)
 
     tables, tables_back = turn_tables(qk_gain, yl, core)
-    sent, _ = lax.optimization_barrier((sent, block))
+    sent, _, tables, tables_back = lax.optimization_barrier((sent, block, tables, tables_back))
     own = exchange(sent)
-    own, tables, tables_back = lax.optimization_barrier((own, tables, tables_back))
     across = other_y(own)
     near = other_core(own)
     w_back = pl.pallas_call(

time: 197 us -> 195 us (0.990)
  local copies, waits for them, and re-layouts: 9.59 us -> 7.55 us
    unnamed x37 -> x29, local copies, waits for them, and re-layouts: 4.49 us -> 1.68 us
    all_to_all x1, waiting for transfers between devices: 16.2 us -> 18.6 us  [exchange(): return lax.all_to_all(values, 'zh', 0, 0, tiled=True)]
  transfers between devices with their start and end apart: 17 -> 17, of which waited for: 9 -> 9; matrix products, arithmetic and copies ran while one was open for 2% -> 3% of each run, Pallas kernels for 14% -> 15%
where the time goes in v8:
time: 195 us; the launch traced here: 194 us
  starting transfers between devices  76.5 us (39%)
  waiting for transfers between devices  48.4 us (25%)
  Pallas kernels  30.3 us (16%)
  blocking collectives  28.8 us (15%)
  local copies, waits for them, and re-layouts  7.55 us (4%)
    all_to_all x1, blocking collectives, exchange(): return lax.all_to_all(values, 'zh', 0, 0, tiled=True)  28.8 us
    all_to_all x1, waiting for transfers between devices, exchange(): return lax.all_to_all(values, 'zh', 0, 0, tiled=True)  18.6 us
    ppermute x3, starting transfers between devices, on_device(): lax.ppermute(unit, ('zh', 'zl'), [(i, (i + 16 - step) % 16) for i in rang...  17.7 us
    pallas_call x1, Pallas kernels, on_device(): pl.pallas_call(chip_backward, out_shape=[jax.ShapeDtypeStruct((2, ZS, TOK...  11.9 us
    ppermute x3, starting transfers between devices, on_device(): lax.ppermute(block, 'x', [(i, (i + 4 - step) % 4) for i in range(4)])  11.4 us
    all_to_all x1, starting transfers between devices, exchange(): return lax.all_to_all(values, 'zh', 0, 0, tiled=True)  8.91 us
    pallas_call x1, Pallas kernels, on_device(): pl.pallas_call(chip_forward, out_shape=[wide] * 5 + [factors] * 2 + [jax....  8.46 us
    all_to_all x1, starting transfers between devices, on_device(): lax.all_to_all(jnp.broadcast_to(share[None], (16, 3, D)), CLIP, 0, 0, til...  7.3 us
  transfers between devices with their start and end apart: 17, of which 9 were waited for; matrix products, arithmetic and copies ran while one was open for 3% of the time, Pallas kernels for 15%

profile of v8, /device:TPU:24, one launch (start us, length us, event | category | flops | bytes accessed | tf_op | source)
XLA Modules:
  0.0 194.1 jit_solution(12831671954423600512)
XLA Ops:
  0.7 2.0 %shard_map.87 = bf16[72,1152]{1,0:T(8,128)(2,1)} custom-call(s32[1]{0:T(128)} %bitcast.6.place_ref, bf16[72,3456]{1,0:T(8,128)(2,1)} %w_qkv_ref.1, bf16[72,1152]{1,0:T(8,128)(2,1)} %w_out_ref.1), custom_call_target="tpu_custom_call" | custom-call | flops 1000000 | bytes 2000000 | tf_op jit(solution)/shard_map/pallas_call | solution.py:339
  2.7 3.8 %collective-permute-start.2 = (bf16[72,1152]{1,0:T(8,128)(2,1)}, bf16[72,1152]{1,0:T(8,128)(2,1)S(1)}, u32[]{:S(2)}, u32[]{:S(2)}) collective-permute-start(bf16[72,1152]{1,0:T(8,128)(2,1)} %shard_map.87), channel_id=1, source_target_pairs={{0,4},{4,8},{8,12},{12,32},{32,36},{36,40},{40,44},{44,64},{64,68}... | collective-permute-start | bytes 497672 | tf_op jit(solution)/shard_map/ppermute | solution.py:350
  6.5 10.9 %collective-permute-start.1 = (bf16[72,1152]{1,0:T(8,128)(2,1)}, bf16[72,1152]{1,0:T(8,128)(2,1)S(1)}, u32[]{:S(2)}, u32[]{:S(2)}) collective-permute-start(bf16[72,1152]{1,0:T(8,128)(2,1)} %shard_map.87), channel_id=1, source_target_pairs={{0,104},{4,108},{8,0},{12,4},{32,8},{36,12},{40,32},{44,36},{64,40... | collective-permute-start | bytes 497672 | tf_op jit(solution)/shard_map/ppermute | solution.py:350
  17.4 2.9 %collective-permute-start = (bf16[72,1152]{1,0:T(8,128)(2,1)}, bf16[72,1152]{1,0:T(8,128)(2,1)S(1)}, u32[]{:S(2)}, u32[]{:S(2)}) collective-permute-start(bf16[72,1152]{1,0:T(8,128)(2,1)} %shard_map.87), channel_id=1, source_target_pairs={{0,108},{4,0},{8,4},{12,8},{32,12},{36,32},{40,36},{44,40},{64,44}... | collective-permute-start | bytes 497672 | tf_op jit(solution)/shard_map/ppermute | solution.py:350
  24.5 2.5 %shard_map.86 = bf16[4,64,1152]{2,1,0:T(8,128)(2,1)} custom-call(f32[2]{0:T(128)S(1)} %pad_maximum_fusion.5.power_ref, s32[2]{0:T(128)S(1)} %pad_add_fusion.spot_ref, bf16[128,1152]{1,0:T(8,128)(2,1)S(1)} %bitcast.27, bf16[128,1152]{1,0:T(8,128)(2,1)S(1)} %bitcast.29, f32[3,1152]{1,0:T(4,128)S(1)} %bitcast.31), custom_call_target="tpu_custom_call" | custom-call | flops 2949120 | bytes 1179648 | tf_op jit(solution)/shard_map/pallas_call | solution.py:356
  27.9 8.9 %all-to-all-start = ((bf16[4,64,1152]{2,1,0:T(8,128)(2,1)}), bf16[4,64,1152]{2,1,0:T(8,128)(2,1)S(1)}, u32[]{:S(2)}, u32[]{:S(2)}) async-start(bf16[4,64,1152]{2,1,0:T(8,128)(2,1)} %shard_map.86), calls=%async_computation | async-start | bytes 1179648 | tf_op jit(solution)/shard_map/all_to_all | solution.py:373
  36.8 3.4 %collective-permute-start.7 = (bf16[288,1152]{1,0:T(8,128)(2,1)S(1)}, bf16[288,1152]{1,0:T(8,128)(2,1)S(1)}, u32[]{:S(2)}, u32[]{:S(2)}) collective-permute-start(bf16[288,1152]{1,0:T(8,128)(2,1)S(1)} %pad_maximum_fusion.refs_0_.refs_4_), channel_id=1, source_target_pairs={{0,1},{1,2},{2,3},{3,0},{4,5},{5,6},{6,7},{7,4},{8,9},{9,10},{10,1... | collective-permute-start | bytes 1990664 | tf_op jit(solution)/shard_map/ppermute | solution.py:353
  40.2 4.6 %collective-permute-start.6 = (bf16[288,1152]{1,0:T(8,128)(2,1)S(1)}, bf16[288,1152]{1,0:T(8,128)(2,1)S(1)}, u32[]{:S(2)}, u32[]{:S(2)}) collective-permute-start(bf16[288,1152]{1,0:T(8,128)(2,1)S(1)} %pad_maximum_fusion.refs_0_.refs_4_), channel_id=1, source_target_pairs={{0,2},{1,3},{2,0},{3,1},{4,6},{5,7},{6,4},{7,5},{8,10},{9,11},{10,... | collective-permute-start | bytes 1990664 | tf_op jit(solution)/shard_map/ppermute | solution.py:353
  44.9 3.3 %collective-permute-start.5 = (bf16[288,1152]{1,0:T(8,128)(2,1)S(1)}, bf16[288,1152]{1,0:T(8,128)(2,1)}, u32[]{:S(2)}, u32[]{:S(2)}) collective-permute-start(bf16[288,1152]{1,0:T(8,128)(2,1)S(1)} %pad_maximum_fusion.refs_0_.refs_4_), channel_id=1, source_target_pairs={{0,3},{1,0},{2,1},{3,2},{4,7},{5,4},{6,5},{7,6},{8,11},{9,8},{10,9... | collective-permute-start | bytes 1990664 | tf_op jit(solution)/shard_map/ppermute | solution.py:353
  48.2 18.6 %all-to-all-done.refs_0_ = bf16[4,64,1152]{2,1,0:T(8,128)(2,1)S(1)} async-done(((bf16[4,64,1152]{2,1,0:T(8,128)(2,1)}), bf16[4,64,1152]{2,1,0:T(8,128)(2,1)S(1)}, u32[]{:S(2)}, u32[]{:S(2)}) %all-to-all-start) | async-done | bytes 589856 | tf_op jit(solution)/shard_map/all_to_all | solution.py:373
  66.9 2.6 %collective-permute-start.4 = (bf16[4,64,1152]{2,1,0:T(8,128)(2,1)S(1)}, bf16[4,64,1152]{2,1,0:T(8,128)(2,1)}, u32[]{:S(2)}, u32[]{:S(2)}) collective-permute-start(bf16[4,64,1152]{2,1,0:T(8,128)(2,1)S(1)} %all-to-all-done.refs_0_), channel_id=1, source_target_pairs={{0,128},{128,0},{1,129},{129,1},{2,130},{130,2},{3,131},{131,3},{4... | collective-permute-start | bytes 1769480 | tf_op jit(solution)/shard_map/ppermute | solution.py:370
  69.5 0.8 collective-permute-done.6.refs_2_.refs_6_
  70.4 1.7 collective-permute-done.5.refs_1_.refs_5_
  72.0 3.2 %shard_map.88 = bf16[4,288,288]{2,1,0:T(8,128)(2,1)} custom-call(s32[2]{0:T(128)} %copy-done.3, bf16[288,1152]{1,0:T(8,128)(2,1)} %copy-done.5, bf16[288,1152]{1,0:T(8,128)(2,1)} %collective-permute-done.5.refs_1_.refs_5_, bf16[288,1152]{1,0:T(8,128)(2,1)} %copy-done.8, bf16[288,1152]{1,0:T(8,128)(2,1)} %copy-done.7), custom_call_target="tpu_custom_call" | custom-call | flops 1000000 | bytes 2000000 | tf_op jit(solution)/shard_map/pallas_call | solution.py:380
  75.2 1.9 collective-permute-start.3
  77.1 6.7 %collective-permute-done.4.refs_2_ = bf16[4,64,1152]{2,1,0:T(8,128)(2,1)} collective-permute-done((bf16[4,64,1152]{2,1,0:T(8,128)(2,1)S(1)}, bf16[4,64,1152]{2,1,0:T(8,128)(2,1)}, u32[]{:S(2)}, u32[]{:S(2)}) %collective-permute-start.4) | collective-permute-done | bytes 589856 | tf_op jit(solution)/shard_map/ppermute | solution.py:370
  83.8 1.9 collective-permute-start.8
  85.8 4.1 %all-to-all-start.1 = ((bf16[4,288,288]{2,1,0:T(8,128)(2,1)}), bf16[4,288,288]{2,1,0:T(8,128)(2,1)S(1)}, u32[]{:S(2)}, u32[]{:S(2)}) async-start(bf16[4,288,288]{2,1,0:T(8,128)(2,1)} %shard_map.88), calls=%async_computation.1 | async-start | bytes 1769472 | tf_op jit(solution)/shard_map/all_to_all | solution.py:391
  91.5 8.5 %shard_map.89 = (bf16[512,384]{1,0:T(8,128)(2,1)}, bf16[512,384]{1,0:T(8,128)(2,1)}, bf16[512,384]{1,0:T(8,128)(2,1)}, bf16[512,384]{1,0:T(8,128)(2,1)}, bf16[51...) custom-call(bf16[4,64,1152]{2,1,0:T(8,128)(2,1)} %copy-done.9, ...), custom_call_target="tpu_custom_call" | custom-call | flops 1698693120 | bytes 12000000 | tf_op jit(solution)/shard_map/pallas_call | solution.py:395
  100.0 0.9 all-to-all-done.1.refs_8_
  100.9 7.3 %all-to-all-start.2 = ((bf16[8,36,1152]{2,1,0:T(8,128)(2,1)}), bf16[8,36,1152]{2,1,0:T(8,128)(2,1)S(1)}, u32[]{:S(2)}, u32[]{:S(2)}) async-start(bf16[8,36,1152]{2,1,0:T(8,128)(2,1)} %get-tuple-element.39), calls=%async_computation.2 | async-start | bytes 1474560 | tf_op jit(solution)/shard_map/all_to_all | solution.py:406
  108.2 11.9 %shard_map.90 = (f32[2,4,32,1152]{3,2,1,0:T(8,128)}, bf16[2,4,32,1152]{3,2,1,0:T(8,128)(2,1)}) custom-call(bf16[4,64,1152]{2,1,0:T(8,128)(2,1)} %copy-done.9, bf16[4,64,1152]{2,1,0:T(8,128)(2,1)} %copy-done.12, bf16[4,64,1152]{2,1,0:T(8,128)(2,1)} %collective-permute-done.4.refs_2_, bf16[4,64,1152]{2,1,0:T(8,128)(2,1)} %copy-done.13, ...), custom_call_target="tpu_custom_call" | custom-call | flops 1358954496 | bytes 14000000 | tf_op jit(solution)/shard_map/pallas_call | solution.py:408
  120.1 2.1 %collective-permute-start.9 = (bf16[2,4,32,1152]{3,2,1,0:T(8,128)(2,1)}, bf16[2,4,32,1152]{3,2,1,0:T(8,128)(2,1)S(1)}, u32[]{:S(2)}, u32[]{:S(2)}) collective-permute-start(bf16[2,4,32,1152]{3,2,1,0:T(8,128)(2,1)} %get-tuple-element.40), channel_id=1, source_target_pairs={{0,16},{16,0},{1,17},{17,1},{2,18},{18,2},{3,19},{19,3},{4,20},{20... | collective-permute-start | bytes 1769480 | tf_op jit(solution)/shard_map/ppermute | solution.py:367
  123.0 3.6 %all-to-all-start.3 = ((bf16[4,9,1152]{2,1,0:T(8,128)(2,1)}), bf16[4,9,1152]{2,1,0:T(8,128)(2,1)S(1)}, u32[]{:S(2)}, u32[]{:S(2)}) async-start(bf16[4,9,1152]{2,1,0:T(8,128)(2,1)} %reshape.601), calls=%async_computation.3 | async-start | bytes 294912 | tf_op jit(solution)/shard_map/all_to_all | solution.py:432
  126.6 6.6 %all-to-all-done.3 = bf16[4,9,1152]{2,1,0:T(8,128)(2,1)S(1)} async-done(((bf16[4,9,1152]{2,1,0:T(8,128)(2,1)}), bf16[4,9,1152]{2,1,0:T(8,128)(2,1)S(1)}, u32[]{:S(2)}, u32[]{:S(2)}) %all-to-all-start.3) | async-done | bytes 82976 | tf_op jit(solution)/shard_map/all_to_all | solution.py:432
  133.3 3.6 %collective-permute-start.10 = (bf16[4,32,1152]{2,1,0:T(8,128)(2,1)S(1)}, bf16[4,32,1152]{2,1,0:T(8,128)(2,1)S(1)}, u32[]{:S(2)}, u32[]{:S(2)}) collective-permute-start(bf16[4,32,1152]{2,1,0:T(8,128)(2,1)S(1)} %fusion.3), channel_id=1, source_target_pairs={{0,128},{128,0},{1,129},{129,1},{2,130},{130,2},{3,131},{131,3},{4... | collective-permute-start | bytes 884744 | tf_op jit(solution)/shard_map/ppermute | solution.py:370
  137.6 4.2 %all-to-all-start.4 = ((bf16[8,3,1152]{2,1,0:T(4,128)(2,1)}), bf16[8,3,1152]{2,1,0:T(4,128)(2,1)S(1)}, u32[]{:S(2)}, u32[]{:S(2)}) async-start(bf16[8,3,1152]{2,1,0:T(4,128)(2,1)} %bitcast.11), calls=%async_computation.4 | async-start | bytes 147456 | tf_op jit(solution)/shard_map/all_to_all | solution.py:438
  141.8 5.4 %all-to-all-done.4 = bf16[8,3,1152]{2,1,0:T(4,128)(2,1)S(1)} async-done(((bf16[8,3,1152]{2,1,0:T(4,128)(2,1)}), bf16[8,3,1152]{2,1,0:T(4,128)(2,1)S(1)}, u32[]{:S(2)}, u32[]{:S(2)}) %all-to-all-start.4) | async-done | bytes 55328 | tf_op jit(solution)/shard_map/all_to_all | solution.py:438
  147.4 28.8 %all_to_all.35.back_ref = bf16[4,40,1152]{2,1,0:T(8,128)(2,1)S(1)} all-to-all(bf16[4,40,1152]{2,1,0:T(8,128)(2,1)S(1)} %fusion.2), channel_id=1, replica_groups=mesh['yh'=2,'yl'=2,'zh'=4,'c'=2,'zl'=4,'x'=4] {'zh'}, dimensions={0} | all-to-all | bytes 737280 | tf_op jit(solution)/shard_map/all_to_all | solution.py:373
  176.9 7.3 %all-to-all-start.6 = ((bf16[16,3,1152]{2,1,0:T(4,128)(2,1)}), bf16[16,3,1152]{2,1,0:T(4,128)(2,1)S(1)}, u32[]{:S(2)}, u32[]{:S(2)}) async-start(bf16[16,3,1152]{2,1,0:T(4,128)(2,1)} %broadcast_in_dim.35), calls=%async_computation.6 | async-start | bytes 294912 | tf_op jit(solution)/shard_map/all_to_all | solution.py:452
  184.3 2.3 %shard_map.91 = bf16[128,1152]{1,0:T(8,128)(2,1)} custom-call(f32[2]{0:T(128)S(1)} %pad_maximum_fusion.5.power_ref, s32[2]{0:T(128)S(1)} %copy-done.4, bf16[128,1152]{1,0:T(8,128)(2,1)S(1)} %bitcast.28, bf16[128,1152]{1,0:T(8,128)(2,1)S(1)} %bitcast.30, f32[3,1152]{1,0:T(4,128)S(1)} %bitcast.32, bf16[4,40,1152]{2,1,0:T(8,128)(2,1)S(1)} %all_to_all.35.back_ref), custom_call_target="tpu_custom_call" | custom-call | flops 4423680 | bytes 1179648 | tf_op jit(solution)/shard_map/pallas_call | solution.py:442
  186.5 6.8 %all-to-all-done.6 = bf16[16,3,1152]{2,1,0:T(4,128)(2,1)S(1)} async-done(((bf16[16,3,1152]{2,1,0:T(4,128)(2,1)}), bf16[16,3,1152]{2,1,0:T(4,128)(2,1)S(1)}, u32[]{:S(2)}, u32[]{:S(2)}) %all-to-all-start.6) | async-done | bytes 110624 | tf_op jit(solution)/shard_map/all_to_all | solution.py:452
  (77 shorter events, 9.2 us)
Async XLA Ops:
  0.6 21.2 %copy-start = (f32[1,2,3,1152]{3,1,2,0:T(2,128)S(1)}, f32[1,2,3,1152]{3,1,2,0:T(2,128)}, u32[]{:S(2)}) copy-start(f32[1,2,3,1152]{3,1,2,0:T(2,128)} %param.9) | copy-start | bytes 82948
  0.7 23.9 %copy-start.1 = (bf16[1,1,128,1152]{3,2,1,0:T(8,128)(2,1)S(1)}, bf16[1,1,128,1152]{3,2,1,0:T(8,128)(2,1)}, u32[]{:S(2)}) copy-start(bf16[1,1,128,1152]{3,2,1,0:T(8,128)(2,1)} %param.7) | copy-start | bytes 884740
  0.7 23.9 %copy-start.2 = (bf16[1,1,128,1152]{3,2,1,0:T(8,128)(2,1)S(1)}, bf16[1,1,128,1152]{3,2,1,0:T(8,128)(2,1)}, u32[]{:S(2)}) copy-start(bf16[1,1,128,1152]{3,2,1,0:T(8,128)(2,1)} %param.10) | copy-start | bytes 884740
  2.7 24.4 %collective-permute-start.2 = (bf16[72,1152]{1,0:T(8,128)(2,1)}, bf16[72,1152]{1,0:T(8,128)(2,1)S(1)}, u32[]{:S(2)}, u32[]{:S(2)}) collective-permute-start(bf16[72,1152]{1,0:T(8,128)(2,1)} %shard_map.87), channel_id=1, source_target_pairs={{0,4},{4,8},{8,12},{12,32},{32,36},{36,40},{40,44},{44,64},{64,68}... | collective-permute-start | bytes 497672 | tf_op jit(solution)/shard_map/ppermute | solution.py:350
  6.5 20.5 %collective-permute-start.1 = (bf16[72,1152]{1,0:T(8,128)(2,1)}, bf16[72,1152]{1,0:T(8,128)(2,1)S(1)}, u32[]{:S(2)}, u32[]{:S(2)}) collective-permute-start(bf16[72,1152]{1,0:T(8,128)(2,1)} %shard_map.87), channel_id=1, source_target_pairs={{0,104},{4,108},{8,0},{12,4},{32,8},{36,12},{40,32},{44,36},{64,40... | collective-permute-start | bytes 497672 | tf_op jit(solution)/shard_map/ppermute | solution.py:350
  17.4 10.4 %collective-permute-start = (bf16[72,1152]{1,0:T(8,128)(2,1)}, bf16[72,1152]{1,0:T(8,128)(2,1)S(1)}, u32[]{:S(2)}, u32[]{:S(2)}) collective-permute-start(bf16[72,1152]{1,0:T(8,128)(2,1)} %shard_map.87), channel_id=1, source_target_pairs={{0,108},{4,0},{8,4},{12,8},{32,12},{36,32},{40,36},{44,40},{64,44}... | collective-permute-start | bytes 497672 | tf_op jit(solution)/shard_map/ppermute | solution.py:350
  22.2 4.9 %copy-start.3 = (s32[2]{0:T(128)}, s32[2]{0:T(128)S(1)}, u32[]{:S(2)}) copy-start(s32[2]{0:T(128)S(1)} %pad_add_fusion.spot_ref) | copy-start | bytes 28
  22.8 5.0 %copy-start.11 = (bf16[72,1152]{1,0:T(8,128)(2,1)S(1)}, bf16[72,1152]{1,0:T(8,128)(2,1)}, u32[]{:S(2)}) copy-start(bf16[72,1152]{1,0:T(8,128)(2,1)} %shard_map.87) | copy-start | bytes 497668
  27.9 44.1 %copy-start.5 = (bf16[288,1152]{1,0:T(8,128)(2,1)}, bf16[288,1152]{1,0:T(8,128)(2,1)S(1)}, u32[]{:S(2)}) copy-start(bf16[288,1152]{1,0:T(8,128)(2,1)S(1)} %pad_maximum_fusion.refs_0_.refs_4_) | copy-start | bytes 1990660
  27.9 38.9 %all-to-all-start = ((bf16[4,64,1152]{2,1,0:T(8,128)(2,1)}), bf16[4,64,1152]{2,1,0:T(8,128)(2,1)S(1)}, u32[]{:S(2)}, u32[]{:S(2)}) async-start(bf16[4,64,1152]{2,1,0:T(8,128)(2,1)} %shard_map.86), calls=%async_computation | async-start | bytes 1179648 | tf_op jit(solution)/shard_map/all_to_all | solution.py:373
  36.8 32.7 %collective-permute-start.7 = (bf16[288,1152]{1,0:T(8,128)(2,1)S(1)}, bf16[288,1152]{1,0:T(8,128)(2,1)S(1)}, u32[]{:S(2)}, u32[]{:S(2)}) collective-permute-start(bf16[288,1152]{1,0:T(8,128)(2,1)S(1)} %pad_maximum_fusion.refs_0_.refs_4_), channel_id=1, source_target_pairs={{0,1},{1,2},{2,3},{3,0},{4,5},{5,6},{6,7},{7,4},{8,9},{9,10},{10,1... | collective-permute-start | bytes 1990664 | tf_op jit(solution)/shard_map/ppermute | solution.py:353
  40.2 30.1 %collective-permute-start.6 = (bf16[288,1152]{1,0:T(8,128)(2,1)S(1)}, bf16[288,1152]{1,0:T(8,128)(2,1)S(1)}, u32[]{:S(2)}, u32[]{:S(2)}) collective-permute-start(bf16[288,1152]{1,0:T(8,128)(2,1)S(1)} %pad_maximum_fusion.refs_0_.refs_4_), channel_id=1, source_target_pairs={{0,2},{1,3},{2,0},{3,1},{4,6},{5,7},{6,4},{7,5},{8,10},{9,11},{10,... | collective-permute-start | bytes 1990664 | tf_op jit(solution)/shard_map/ppermute | solution.py:353
  44.9 27.1 %collective-permute-start.5 = (bf16[288,1152]{1,0:T(8,128)(2,1)S(1)}, bf16[288,1152]{1,0:T(8,128)(2,1)}, u32[]{:S(2)}, u32[]{:S(2)}) collective-permute-start(bf16[288,1152]{1,0:T(8,128)(2,1)S(1)} %pad_maximum_fusion.refs_0_.refs_4_), channel_id=1, source_target_pairs={{0,3},{1,0},{2,1},{3,2},{4,7},{5,4},{6,5},{7,6},{8,11},{9,8},{10,9... | collective-permute-start | bytes 1990664 | tf_op jit(solution)/shard_map/ppermute | solution.py:353
  66.9 23.0 %copy-start.9 = (bf16[4,64,1152]{2,1,0:T(8,128)(2,1)}, bf16[4,64,1152]{2,1,0:T(8,128)(2,1)S(1)}, u32[]{:S(2)}) copy-start(bf16[4,64,1152]{2,1,0:T(8,128)(2,1)S(1)} %all-to-all-done.refs_0_) | copy-start | bytes 1769476
  66.9 17.0 %collective-permute-start.4 = (bf16[4,64,1152]{2,1,0:T(8,128)(2,1)S(1)}, bf16[4,64,1152]{2,1,0:T(8,128)(2,1)}, u32[]{:S(2)}, u32[]{:S(2)}) collective-permute-start(bf16[4,64,1152]{2,1,0:T(8,128)(2,1)S(1)} %all-to-all-done.refs_0_), channel_id=1, source_target_pairs={{0,128},{128,0},{1,129},{129,1},{2,130},{130,2},{3,131},{131,3},{4... | collective-permute-start | bytes 1769480 | tf_op jit(solution)/shard_map/ppermute | solution.py:370
  69.5 2.5 %copy-start.7 = (bf16[288,1152]{1,0:T(8,128)(2,1)}, bf16[288,1152]{1,0:T(8,128)(2,1)S(1)}, u32[]{:S(2)}) copy-start(bf16[288,1152]{1,0:T(8,128)(2,1)S(1)} %collective-permute-done.7.refs_3_.refs_7_) | copy-start | bytes 1990660
  70.3 1.7 copy-start.8
  75.2 14.7 %collective-permute-start.3 = (bf16[4,64,1152]{2,1,0:T(8,128)(2,1)S(1)}, bf16[4,64,1152]{2,1,0:T(8,128)(2,1)S(1)}, u32[]{:S(2)}, u32[]{:S(2)}) collective-permute-start(bf16[4,64,1152]{2,1,0:T(8,128)(2,1)S(1)} %all-to-all-done.refs_0_), channel_id=1, source_target_pairs={{0,16},{16,0},{1,17},{17,1},{2,18},{18,2},{3,19},{19,3},{4,20},{20... | collective-permute-start | bytes 1769480 | tf_op jit(solution)/shard_map/ppermute | solution.py:367
  83.8 6.0 %collective-permute-start.8 = (bf16[4,64,1152]{2,1,0:T(8,128)(2,1)}, bf16[4,64,1152]{2,1,0:T(8,128)(2,1)S(1)}, u32[]{:S(2)}, u32[]{:S(2)}) collective-permute-start(bf16[4,64,1152]{2,1,0:T(8,128)(2,1)} %collective-permute-done.4.refs_2_), channel_id=1, source_target_pairs={{0,16},{16,0},{1,17},{17,1},{2,18},{18,2},{3,19},{19,3},{4,20},{20... | collective-permute-start | bytes 1769480 | tf_op jit(solution)/shard_map/ppermute | solution.py:367
  85.8 15.1 %all-to-all-start.1 = ((bf16[4,288,288]{2,1,0:T(8,128)(2,1)}), bf16[4,288,288]{2,1,0:T(8,128)(2,1)S(1)}, u32[]{:S(2)}, u32[]{:S(2)}) async-start(bf16[4,288,288]{2,1,0:T(8,128)(2,1)} %shard_map.88), calls=%async_computation.1 | async-start | bytes 1769472 | tf_op jit(solution)/shard_map/all_to_all | solution.py:391
  89.9 0.8 copy-start.12
  90.7 0.8 copy-start.13
  100.9 7.3 %copy-start.6 = (bf16[4,288,288]{2,1,0:T(8,128)(2,1)}, bf16[4,288,288]{2,1,0:T(8,128)(2,1)S(1)}, u32[]{:S(2)}) copy-start(bf16[4,288,288]{2,1,0:T(8,128)(2,1)S(1)} %all-to-all-done.1.refs_8_) | copy-start | bytes 1990660
  100.9 19.2 %all-to-all-start.2 = ((bf16[8,36,1152]{2,1,0:T(8,128)(2,1)}), bf16[8,36,1152]{2,1,0:T(8,128)(2,1)S(1)}, u32[]{:S(2)}, u32[]{:S(2)}) async-start(bf16[8,36,1152]{2,1,0:T(8,128)(2,1)} %get-tuple-element.39), calls=%async_computation.2 | async-start | bytes 1474560 | tf_op jit(solution)/shard_map/all_to_all | solution.py:406
  120.1 6.5 %copy-start.10 = (f32[2,4,32,1152]{3,2,1,0:T(8,128)S(1)}, f32[2,4,32,1152]{3,2,1,0:T(8,128)}, u32[]{:S(2)}) copy-start(f32[2,4,32,1152]{3,2,1,0:T(8,128)} %get-tuple-element.37) | copy-start | bytes 3538948
  120.1 6.5 %collective-permute-start.9 = (bf16[2,4,32,1152]{3,2,1,0:T(8,128)(2,1)}, bf16[2,4,32,1152]{3,2,1,0:T(8,128)(2,1)S(1)}, u32[]{:S(2)}, u32[]{:S(2)}) collective-permute-start(bf16[2,4,32,1152]{3,2,1,0:T(8,128)(2,1)} %get-tuple-element.40), channel_id=1, source_target_pairs={{0,16},{16,0},{1,17},{17,1},{2,18},{18,2},{3,19},{19,3},{4,20},{20... | collective-permute-start | bytes 1769480 | tf_op jit(solution)/shard_map/ppermute | solution.py:367
  123.0 10.3 %all-to-all-start.3 = ((bf16[4,9,1152]{2,1,0:T(8,128)(2,1)}), bf16[4,9,1152]{2,1,0:T(8,128)(2,1)S(1)}, u32[]{:S(2)}, u32[]{:S(2)}) async-start(bf16[4,9,1152]{2,1,0:T(8,128)(2,1)} %reshape.601), calls=%async_computation.3 | async-start | bytes 294912 | tf_op jit(solution)/shard_map/all_to_all | solution.py:432
  133.3 14.0 %collective-permute-start.10 = (bf16[4,32,1152]{2,1,0:T(8,128)(2,1)S(1)}, bf16[4,32,1152]{2,1,0:T(8,128)(2,1)S(1)}, u32[]{:S(2)}, u32[]{:S(2)}) collective-permute-start(bf16[4,32,1152]{2,1,0:T(8,128)(2,1)S(1)} %fusion.3), channel_id=1, source_target_pairs={{0,128},{128,0},{1,129},{129,1},{2,130},{130,2},{3,131},{131,3},{4... | collective-permute-start | bytes 884744 | tf_op jit(solution)/shard_map/ppermute | solution.py:370
  137.6 9.6 %all-to-all-start.4 = ((bf16[8,3,1152]{2,1,0:T(4,128)(2,1)}), bf16[8,3,1152]{2,1,0:T(4,128)(2,1)S(1)}, u32[]{:S(2)}, u32[]{:S(2)}) async-start(bf16[8,3,1152]{2,1,0:T(4,128)(2,1)} %bitcast.11), calls=%async_computation.4 | async-start | bytes 147456 | tf_op jit(solution)/shard_map/all_to_all | solution.py:438
  147.3 36.9 %copy-start.4 = (s32[2]{0:T(128)S(1)}, s32[2]{0:T(128)}, u32[]{:S(2)}) copy-start(s32[2]{0:T(128)} %copy-done.3) | copy-start | bytes 28
  176.9 16.4 %all-to-all-start.6 = ((bf16[16,3,1152]{2,1,0:T(4,128)(2,1)}), bf16[16,3,1152]{2,1,0:T(4,128)(2,1)S(1)}, u32[]{:S(2)}, u32[]{:S(2)}) async-start(bf16[16,3,1152]{2,1,0:T(4,128)(2,1)} %broadcast_in_dim.35), calls=%async_computation.6 | async-start | bytes 294912 | tf_op jit(solution)/shard_map/all_to_all | solution.py:452

commit v9 on v8

--- a/solution.py
+++ b/solution.py
@@ -342,7 +342,7 @@
         in_specs=[smem, vmem, vmem],
         out_specs=vmem,
         scratch_shapes=[pltpu.VMEM((HD, 4 * PART), F32)],
-        compiler_params=PARAMS,
+        compiler_params=SMALL,
         cost_estimate=cost(10**6, 2 * 10**6),
     )((2 * yl + core)[None], w_qkv, w_out)
     block = jnp.concatenate(
@@ -383,7 +383,7 @@
         in_specs=[smem] + [hbm] * 4,
         out_specs=vmem,
         scratch_shapes=[pltpu.VMEM((4, PART, 384), BF16), pltpu.VMEM((16, HD, PART), F32), four],
-        compiler_params=PARAMS,
+        compiler_params=SMALL,
         cost_estimate=cost(10**6, 2 * 10**6),
     )(spot, *blocks)
     across, w_back = lax.optimization_barrier((across, w_back))

time: 195 us -> 196 us (level)
  Pallas kernels: 30.3 us -> 27.6 us
  transfers between devices with their start and end apart: 17 -> 17, of which waited for: 9 -> 9; matrix products, arithmetic and copies ran while one was open for 3% -> 3% of each run, Pallas kernels for 15% -> 14%
where the time goes in v9:
time: 196 us; the launch traced here: 194 us
  starting transfers between devices  76.8 us (39%)
  waiting for transfers between devices  50.2 us (26%)
  blocking collectives  28.7 us (15%)
  Pallas kernels  27.6 us (14%)
  local copies, waits for them, and re-layouts  8.67 us (4%)
    all_to_all x1, blocking collectives, exchange(): return lax.all_to_all(values, 'zh', 0, 0, tiled=True)  28.7 us
    all_to_all x1, waiting for transfers between devices, exchange(): return lax.all_to_all(values, 'zh', 0, 0, tiled=True)  18.7 us
    ppermute x3, starting transfers between devices, on_device(): lax.ppermute(unit, ('zh', 'zl'), [(i, (i + 16 - step) % 16) for i in rang...  17.7 us
    pallas_call x1, Pallas kernels, on_device(): pl.pallas_call(chip_backward, out_shape=[jax.ShapeDtypeStruct((2, ZS, TOK...  12 us
    ppermute x3, starting transfers between devices, on_device(): lax.ppermute(block, 'x', [(i, (i + 4 - step) % 4) for i in range(4)])  11.4 us
    all_to_all x1, starting transfers between devices, exchange(): return lax.all_to_all(values, 'zh', 0, 0, tiled=True)  9.01 us
    pallas_call x1, Pallas kernels, on_device(): pl.pallas_call(chip_forward, out_shape=[wide] * 5 + [factors] * 2 + [jax....  8.47 us
    ppermute x2, waiting for transfers between devices, other_y(): return lax.ppermute(values, 'yl', [(0, 1), (1, 0)])  8.05 us
  transfers between devices with their start and end apart: 17, of which 9 were waited for; matrix products, arithmetic and copies ran while one was open for 3% of the time, Pallas kernels for 14%

profile of v9, /device:TPU:24, one launch (start us, length us, event | category | flops | bytes accessed | tf_op | source)
XLA Modules:
  0.0 194.5 jit_solution(2336485411062116949)
XLA Ops:
  0.7 1.0 copy-done.7
  1.7 0.9 copy-done.8
  2.8 3.8 %collective-permute-start.2 = (bf16[72,1152]{1,0:T(8,128)(2,1)S(1)}, bf16[72,1152]{1,0:T(8,128)(2,1)S(1)}, u32[]{:S(2)}, u32[]{:S(2)}) collective-permute-start(bf16[72,1152]{1,0:T(8,128)(2,1)S(1)} %shard_map.87), channel_id=1, source_target_pairs={{0,4},{4,8},{8,12},{12,32},{32,36},{36,40},{40,44},{44,64},{64,68}... | collective-permute-start | bytes 497672 | tf_op jit(solution)/shard_map/ppermute | solution.py:350
  6.6 10.9 %collective-permute-start.1 = (bf16[72,1152]{1,0:T(8,128)(2,1)S(1)}, bf16[72,1152]{1,0:T(8,128)(2,1)S(1)}, u32[]{:S(2)}, u32[]{:S(2)}) collective-permute-start(bf16[72,1152]{1,0:T(8,128)(2,1)S(1)} %shard_map.87), channel_id=1, source_target_pairs={{0,104},{4,108},{8,0},{12,4},{32,8},{36,12},{40,32},{44,36},{64,40... | collective-permute-start | bytes 497672 | tf_op jit(solution)/shard_map/ppermute | solution.py:350
  17.6 2.9 %collective-permute-start = (bf16[72,1152]{1,0:T(8,128)(2,1)S(1)}, bf16[72,1152]{1,0:T(8,128)(2,1)S(1)}, u32[]{:S(2)}, u32[]{:S(2)}) collective-permute-start(bf16[72,1152]{1,0:T(8,128)(2,1)S(1)} %shard_map.87), channel_id=1, source_target_pairs={{0,108},{4,0},{8,4},{12,8},{32,12},{36,32},{40,36},{44,40},{64,44}... | collective-permute-start | bytes 497672 | tf_op jit(solution)/shard_map/ppermute | solution.py:350
  24.7 2.5 %shard_map.86 = bf16[4,64,1152]{2,1,0:T(8,128)(2,1)} custom-call(f32[2]{0:T(128)S(1)} %pad_maximum_fusion.5.power_ref, s32[2]{0:T(128)S(1)} %pad_add_fusion.spot_ref, bf16[128,1152]{1,0:T(8,128)(2,1)S(1)} %bitcast.27, bf16[128,1152]{1,0:T(8,128)(2,1)S(1)} %bitcast.29, f32[3,1152]{1,0:T(4,128)S(1)} %bitcast.31), custom_call_target="tpu_custom_call" | custom-call | flops 2949120 | bytes 1179648 | tf_op jit(solution)/shard_map/pallas_call | solution.py:356
  27.8 9.0 %all-to-all-start = ((bf16[4,64,1152]{2,1,0:T(8,128)(2,1)}), bf16[4,64,1152]{2,1,0:T(8,128)(2,1)}, u32[]{:S(2)}, u32[]{:S(2)}) async-start(bf16[4,64,1152]{2,1,0:T(8,128)(2,1)} %shard_map.86), calls=%async_computation | async-start | bytes 1179648 | tf_op jit(solution)/shard_map/all_to_all | solution.py:373
  36.8 3.4 %collective-permute-start.7 = (bf16[288,1152]{1,0:T(8,128)(2,1)S(1)}, bf16[288,1152]{1,0:T(8,128)(2,1)S(1)}, u32[]{:S(2)}, u32[]{:S(2)}) collective-permute-start(bf16[288,1152]{1,0:T(8,128)(2,1)S(1)} %pad_maximum_fusion.refs_0_.refs_4_), channel_id=1, source_target_pairs={{0,1},{1,2},{2,3},{3,0},{4,5},{5,6},{6,7},{7,4},{8,9},{9,10},{10,1... | collective-permute-start | bytes 1990664 | tf_op jit(solution)/shard_map/ppermute | solution.py:353
  40.2 4.6 %collective-permute-start.6 = (bf16[288,1152]{1,0:T(8,128)(2,1)S(1)}, bf16[288,1152]{1,0:T(8,128)(2,1)S(1)}, u32[]{:S(2)}, u32[]{:S(2)}) collective-permute-start(bf16[288,1152]{1,0:T(8,128)(2,1)S(1)} %pad_maximum_fusion.refs_0_.refs_4_), channel_id=1, source_target_pairs={{0,2},{1,3},{2,0},{3,1},{4,6},{5,7},{6,4},{7,5},{8,10},{9,11},{10,... | collective-permute-start | bytes 1990664 | tf_op jit(solution)/shard_map/ppermute | solution.py:353
  44.8 3.3 %collective-permute-start.5 = (bf16[288,1152]{1,0:T(8,128)(2,1)S(1)}, bf16[288,1152]{1,0:T(8,128)(2,1)S(1)}, u32[]{:S(2)}, u32[]{:S(2)}) collective-permute-start(bf16[288,1152]{1,0:T(8,128)(2,1)S(1)} %pad_maximum_fusion.refs_0_.refs_4_), channel_id=1, source_target_pairs={{0,3},{1,0},{2,1},{3,2},{4,7},{5,4},{6,5},{7,6},{8,11},{9,8},{10,9... | collective-permute-start | bytes 1990664 | tf_op jit(solution)/shard_map/ppermute | solution.py:353
  48.2 18.7 %all-to-all-done.refs_0_ = bf16[4,64,1152]{2,1,0:T(8,128)(2,1)} async-done(((bf16[4,64,1152]{2,1,0:T(8,128)(2,1)}), bf16[4,64,1152]{2,1,0:T(8,128)(2,1)}, u32[]{:S(2)}, u32[]{:S(2)}) %all-to-all-start) | async-done | bytes 589856 | tf_op jit(solution)/shard_map/all_to_all | solution.py:373
  66.9 2.6 %collective-permute-start.4 = (bf16[4,64,1152]{2,1,0:T(8,128)(2,1)}, bf16[4,64,1152]{2,1,0:T(8,128)(2,1)}, u32[]{:S(2)}, u32[]{:S(2)}) collective-permute-start(bf16[4,64,1152]{2,1,0:T(8,128)(2,1)} %all-to-all-done.refs_0_), channel_id=1, source_target_pairs={{0,128},{128,0},{1,129},{129,1},{2,130},{130,2},{3,131},{131,3},{4... | collective-permute-start | bytes 1769480 | tf_op jit(solution)/shard_map/ppermute | solution.py:370
  70.3 1.5 collective-permute-done.5.refs_1_.refs_5_
  71.8 2.2 %shard_map.88 = bf16[4,288,288]{2,1,0:T(8,128)(2,1)} custom-call(s32[2]{0:T(128)S(1)} %pad_add_fusion.spot_ref, bf16[288,1152]{1,0:T(8,128)(2,1)S(1)} %pad_maximum_fusion.refs_0_.refs_4_, bf16[288,1152]{1,0:T(8,128)(2,1)S(1)} %collective-permute-done.5.refs_1_.refs_5_, bf16[288,1152]{1,0:T(8,128)(2,1)S(1)} %collective-permute-done.6.refs_2_.refs_6_, ...), custom_call_target="tpu_custom_call" | custom-call | flops 1000000 | bytes 2000000 | tf_op jit(solution)/shard_map/pallas_call | solution.py:380
  74.1 1.9 collective-permute-start.3
  76.0 8.0 %collective-permute-done.4.refs_2_ = bf16[4,64,1152]{2,1,0:T(8,128)(2,1)} collective-permute-done((bf16[4,64,1152]{2,1,0:T(8,128)(2,1)}, bf16[4,64,1152]{2,1,0:T(8,128)(2,1)}, u32[]{:S(2)}, u32[]{:S(2)}) %collective-permute-start.4) | collective-permute-done | bytes 589856 | tf_op jit(solution)/shard_map/ppermute | solution.py:370
  84.1 1.9 collective-permute-start.8
  86.0 4.2 %all-to-all-start.1 = ((bf16[4,288,288]{2,1,0:T(8,128)(2,1)}), bf16[4,288,288]{2,1,0:T(8,128)(2,1)S(1)}, u32[]{:S(2)}, u32[]{:S(2)}) async-start(bf16[4,288,288]{2,1,0:T(8,128)(2,1)} %shard_map.88), calls=%async_computation.1 | async-start | bytes 1769472 | tf_op jit(solution)/shard_map/all_to_all | solution.py:391
  91.0 8.5 %shard_map.89 = (bf16[512,384]{1,0:T(8,128)(2,1)}, bf16[512,384]{1,0:T(8,128)(2,1)}, bf16[512,384]{1,0:T(8,128)(2,1)}, bf16[512,384]{1,0:T(8,128)(2,1)}, bf16[51...) custom-call(bf16[4,64,1152]{2,1,0:T(8,128)(2,1)} %all-to-all-done.refs_0_, ...), custom_call_target="tpu_custom_call" | custom-call | flops 1698693120 | bytes 12000000 | tf_op jit(solution)/shard_map/pallas_call | solution.py:395
  99.5 1.7 all-to-all-done.1.refs_8_
  101.3 7.3 %all-to-all-start.2 = ((bf16[8,36,1152]{2,1,0:T(8,128)(2,1)}), bf16[8,36,1152]{2,1,0:T(8,128)(2,1)S(1)}, u32[]{:S(2)}, u32[]{:S(2)}) async-start(bf16[8,36,1152]{2,1,0:T(8,128)(2,1)} %get-tuple-element.39), calls=%async_computation.2 | async-start | bytes 1474560 | tf_op jit(solution)/shard_map/all_to_all | solution.py:406
  108.5 12.0 %shard_map.90 = (f32[2,4,32,1152]{3,2,1,0:T(8,128)}, bf16[2,4,32,1152]{3,2,1,0:T(8,128)(2,1)}) custom-call(bf16[4,64,1152]{2,1,0:T(8,128)(2,1)} %all-to-all-done.refs_0_, bf16[4,64,1152]{2,1,0:T(8,128)(2,1)} %collective-permute-done.3.refs_1_, bf16[4,64,1152]{2,1,0:T(8,128)(2,1)} %collective-permute-done.4.refs_2_, bf16[4,64,1152]{2,1,0:T(8,128)(2,1)} %copy-done.11, ...), custom_call_target="tpu_custom_call" | custom-call | flops 1358954496 | bytes 14000000 | tf_op jit(solution)/shard_map/pallas_call | solution.py:408
  120.5 2.1 %collective-permute-start.9 = (bf16[2,4,32,1152]{3,2,1,0:T(8,128)(2,1)}, bf16[2,4,32,1152]{3,2,1,0:T(8,128)(2,1)S(1)}, u32[]{:S(2)}, u32[]{:S(2)}) collective-permute-start(bf16[2,4,32,1152]{3,2,1,0:T(8,128)(2,1)} %get-tuple-element.40), channel_id=1, source_target_pairs={{0,16},{16,0},{1,17},{17,1},{2,18},{18,2},{3,19},{19,3},{4,20},{20... | collective-permute-start | bytes 1769480 | tf_op jit(solution)/shard_map/ppermute | solution.py:367
  123.4 3.5 %all-to-all-start.3 = ((bf16[4,9,1152]{2,1,0:T(8,128)(2,1)}), bf16[4,9,1152]{2,1,0:T(8,128)(2,1)S(1)}, u32[]{:S(2)}, u32[]{:S(2)}) async-start(bf16[4,9,1152]{2,1,0:T(8,128)(2,1)} %reshape.601), calls=%async_computation.3 | async-start | bytes 294912 | tf_op jit(solution)/shard_map/all_to_all | solution.py:432
  126.9 6.7 %all-to-all-done.3 = bf16[4,9,1152]{2,1,0:T(8,128)(2,1)S(1)} async-done(((bf16[4,9,1152]{2,1,0:T(8,128)(2,1)}), bf16[4,9,1152]{2,1,0:T(8,128)(2,1)S(1)}, u32[]{:S(2)}, u32[]{:S(2)}) %all-to-all-start.3) | async-done | bytes 82976 | tf_op jit(solution)/shard_map/all_to_all | solution.py:432
  133.7 3.6 %collective-permute-start.10 = (bf16[4,32,1152]{2,1,0:T(8,128)(2,1)S(1)}, bf16[4,32,1152]{2,1,0:T(8,128)(2,1)S(1)}, u32[]{:S(2)}, u32[]{:S(2)}) collective-permute-start(bf16[4,32,1152]{2,1,0:T(8,128)(2,1)S(1)} %fusion.3), channel_id=1, source_target_pairs={{0,128},{128,0},{1,129},{129,1},{2,130},{130,2},{3,131},{131,3},{4... | collective-permute-start | bytes 884744 | tf_op jit(solution)/shard_map/ppermute | solution.py:370
  138.0 4.2 %all-to-all-start.4 = ((bf16[8,3,1152]{2,1,0:T(4,128)(2,1)}), bf16[8,3,1152]{2,1,0:T(4,128)(2,1)S(1)}, u32[]{:S(2)}, u32[]{:S(2)}) async-start(bf16[8,3,1152]{2,1,0:T(4,128)(2,1)} %bitcast.11), calls=%async_computation.4 | async-start | bytes 147456 | tf_op jit(solution)/shard_map/all_to_all | solution.py:438
  142.2 5.4 %all-to-all-done.4 = bf16[8,3,1152]{2,1,0:T(4,128)(2,1)S(1)} async-done(((bf16[8,3,1152]{2,1,0:T(4,128)(2,1)}), bf16[8,3,1152]{2,1,0:T(4,128)(2,1)S(1)}, u32[]{:S(2)}, u32[]{:S(2)}) %all-to-all-start.4) | async-done | bytes 55328 | tf_op jit(solution)/shard_map/all_to_all | solution.py:438
  147.8 28.7 %all_to_all.35.back_ref = bf16[4,40,1152]{2,1,0:T(8,128)(2,1)S(1)} all-to-all(bf16[4,40,1152]{2,1,0:T(8,128)(2,1)S(1)} %fusion.2), channel_id=1, replica_groups=mesh['yh'=2,'yl'=2,'zh'=4,'c'=2,'zl'=4,'x'=4] {'zh'}, dimensions={0} | all-to-all | bytes 737280 | tf_op jit(solution)/shard_map/all_to_all | solution.py:373
  177.1 7.4 %all-to-all-start.6 = ((bf16[16,3,1152]{2,1,0:T(4,128)(2,1)}), bf16[16,3,1152]{2,1,0:T(4,128)(2,1)S(1)}, u32[]{:S(2)}, u32[]{:S(2)}) async-start(bf16[16,3,1152]{2,1,0:T(4,128)(2,1)} %broadcast_in_dim.35), calls=%async_computation.6 | async-start | bytes 294912 | tf_op jit(solution)/shard_map/all_to_all | solution.py:452
  184.6 2.3 %shard_map.91 = bf16[128,1152]{1,0:T(8,128)(2,1)} custom-call(f32[2]{0:T(128)S(1)} %pad_maximum_fusion.5.power_ref, s32[2]{0:T(128)S(1)} %pad_add_fusion.spot_ref, bf16[128,1152]{1,0:T(8,128)(2,1)S(1)} %bitcast.28, bf16[128,1152]{1,0:T(8,128)(2,1)S(1)} %bitcast.30, f32[3,1152]{1,0:T(4,128)S(1)} %bitcast.32, bf16[4,40,1152]{2,1,0:T(8,128)(2,1)S(1)} %all_to_all.35.back_ref), custom_call_target="tpu_custom_call" | custom-call | flops 4423680 | bytes 1179648 | tf_op jit(solution)/shard_map/pallas_call | solution.py:442
  186.9 6.8 %all-to-all-done.6 = bf16[16,3,1152]{2,1,0:T(4,128)(2,1)S(1)} async-done(((bf16[16,3,1152]{2,1,0:T(4,128)(2,1)}), bf16[16,3,1152]{2,1,0:T(4,128)(2,1)S(1)}, u32[]{:S(2)}, u32[]{:S(2)}) %all-to-all-start.6) | async-done | bytes 110624 | tf_op jit(solution)/shard_map/all_to_all | solution.py:452
  (73 shorter events, 9.1 us)
Async XLA Ops:
  0.6 21.4 %copy-start = (f32[1,2,3,1152]{3,1,2,0:T(2,128)S(1)}, f32[1,2,3,1152]{3,1,2,0:T(2,128)}, u32[]{:S(2)}) copy-start(f32[1,2,3,1152]{3,1,2,0:T(2,128)} %param.9) | copy-start | bytes 82948
  0.7 1.0 copy-start.7
  1.7 0.9 copy-start.8
  2.6 22.1 %copy-start.5 = (bf16[1,1,128,1152]{3,2,1,0:T(8,128)(2,1)S(1)}, bf16[1,1,128,1152]{3,2,1,0:T(8,128)(2,1)}, u32[]{:S(2)}) copy-start(bf16[1,1,128,1152]{3,2,1,0:T(8,128)(2,1)} %param.7) | copy-start | bytes 884740
  2.6 22.1 %copy-start.6 = (bf16[1,1,128,1152]{3,2,1,0:T(8,128)(2,1)S(1)}, bf16[1,1,128,1152]{3,2,1,0:T(8,128)(2,1)}, u32[]{:S(2)}) copy-start(bf16[1,1,128,1152]{3,2,1,0:T(8,128)(2,1)} %param.10) | copy-start | bytes 884740
  2.8 24.3 %collective-permute-start.2 = (bf16[72,1152]{1,0:T(8,128)(2,1)S(1)}, bf16[72,1152]{1,0:T(8,128)(2,1)S(1)}, u32[]{:S(2)}, u32[]{:S(2)}) collective-permute-start(bf16[72,1152]{1,0:T(8,128)(2,1)S(1)} %shard_map.87), channel_id=1, source_target_pairs={{0,4},{4,8},{8,12},{12,32},{32,36},{36,40},{40,44},{44,64},{64,68}... | collective-permute-start | bytes 497672 | tf_op jit(solution)/shard_map/ppermute | solution.py:350
  6.6 20.5 %collective-permute-start.1 = (bf16[72,1152]{1,0:T(8,128)(2,1)S(1)}, bf16[72,1152]{1,0:T(8,128)(2,1)S(1)}, u32[]{:S(2)}, u32[]{:S(2)}) collective-permute-start(bf16[72,1152]{1,0:T(8,128)(2,1)S(1)} %shard_map.87), channel_id=1, source_target_pairs={{0,104},{4,108},{8,0},{12,4},{32,8},{36,12},{40,32},{44,36},{64,40... | collective-permute-start | bytes 497672 | tf_op jit(solution)/shard_map/ppermute | solution.py:350
  17.6 10.1 %collective-permute-start = (bf16[72,1152]{1,0:T(8,128)(2,1)S(1)}, bf16[72,1152]{1,0:T(8,128)(2,1)S(1)}, u32[]{:S(2)}, u32[]{:S(2)}) collective-permute-start(bf16[72,1152]{1,0:T(8,128)(2,1)S(1)} %shard_map.87), channel_id=1, source_target_pairs={{0,108},{4,0},{8,4},{12,8},{32,12},{36,32},{40,36},{44,40},{64,44}... | collective-permute-start | bytes 497672 | tf_op jit(solution)/shard_map/ppermute | solution.py:350
  27.7 46.3 %copy-start.1 = (bf16[288,1152]{1,0:T(8,128)(2,1)}, bf16[288,1152]{1,0:T(8,128)(2,1)S(1)}, u32[]{:S(2)}) copy-start(bf16[288,1152]{1,0:T(8,128)(2,1)S(1)} %pad_maximum_fusion.refs_0_.refs_4_) | copy-start | bytes 1990660
  27.8 39.2 %all-to-all-start = ((bf16[4,64,1152]{2,1,0:T(8,128)(2,1)}), bf16[4,64,1152]{2,1,0:T(8,128)(2,1)}, u32[]{:S(2)}, u32[]{:S(2)}) async-start(bf16[4,64,1152]{2,1,0:T(8,128)(2,1)} %shard_map.86), calls=%async_computation | async-start | bytes 1179648 | tf_op jit(solution)/shard_map/all_to_all | solution.py:373
  36.8 32.8 %collective-permute-start.7 = (bf16[288,1152]{1,0:T(8,128)(2,1)S(1)}, bf16[288,1152]{1,0:T(8,128)(2,1)S(1)}, u32[]{:S(2)}, u32[]{:S(2)}) collective-permute-start(bf16[288,1152]{1,0:T(8,128)(2,1)S(1)} %pad_maximum_fusion.refs_0_.refs_4_), channel_id=1, source_target_pairs={{0,1},{1,2},{2,3},{3,0},{4,5},{5,6},{6,7},{7,4},{8,9},{9,10},{10,1... | collective-permute-start | bytes 1990664 | tf_op jit(solution)/shard_map/ppermute | solution.py:353
  40.2 30.1 %collective-permute-start.6 = (bf16[288,1152]{1,0:T(8,128)(2,1)S(1)}, bf16[288,1152]{1,0:T(8,128)(2,1)S(1)}, u32[]{:S(2)}, u32[]{:S(2)}) collective-permute-start(bf16[288,1152]{1,0:T(8,128)(2,1)S(1)} %pad_maximum_fusion.refs_0_.refs_4_), channel_id=1, source_target_pairs={{0,2},{1,3},{2,0},{3,1},{4,6},{5,7},{6,4},{7,5},{8,10},{9,11},{10,... | collective-permute-start | bytes 1990664 | tf_op jit(solution)/shard_map/ppermute | solution.py:353
  44.8 27.0 %collective-permute-start.5 = (bf16[288,1152]{1,0:T(8,128)(2,1)S(1)}, bf16[288,1152]{1,0:T(8,128)(2,1)S(1)}, u32[]{:S(2)}, u32[]{:S(2)}) collective-permute-start(bf16[288,1152]{1,0:T(8,128)(2,1)S(1)} %pad_maximum_fusion.refs_0_.refs_4_), channel_id=1, source_target_pairs={{0,3},{1,0},{2,1},{3,2},{4,7},{5,4},{6,5},{7,6},{8,11},{9,8},{10,9... | collective-permute-start | bytes 1990664 | tf_op jit(solution)/shard_map/ppermute | solution.py:353
  66.9 17.2 %collective-permute-start.4 = (bf16[4,64,1152]{2,1,0:T(8,128)(2,1)}, bf16[4,64,1152]{2,1,0:T(8,128)(2,1)}, u32[]{:S(2)}, u32[]{:S(2)}) collective-permute-start(bf16[4,64,1152]{2,1,0:T(8,128)(2,1)} %all-to-all-done.refs_0_), channel_id=1, source_target_pairs={{0,128},{128,0},{1,129},{129,1},{2,130},{130,2},{3,131},{131,3},{4... | collective-permute-start | bytes 1769480 | tf_op jit(solution)/shard_map/ppermute | solution.py:370
  69.6 4.5 %copy-start.2 = (bf16[288,1152]{1,0:T(8,128)(2,1)}, bf16[288,1152]{1,0:T(8,128)(2,1)S(1)}, u32[]{:S(2)}) copy-start(bf16[288,1152]{1,0:T(8,128)(2,1)S(1)} %collective-permute-done.7.refs_3_.refs_7_) | copy-start | bytes 1990660
  70.3 3.8 %copy-start.3 = (bf16[288,1152]{1,0:T(8,128)(2,1)}, bf16[288,1152]{1,0:T(8,128)(2,1)S(1)}, u32[]{:S(2)}) copy-start(bf16[288,1152]{1,0:T(8,128)(2,1)S(1)} %collective-permute-done.6.refs_2_.refs_6_) | copy-start | bytes 1990660
  71.8 2.3 %copy-start.4 = (bf16[288,1152]{1,0:T(8,128)(2,1)}, bf16[288,1152]{1,0:T(8,128)(2,1)S(1)}, u32[]{:S(2)}) copy-start(bf16[288,1152]{1,0:T(8,128)(2,1)S(1)} %collective-permute-done.5.refs_1_.refs_5_) | copy-start | bytes 1990660
  74.1 16.1 %collective-permute-start.3 = (bf16[4,64,1152]{2,1,0:T(8,128)(2,1)}, bf16[4,64,1152]{2,1,0:T(8,128)(2,1)}, u32[]{:S(2)}, u32[]{:S(2)}) collective-permute-start(bf16[4,64,1152]{2,1,0:T(8,128)(2,1)} %all-to-all-done.refs_0_), channel_id=1, source_target_pairs={{0,16},{16,0},{1,17},{17,1},{2,18},{18,2},{3,19},{19,3},{4,20},{20... | collective-permute-start | bytes 1769480 | tf_op jit(solution)/shard_map/ppermute | solution.py:367
  84.1 6.1 %collective-permute-start.8 = (bf16[4,64,1152]{2,1,0:T(8,128)(2,1)}, bf16[4,64,1152]{2,1,0:T(8,128)(2,1)S(1)}, u32[]{:S(2)}, u32[]{:S(2)}) collective-permute-start(bf16[4,64,1152]{2,1,0:T(8,128)(2,1)} %collective-permute-done.4.refs_2_), channel_id=1, source_target_pairs={{0,16},{16,0},{1,17},{17,1},{2,18},{18,2},{3,19},{19,3},{4,20},{20... | collective-permute-start | bytes 1769480 | tf_op jit(solution)/shard_map/ppermute | solution.py:367
  86.0 15.3 %all-to-all-start.1 = ((bf16[4,288,288]{2,1,0:T(8,128)(2,1)}), bf16[4,288,288]{2,1,0:T(8,128)(2,1)S(1)}, u32[]{:S(2)}, u32[]{:S(2)}) async-start(bf16[4,288,288]{2,1,0:T(8,128)(2,1)} %shard_map.88), calls=%async_computation.1 | async-start | bytes 1769472 | tf_op jit(solution)/shard_map/all_to_all | solution.py:391
  90.2 0.8 copy-start.11
  101.3 7.3 %copy-start.9 = (bf16[4,288,288]{2,1,0:T(8,128)(2,1)}, bf16[4,288,288]{2,1,0:T(8,128)(2,1)S(1)}, u32[]{:S(2)}) copy-start(bf16[4,288,288]{2,1,0:T(8,128)(2,1)S(1)} %all-to-all-done.1.refs_8_) | copy-start | bytes 1990660
  101.3 19.2 %all-to-all-start.2 = ((bf16[8,36,1152]{2,1,0:T(8,128)(2,1)}), bf16[8,36,1152]{2,1,0:T(8,128)(2,1)S(1)}, u32[]{:S(2)}, u32[]{:S(2)}) async-start(bf16[8,36,1152]{2,1,0:T(8,128)(2,1)} %get-tuple-element.39), calls=%async_computation.2 | async-start | bytes 1474560 | tf_op jit(solution)/shard_map/all_to_all | solution.py:406
  120.5 6.4 %copy-start.10 = (f32[2,4,32,1152]{3,2,1,0:T(8,128)S(1)}, f32[2,4,32,1152]{3,2,1,0:T(8,128)}, u32[]{:S(2)}) copy-start(f32[2,4,32,1152]{3,2,1,0:T(8,128)} %get-tuple-element.37) | copy-start | bytes 3538948
  120.5 6.4 %collective-permute-start.9 = (bf16[2,4,32,1152]{3,2,1,0:T(8,128)(2,1)}, bf16[2,4,32,1152]{3,2,1,0:T(8,128)(2,1)S(1)}, u32[]{:S(2)}, u32[]{:S(2)}) collective-permute-start(bf16[2,4,32,1152]{3,2,1,0:T(8,128)(2,1)} %get-tuple-element.40), channel_id=1, source_target_pairs={{0,16},{16,0},{1,17},{17,1},{2,18},{18,2},{3,19},{19,3},{4,20},{20... | collective-permute-start | bytes 1769480 | tf_op jit(solution)/shard_map/ppermute | solution.py:367
  123.4 10.3 %all-to-all-start.3 = ((bf16[4,9,1152]{2,1,0:T(8,128)(2,1)}), bf16[4,9,1152]{2,1,0:T(8,128)(2,1)S(1)}, u32[]{:S(2)}, u32[]{:S(2)}) async-start(bf16[4,9,1152]{2,1,0:T(8,128)(2,1)} %reshape.601), calls=%async_computation.3 | async-start | bytes 294912 | tf_op jit(solution)/shard_map/all_to_all | solution.py:432
  133.7 13.9 %collective-permute-start.10 = (bf16[4,32,1152]{2,1,0:T(8,128)(2,1)S(1)}, bf16[4,32,1152]{2,1,0:T(8,128)(2,1)S(1)}, u32[]{:S(2)}, u32[]{:S(2)}) collective-permute-start(bf16[4,32,1152]{2,1,0:T(8,128)(2,1)S(1)} %fusion.3), channel_id=1, source_target_pairs={{0,128},{128,0},{1,129},{129,1},{2,130},{130,2},{3,131},{131,3},{4... | collective-permute-start | bytes 884744 | tf_op jit(solution)/shard_map/ppermute | solution.py:370
  138.0 9.6 %all-to-all-start.4 = ((bf16[8,3,1152]{2,1,0:T(4,128)(2,1)}), bf16[8,3,1152]{2,1,0:T(4,128)(2,1)S(1)}, u32[]{:S(2)}, u32[]{:S(2)}) async-start(bf16[8,3,1152]{2,1,0:T(4,128)(2,1)} %bitcast.11), calls=%async_computation.4 | async-start | bytes 147456 | tf_op jit(solution)/shard_map/all_to_all | solution.py:438
  177.1 16.5 %all-to-all-start.6 = ((bf16[16,3,1152]{2,1,0:T(4,128)(2,1)}), bf16[16,3,1152]{2,1,0:T(4,128)(2,1)S(1)}, u32[]{:S(2)}, u32[]{:S(2)}) async-start(bf16[16,3,1152]{2,1,0:T(4,128)(2,1)} %broadcast_in_dim.35), calls=%async_computation.6 | async-start | bytes 294912 | tf_op jit(solution)/shard_map/all_to_all | solution.py:452
